TPU v7x, 32 devices: a whole 2x2x4 slice. The times are simulated.
32 devices in a mesh: space: 8 (over z, x), tm: 4 (over y, core).
Axes of the slice: x: 2, y: 2, z: 4, core: 2. Of those that a mesh axis runs over, the one named last changes fastest.
Arguments:
- right_side: bfloat16 [4, 8, 4, 4, 64, 64], P('tm', 'space'), may hold values from -6 to 6
- batch_order: int32 [32], replicated, may hold values from 0 to 31, each once
- light_diag: bfloat16 [4, 8, 4, 4, 64, 128], P('tm', 'space'), may hold values from -1 to 2
- light_hops: bfloat16 [8, 4, 8, 4, 4, 64, 128], P(None, 'tm', 'space'), may hold values from -0.125 to 0.125
- charm_diag: bfloat16 [4, 8, 4, 4, 64, 128], P('tm', 'space'), may hold values from -1 to 2
- charm_hops: bfloat16 [8, 4, 8, 4, 4, 64, 128], P(None, 'tm', 'space'), may hold values from -0.125 to 0.125
- current_blocks: bfloat16 [4, 8, 4, 4, 64, 128], P('tm', 'space'), may hold values from -0.5 to 0.5
Outputs:
- light_field: bfloat16 [4, 8, 4, 4, 64, 64], P('tm', 'space')
- seq_field: bfloat16 [4, 8, 4, 4, 64, 64], P('tm', 'space')
- margin: float32 [2, 32, 32], replicated
All inputs are finite; a program needn't handle non-finite values.
Results may differ from a plain program's by a relative error of at most 0.015.
Values may be sent and summed in bfloat16 or wider, within the bound.
No kernel may reach another device: no remote copies, remote signals or barrier semaphores. Data moves between devices by JAX's collectives and lax.ppermute only.
A program may use at most 64 MiB of HBM per device.

v0:
```python
import math

import jax
import jax.numpy as jnp
from jax import lax
from jax.sharding import PartitionSpec as P

SWEEPS = 4


def padded(block, sides, width):
    for axis, dim in sides:
        count = lax.axis_size(axis)
        forward = [(i, i + 1) for i in range(count - 1)]
        forward.append((count - 1, 0))
        backward = [(target, source) for source, target in forward]
        low = lax.ppermute(
            lax.slice_in_dim(block, block.shape[dim] - width, None, axis=dim), axis, forward
        )
        high = lax.ppermute(lax.slice_in_dim(block, 0, width, axis=dim), axis, backward)
        block = jnp.concatenate([low, block, high], axis=dim)
    return block


def expand(spinor):
    columns = spinor.shape[-1] // 2
    lower = jnp.concatenate([-spinor[..., columns:], spinor[..., :columns]], axis=-1)
    return jnp.concatenate([spinor, lower], axis=-2)


def apply_wide(blocks, widened):
    return jnp.einsum("tzxyij,tzxyjk->tzxyik", blocks, widened, preferred_element_type=jnp.float32)


def local_terms(hop_blocks, center):
    total = apply_wide(hop_blocks[0], jnp.roll(center, -1, axis=2))
    total = total + apply_wide(hop_blocks[1], jnp.roll(center, 1, axis=2))
    total = total + apply_wide(hop_blocks[2], jnp.roll(center, -1, axis=3))
    total = total + apply_wide(hop_blocks[3], jnp.roll(center, 1, axis=3))
    return total


def remote_terms(hop_blocks, widened):
    total = apply_wide(hop_blocks[4], widened[1:-1, 2:])
    total = total + apply_wide(hop_blocks[5], widened[1:-1, :-2])
    total = total + apply_wide(hop_blocks[6], widened[2:, 1:-1])
    total = total + apply_wide(hop_blocks[7], widened[:-2, 1:-1])
    return total


def fetch_faces(spinor):
    return padded(spinor, (("space", 1), ("tm", 0)), 1)


def solve_system(diag_inverse, hop_blocks, source):
    spinor = apply_wide(diag_inverse, expand(source)).astype(jnp.bfloat16)
    for sweep_index in range(SWEEPS - 1):
        partial_sum = source.astype(jnp.float32) + local_terms(hop_blocks, expand(spinor))
        widened = expand(fetch_faces(spinor))
        residue = (partial_sum + remote_terms(hop_blocks, widened)).astype(jnp.bfloat16)
        spinor = apply_wide(diag_inverse, expand(residue)).astype(jnp.bfloat16)
    return spinor


def body(right_side, batch_order, light_diag, light_hops, charm_diag, charm_hops, current_blocks):
    columns = right_side.shape[-1] // 2
    column_index = jnp.concatenate([batch_order, batch_order + columns])
    source = jnp.take(right_side, column_index, axis=-1)
    light_field = solve_system(light_diag, light_hops, source)
    inserted = apply_wide(current_blocks, expand(light_field)).astype(jnp.bfloat16)
    seq_field = solve_system(charm_diag, charm_hops, inserted)
    flat_light = light_field.reshape(-1, 2 * columns)
    flat_seq = seq_field.reshape(-1, 2 * columns)
    gram = lax.dot_general(
        flat_light, flat_seq, (((0,), (0,)), ((), ())), preferred_element_type=jnp.float32
    )
    real_sum = gram[:columns, :columns] + gram[columns:, columns:]
    imag_sum = gram[:columns, columns:] - gram[columns:, :columns]
    summed = lax.psum(jnp.stack([real_sum, imag_sum]), ("space", "tm"))
    site_count = (
        light_field.shape[0]
        * light_field.shape[1]
        * light_field.shape[2]
        * light_field.shape[3]
        * lax.axis_size("space")
        * lax.axis_size("tm")
    )
    factor_norm = 1.0 / math.sqrt(site_count * light_field.shape[4])
    return (light_field, seq_field, summed * factor_norm)


def solution(mesh):
    return jax.shard_map(
        body,
        mesh=mesh,
        in_specs=(
            P("tm", "space", None, None, None, None),
            P(),
            P("tm", "space", None, None, None, None),
            P(None, "tm", "space", None, None, None, None),
            P("tm", "space", None, None, None, None),
            P(None, "tm", "space", None, None, None, None),
            P("tm", "space", None, None, None, None),
        ),
        out_specs=(
            P("tm", "space", None, None, None, None),
            P("tm", "space", None, None, None, None),
            P(),
        ),
        check_vma=False,
    )
```

profile of v0, /device:TPU:0, one launch (start us, length us, event | category | flops | bytes accessed | tf_op | source)
XLA Modules:
  0.0 272.8 jit_solution(7316783508530896615)
XLA Ops:
  5.4 3.0 %collective-permute-start = (bf16[1,1,4,4,64,64]{4,5,3,2,1,0:T(8,128)(2,1)S(1)}, bf16[1,1,4,4,64,64]{4,5,3,2,1,0:T(8,128)(2,1)S(1)}, u32[]{:S(2)}, u32[]{:S(2)}) collective-permute-start(bf16[1,1,4,4,64,64]{4,5,3,2,1,0:T(8,128)(2,1)S(1)} %fusion.30), channel_id=1, source_target_pairs={{0,4},{4,8},{8,12},{12,16},{16,20},{20,24},{24,28},{28,0},{1,5},{5... | collective-permute-start | bytes 393224 | tf_op jit(solution)/shard_map/ppermute | solution.py:17
  8.4 3.1 %collective-permute-start.1 = (bf16[1,1,4,4,64,64]{4,5,3,2,1,0:T(8,128)(2,1)S(1)}, bf16[1,1,4,4,64,64]{4,5,3,2,1,0:T(8,128)(2,1)S(1)}, u32[]{:S(2)}, u32[]{:S(2)}) collective-permute-start(bf16[1,1,4,4,64,64]{4,5,3,2,1,0:T(8,128)(2,1)S(1)} %fusion.30), channel_id=1, source_target_pairs={{4,0},{8,4},{12,8},{16,12},{20,16},{24,20},{28,24},{0,28},{5,1},{9... | collective-permute-start | bytes 393224 | tf_op jit(solution)/shard_map/ppermute | solution.py:20
  12.4 7.2 %collective-permute-done = bf16[1,1,4,4,64,64]{4,5,3,2,1,0:T(8,128)(2,1)S(1)} collective-permute-done((bf16[1,1,4,4,64,64]{4,5,3,2,1,0:T(8,128)(2,1)S(1)}, bf16[1,1,4,4,64,64]{4,5,3,2,1,0:T(8,128)(2,1)S(1)}, u32[]{:S(2)}, u32[]{:S(2)}) %collective-permute-start) | collective-permute-done | bytes 131104 | tf_op jit(solution)/shard_map/ppermute | solution.py:17
  24.3 15.7 %collective-permute-done.2 = bf16[1,3,4,4,64,64]{4,5,3,2,1,0:T(8,128)(2,1)S(1)} collective-permute-done((bf16[1,3,4,4,64,64]{4,5,3,2,1,0:T(8,128)(2,1)S(1)}, bf16[1,3,4,4,64,64]{4,5,3,2,1,0:T(8,128)(2,1)S(1)}, u32[]{:S(2)}, u32[]{:S(2)}) %collective-permute-start.2) | collective-permute-done | bytes 393248 | tf_op jit(solution)/shard_map/ppermute | solution.py:17
  43.9 4.4 %collective-permute-start.5 = (bf16[1,1,4,4,64,64]{4,5,3,2,1,0:T(8,128)(2,1)S(1)}, bf16[1,1,4,4,64,64]{4,5,3,2,1,0:T(8,128)(2,1)S(1)}, u32[]{:S(2)}, u32[]{:S(2)}) collective-permute-start(bf16[1,1,4,4,64,64]{4,5,3,2,1,0:T(8,128)(2,1)S(1)} %fusion.31), channel_id=1, source_target_pairs={{4,0},{8,4},{12,8},{16,12},{20,16},{24,20},{28,24},{0,28},{5,1},{9... | collective-permute-start | bytes 393224 | tf_op jit(solution)/shard_map/ppermute | solution.py:20
  49.2 6.8 %collective-permute-done.4 = bf16[1,1,4,4,64,64]{4,5,3,2,1,0:T(8,128)(2,1)S(1)} collective-permute-done((bf16[1,1,4,4,64,64]{4,5,3,2,1,0:T(8,128)(2,1)S(1)}, bf16[1,1,4,4,64,64]{4,5,3,2,1,0:T(8,128)(2,1)S(1)}, u32[]{:S(2)}, u32[]{:S(2)}) %collective-permute-start.4) | collective-permute-done | bytes 131104 | tf_op jit(solution)/shard_map/ppermute | solution.py:17
  56.0 2.9 %collective-permute-done.5 = bf16[1,1,4,4,64,64]{4,5,3,2,1,0:T(8,128)(2,1)S(1)} collective-permute-done((bf16[1,1,4,4,64,64]{4,5,3,2,1,0:T(8,128)(2,1)S(1)}, bf16[1,1,4,4,64,64]{4,5,3,2,1,0:T(8,128)(2,1)S(1)}, u32[]{:S(2)}, u32[]{:S(2)}) %collective-permute-start.5) | collective-permute-done | bytes 131104 | tf_op jit(solution)/shard_map/ppermute | solution.py:20
  61.4 15.7 %collective-permute-done.6 = bf16[1,3,4,4,64,64]{4,5,3,2,1,0:T(8,128)(2,1)S(1)} collective-permute-done((bf16[1,3,4,4,64,64]{4,5,3,2,1,0:T(8,128)(2,1)S(1)}, bf16[1,3,4,4,64,64]{4,5,3,2,1,0:T(8,128)(2,1)S(1)}, u32[]{:S(2)}, u32[]{:S(2)}) %collective-permute-start.6) | collective-permute-done | bytes 393248 | tf_op jit(solution)/shard_map/ppermute | solution.py:17
  80.7 4.7 %collective-permute-start.9 = (bf16[1,1,4,4,64,64]{4,5,3,2,1,0:T(8,128)(2,1)S(1)}, bf16[1,1,4,4,64,64]{4,5,3,2,1,0:T(8,128)(2,1)S(1)}, u32[]{:S(2)}, u32[]{:S(2)}) collective-permute-start(bf16[1,1,4,4,64,64]{4,5,3,2,1,0:T(8,128)(2,1)S(1)} %fusion.32), channel_id=1, source_target_pairs={{4,0},{8,4},{12,8},{16,12},{20,16},{24,20},{28,24},{0,28},{5,1},{9... | collective-permute-start | bytes 393224 | tf_op jit(solution)/shard_map/ppermute | solution.py:20
  86.3 6.6 %collective-permute-done.8 = bf16[1,1,4,4,64,64]{4,5,3,2,1,0:T(8,128)(2,1)S(1)} collective-permute-done((bf16[1,1,4,4,64,64]{4,5,3,2,1,0:T(8,128)(2,1)S(1)}, bf16[1,1,4,4,64,64]{4,5,3,2,1,0:T(8,128)(2,1)S(1)}, u32[]{:S(2)}, u32[]{:S(2)}) %collective-permute-start.8) | collective-permute-done | bytes 131104 | tf_op jit(solution)/shard_map/ppermute | solution.py:17
  92.9 3.3 %collective-permute-done.9 = bf16[1,1,4,4,64,64]{4,5,3,2,1,0:T(8,128)(2,1)S(1)} collective-permute-done((bf16[1,1,4,4,64,64]{4,5,3,2,1,0:T(8,128)(2,1)S(1)}, bf16[1,1,4,4,64,64]{4,5,3,2,1,0:T(8,128)(2,1)S(1)}, u32[]{:S(2)}, u32[]{:S(2)}) %collective-permute-start.9) | collective-permute-done | bytes 131104 | tf_op jit(solution)/shard_map/ppermute | solution.py:20
  98.8 15.7 %collective-permute-done.10 = bf16[1,3,4,4,64,64]{4,5,3,2,1,0:T(8,128)(2,1)S(1)} collective-permute-done((bf16[1,3,4,4,64,64]{4,5,3,2,1,0:T(8,128)(2,1)S(1)}, bf16[1,3,4,4,64,64]{4,5,3,2,1,0:T(8,128)(2,1)S(1)}, u32[]{:S(2)}, u32[]{:S(2)}) %collective-permute-start.10) | collective-permute-done | bytes 393248 | tf_op jit(solution)/shard_map/ppermute | solution.py:17
  119.4 4.7 %collective-permute-start.13 = (bf16[1,1,4,4,64,64]{4,5,3,2,1,0:T(8,128)(2,1)S(1)}, bf16[1,1,4,4,64,64]{4,5,3,2,1,0:T(8,128)(2,1)S(1)}, u32[]{:S(2)}, u32[]{:S(2)}) collective-permute-start(bf16[1,1,4,4,64,64]{4,5,3,2,1,0:T(8,128)(2,1)S(1)} %fusion.33), channel_id=1, source_target_pairs={{4,0},{8,4},{12,8},{16,12},{20,16},{24,20},{28,24},{0,28},{5,1},{9... | collective-permute-start | bytes 393224 | tf_op jit(solution)/shard_map/ppermute | solution.py:20
  131.6 3.3 %collective-permute-done.13 = bf16[1,1,4,4,64,64]{4,5,3,2,1,0:T(8,128)(2,1)S(1)} collective-permute-done((bf16[1,1,4,4,64,64]{4,5,3,2,1,0:T(8,128)(2,1)S(1)}, bf16[1,1,4,4,64,64]{4,5,3,2,1,0:T(8,128)(2,1)S(1)}, u32[]{:S(2)}, u32[]{:S(2)}) %collective-permute-start.13) | collective-permute-done | bytes 131104 | tf_op jit(solution)/shard_map/ppermute | solution.py:20
  137.4 15.7 %collective-permute-done.14 = bf16[1,3,4,4,64,64]{4,5,3,2,1,0:T(8,128)(2,1)S(1)} collective-permute-done((bf16[1,3,4,4,64,64]{4,5,3,2,1,0:T(8,128)(2,1)S(1)}, bf16[1,3,4,4,64,64]{4,5,3,2,1,0:T(8,128)(2,1)S(1)}, u32[]{:S(2)}, u32[]{:S(2)}) %collective-permute-start.14) | collective-permute-done | bytes 393248 | tf_op jit(solution)/shard_map/ppermute | solution.py:17
  157.3 4.7 %collective-permute-start.17 = (bf16[1,1,4,4,64,64]{4,5,3,2,1,0:T(8,128)(2,1)S(1)}, bf16[1,1,4,4,64,64]{4,5,3,2,1,0:T(8,128)(2,1)S(1)}, u32[]{:S(2)}, u32[]{:S(2)}) collective-permute-start(bf16[1,1,4,4,64,64]{4,5,3,2,1,0:T(8,128)(2,1)S(1)} %fusion.34), channel_id=1, source_target_pairs={{4,0},{8,4},{12,8},{16,12},{20,16},{24,20},{28,24},{0,28},{5,1},{9... | collective-permute-start | bytes 393224 | tf_op jit(solution)/shard_map/ppermute | solution.py:20
  162.9 6.6 %collective-permute-done.16 = bf16[1,1,4,4,64,64]{4,5,3,2,1,0:T(8,128)(2,1)S(1)} collective-permute-done((bf16[1,1,4,4,64,64]{4,5,3,2,1,0:T(8,128)(2,1)S(1)}, bf16[1,1,4,4,64,64]{4,5,3,2,1,0:T(8,128)(2,1)S(1)}, u32[]{:S(2)}, u32[]{:S(2)}) %collective-permute-start.16) | collective-permute-done | bytes 131104 | tf_op jit(solution)/shard_map/ppermute | solution.py:17
  169.5 2.9 %collective-permute-done.17 = bf16[1,1,4,4,64,64]{4,5,3,2,1,0:T(8,128)(2,1)S(1)} collective-permute-done((bf16[1,1,4,4,64,64]{4,5,3,2,1,0:T(8,128)(2,1)S(1)}, bf16[1,1,4,4,64,64]{4,5,3,2,1,0:T(8,128)(2,1)S(1)}, u32[]{:S(2)}, u32[]{:S(2)}) %collective-permute-start.17) | collective-permute-done | bytes 131104 | tf_op jit(solution)/shard_map/ppermute | solution.py:20
  175.0 15.7 %collective-permute-done.18 = bf16[1,3,4,4,64,64]{4,5,3,2,1,0:T(8,128)(2,1)S(1)} collective-permute-done((bf16[1,3,4,4,64,64]{4,5,3,2,1,0:T(8,128)(2,1)S(1)}, bf16[1,3,4,4,64,64]{4,5,3,2,1,0:T(8,128)(2,1)S(1)}, u32[]{:S(2)}, u32[]{:S(2)}) %collective-permute-start.18) | collective-permute-done | bytes 393248 | tf_op jit(solution)/shard_map/ppermute | solution.py:17
  194.3 4.7 %collective-permute-start.21 = (bf16[1,1,4,4,64,64]{4,5,3,2,1,0:T(8,128)(2,1)S(1)}, bf16[1,1,4,4,64,64]{4,5,3,2,1,0:T(8,128)(2,1)S(1)}, u32[]{:S(2)}, u32[]{:S(2)}) collective-permute-start(bf16[1,1,4,4,64,64]{4,5,3,2,1,0:T(8,128)(2,1)S(1)} %fusion.35), channel_id=1, source_target_pairs={{4,0},{8,4},{12,8},{16,12},{20,16},{24,20},{28,24},{0,28},{5,1},{9... | collective-permute-start | bytes 393224 | tf_op jit(solution)/shard_map/ppermute | solution.py:20
  199.9 6.6 %collective-permute-done.20 = bf16[1,1,4,4,64,64]{4,5,3,2,1,0:T(8,128)(2,1)S(1)} collective-permute-done((bf16[1,1,4,4,64,64]{4,5,3,2,1,0:T(8,128)(2,1)S(1)}, bf16[1,1,4,4,64,64]{4,5,3,2,1,0:T(8,128)(2,1)S(1)}, u32[]{:S(2)}, u32[]{:S(2)}) %collective-permute-start.20) | collective-permute-done | bytes 131104 | tf_op jit(solution)/shard_map/ppermute | solution.py:17
  206.5 2.8 %collective-permute-done.21 = bf16[1,1,4,4,64,64]{4,5,3,2,1,0:T(8,128)(2,1)S(1)} collective-permute-done((bf16[1,1,4,4,64,64]{4,5,3,2,1,0:T(8,128)(2,1)S(1)}, bf16[1,1,4,4,64,64]{4,5,3,2,1,0:T(8,128)(2,1)S(1)}, u32[]{:S(2)}, u32[]{:S(2)}) %collective-permute-start.21) | collective-permute-done | bytes 131104 | tf_op jit(solution)/shard_map/ppermute | solution.py:20
  211.8 15.7 %collective-permute-done.22 = bf16[1,3,4,4,64,64]{4,5,3,2,1,0:T(8,128)(2,1)S(1)} collective-permute-done((bf16[1,3,4,4,64,64]{4,5,3,2,1,0:T(8,128)(2,1)S(1)}, bf16[1,3,4,4,64,64]{4,5,3,2,1,0:T(8,128)(2,1)S(1)}, u32[]{:S(2)}, u32[]{:S(2)}) %collective-permute-start.22) | collective-permute-done | bytes 393248 | tf_op jit(solution)/shard_map/ppermute | solution.py:17
  231.6 39.7 %psum.7 = f32[2,32,32]{2,1,0:T(8,128)S(1)} all-reduce(f32[2,32,32]{2,1,0:T(8,128)S(1)} %pad_maximum_fusion.66), channel_id=1, replica_groups=mesh['space'=8,'tm'=4] {'space','tm'}, use_global_device_ids=true, to_apply=%region_0.1 | all-reduce | flops 2048 | bytes 16384 | tf_op jit(solution)/shard_map/psum | solution.py:79
  (180 shorter events, 59.3 us)
Async XLA Ops:
  5.4 14.2 %collective-permute-start = (bf16[1,1,4,4,64,64]{4,5,3,2,1,0:T(8,128)(2,1)S(1)}, bf16[1,1,4,4,64,64]{4,5,3,2,1,0:T(8,128)(2,1)S(1)}, u32[]{:S(2)}, u32[]{:S(2)}) collective-permute-start(bf16[1,1,4,4,64,64]{4,5,3,2,1,0:T(8,128)(2,1)S(1)} %fusion.30), channel_id=1, source_target_pairs={{0,4},{4,8},{8,12},{12,16},{16,20},{20,24},{24,28},{28,0},{1,5},{5... | collective-permute-start | bytes 393224 | tf_op jit(solution)/shard_map/ppermute | solution.py:17
  8.4 13.4 %collective-permute-start.1 = (bf16[1,1,4,4,64,64]{4,5,3,2,1,0:T(8,128)(2,1)S(1)}, bf16[1,1,4,4,64,64]{4,5,3,2,1,0:T(8,128)(2,1)S(1)}, u32[]{:S(2)}, u32[]{:S(2)}) collective-permute-start(bf16[1,1,4,4,64,64]{4,5,3,2,1,0:T(8,128)(2,1)S(1)} %fusion.30), channel_id=1, source_target_pairs={{4,0},{8,4},{12,8},{16,12},{20,16},{24,20},{28,24},{0,28},{5,1},{9... | collective-permute-start | bytes 393224 | tf_op jit(solution)/shard_map/ppermute | solution.py:20
  21.9 18.0 %collective-permute-start.2 = (bf16[1,3,4,4,64,64]{4,5,3,2,1,0:T(8,128)(2,1)S(1)}, bf16[1,3,4,4,64,64]{4,5,3,2,1,0:T(8,128)(2,1)S(1)}, u32[]{:S(2)}, u32[]{:S(2)}) collective-permute-start(bf16[1,3,4,4,64,64]{4,5,3,2,1,0:T(8,128)(2,1)S(1)} %pad_maximum_fusion.6), channel_id=1, source_target_pairs={{0,1},{1,2},{2,3},{3,0},{4,5},{5,6},{6,7},{7,4},{8,9},{9,10},{10,1... | collective-permute-start | bytes 1179656 | tf_op jit(solution)/shard_map/ppermute | solution.py:17
  22.0 18.9 %collective-permute-start.3 = (bf16[1,3,4,4,64,64]{4,5,3,2,1,0:T(8,128)(2,1)S(1)}, bf16[1,3,4,4,64,64]{4,5,3,2,1,0:T(8,128)(2,1)S(1)}, u32[]{:S(2)}, u32[]{:S(2)}) collective-permute-start(bf16[1,3,4,4,64,64]{4,5,3,2,1,0:T(8,128)(2,1)S(1)} %pad_maximum_fusion.6), channel_id=1, source_target_pairs={{1,0},{2,1},{3,2},{0,3},{5,4},{6,5},{7,6},{4,7},{9,8},{10,9},{11,1... | collective-permute-start | bytes 1179656 | tf_op jit(solution)/shard_map/ppermute | solution.py:20
  43.5 12.5 %collective-permute-start.4 = (bf16[1,1,4,4,64,64]{4,5,3,2,1,0:T(8,128)(2,1)S(1)}, bf16[1,1,4,4,64,64]{4,5,3,2,1,0:T(8,128)(2,1)S(1)}, u32[]{:S(2)}, u32[]{:S(2)}) collective-permute-start(bf16[1,1,4,4,64,64]{4,5,3,2,1,0:T(8,128)(2,1)S(1)} %fusion.31), channel_id=1, source_target_pairs={{0,4},{4,8},{8,12},{12,16},{16,20},{20,24},{24,28},{28,0},{1,5},{5... | collective-permute-start | bytes 393224 | tf_op jit(solution)/shard_map/ppermute | solution.py:17
  43.9 15.0 %collective-permute-start.5 = (bf16[1,1,4,4,64,64]{4,5,3,2,1,0:T(8,128)(2,1)S(1)}, bf16[1,1,4,4,64,64]{4,5,3,2,1,0:T(8,128)(2,1)S(1)}, u32[]{:S(2)}, u32[]{:S(2)}) collective-permute-start(bf16[1,1,4,4,64,64]{4,5,3,2,1,0:T(8,128)(2,1)S(1)} %fusion.31), channel_id=1, source_target_pairs={{4,0},{8,4},{12,8},{16,12},{20,16},{24,20},{28,24},{0,28},{5,1},{9... | collective-permute-start | bytes 393224 | tf_op jit(solution)/shard_map/ppermute | solution.py:20
  59.1 18.0 %collective-permute-start.6 = (bf16[1,3,4,4,64,64]{4,5,3,2,1,0:T(8,128)(2,1)S(1)}, bf16[1,3,4,4,64,64]{4,5,3,2,1,0:T(8,128)(2,1)S(1)}, u32[]{:S(2)}, u32[]{:S(2)}) collective-permute-start(bf16[1,3,4,4,64,64]{4,5,3,2,1,0:T(8,128)(2,1)S(1)} %pad_maximum_fusion.7), channel_id=1, source_target_pairs={{0,1},{1,2},{2,3},{3,0},{4,5},{5,6},{6,7},{7,4},{8,9},{9,10},{10,1... | collective-permute-start | bytes 1179656 | tf_op jit(solution)/shard_map/ppermute | solution.py:17
  59.1 18.9 %collective-permute-start.7 = (bf16[1,3,4,4,64,64]{4,5,3,2,1,0:T(8,128)(2,1)S(1)}, bf16[1,3,4,4,64,64]{4,5,3,2,1,0:T(8,128)(2,1)S(1)}, u32[]{:S(2)}, u32[]{:S(2)}) collective-permute-start(bf16[1,3,4,4,64,64]{4,5,3,2,1,0:T(8,128)(2,1)S(1)} %pad_maximum_fusion.7), channel_id=1, source_target_pairs={{1,0},{2,1},{3,2},{0,3},{5,4},{6,5},{7,6},{4,7},{9,8},{10,9},{11,1... | collective-permute-start | bytes 1179656 | tf_op jit(solution)/shard_map/ppermute | solution.py:20
  80.7 12.3 %collective-permute-start.8 = (bf16[1,1,4,4,64,64]{4,5,3,2,1,0:T(8,128)(2,1)S(1)}, bf16[1,1,4,4,64,64]{4,5,3,2,1,0:T(8,128)(2,1)S(1)}, u32[]{:S(2)}, u32[]{:S(2)}) collective-permute-start(bf16[1,1,4,4,64,64]{4,5,3,2,1,0:T(8,128)(2,1)S(1)} %fusion.32), channel_id=1, source_target_pairs={{0,4},{4,8},{8,12},{12,16},{16,20},{20,24},{24,28},{28,0},{1,5},{5... | collective-permute-start | bytes 393224 | tf_op jit(solution)/shard_map/ppermute | solution.py:17
  80.7 15.5 %collective-permute-start.9 = (bf16[1,1,4,4,64,64]{4,5,3,2,1,0:T(8,128)(2,1)S(1)}, bf16[1,1,4,4,64,64]{4,5,3,2,1,0:T(8,128)(2,1)S(1)}, u32[]{:S(2)}, u32[]{:S(2)}) collective-permute-start(bf16[1,1,4,4,64,64]{4,5,3,2,1,0:T(8,128)(2,1)S(1)} %fusion.32), channel_id=1, source_target_pairs={{4,0},{8,4},{12,8},{16,12},{20,16},{24,20},{28,24},{0,28},{5,1},{9... | collective-permute-start | bytes 393224 | tf_op jit(solution)/shard_map/ppermute | solution.py:20
  96.4 18.0 %collective-permute-start.10 = (bf16[1,3,4,4,64,64]{4,5,3,2,1,0:T(8,128)(2,1)S(1)}, bf16[1,3,4,4,64,64]{4,5,3,2,1,0:T(8,128)(2,1)S(1)}, u32[]{:S(2)}, u32[]{:S(2)}) collective-permute-start(bf16[1,3,4,4,64,64]{4,5,3,2,1,0:T(8,128)(2,1)S(1)} %pad_maximum_fusion.8), channel_id=1, source_target_pairs={{0,1},{1,2},{2,3},{3,0},{4,5},{5,6},{6,7},{7,4},{8,9},{9,10},{10,1... | collective-permute-start | bytes 1179656 | tf_op jit(solution)/shard_map/ppermute | solution.py:17
  96.5 18.9 %collective-permute-start.11 = (bf16[1,3,4,4,64,64]{4,5,3,2,1,0:T(8,128)(2,1)S(1)}, bf16[1,3,4,4,64,64]{4,5,3,2,1,0:T(8,128)(2,1)S(1)}, u32[]{:S(2)}, u32[]{:S(2)}) collective-permute-start(bf16[1,3,4,4,64,64]{4,5,3,2,1,0:T(8,128)(2,1)S(1)} %pad_maximum_fusion.8), channel_id=1, source_target_pairs={{1,0},{2,1},{3,2},{0,3},{5,4},{6,5},{7,6},{4,7},{9,8},{10,9},{11,1... | collective-permute-start | bytes 1179656 | tf_op jit(solution)/shard_map/ppermute | solution.py:20
  119.3 12.3 %collective-permute-start.12 = (bf16[1,1,4,4,64,64]{4,5,3,2,1,0:T(8,128)(2,1)S(1)}, bf16[1,1,4,4,64,64]{4,5,3,2,1,0:T(8,128)(2,1)S(1)}, u32[]{:S(2)}, u32[]{:S(2)}) collective-permute-start(bf16[1,1,4,4,64,64]{4,5,3,2,1,0:T(8,128)(2,1)S(1)} %fusion.33), channel_id=1, source_target_pairs={{0,4},{4,8},{8,12},{12,16},{16,20},{20,24},{24,28},{28,0},{1,5},{5... | collective-permute-start | bytes 393224 | tf_op jit(solution)/shard_map/ppermute | solution.py:17
  119.4 15.5 %collective-permute-start.13 = (bf16[1,1,4,4,64,64]{4,5,3,2,1,0:T(8,128)(2,1)S(1)}, bf16[1,1,4,4,64,64]{4,5,3,2,1,0:T(8,128)(2,1)S(1)}, u32[]{:S(2)}, u32[]{:S(2)}) collective-permute-start(bf16[1,1,4,4,64,64]{4,5,3,2,1,0:T(8,128)(2,1)S(1)} %fusion.33), channel_id=1, source_target_pairs={{4,0},{8,4},{12,8},{16,12},{20,16},{24,20},{28,24},{0,28},{5,1},{9... | collective-permute-start | bytes 393224 | tf_op jit(solution)/shard_map/ppermute | solution.py:20
  135.0 18.0 %collective-permute-start.14 = (bf16[1,3,4,4,64,64]{4,5,3,2,1,0:T(8,128)(2,1)S(1)}, bf16[1,3,4,4,64,64]{4,5,3,2,1,0:T(8,128)(2,1)S(1)}, u32[]{:S(2)}, u32[]{:S(2)}) collective-permute-start(bf16[1,3,4,4,64,64]{4,5,3,2,1,0:T(8,128)(2,1)S(1)} %pad_maximum_fusion.9), channel_id=1, source_target_pairs={{0,1},{1,2},{2,3},{3,0},{4,5},{5,6},{6,7},{7,4},{8,9},{9,10},{10,1... | collective-permute-start | bytes 1179656 | tf_op jit(solution)/shard_map/ppermute | solution.py:17
  135.1 18.9 %collective-permute-start.15 = (bf16[1,3,4,4,64,64]{4,5,3,2,1,0:T(8,128)(2,1)S(1)}, bf16[1,3,4,4,64,64]{4,5,3,2,1,0:T(8,128)(2,1)S(1)}, u32[]{:S(2)}, u32[]{:S(2)}) collective-permute-start(bf16[1,3,4,4,64,64]{4,5,3,2,1,0:T(8,128)(2,1)S(1)} %pad_maximum_fusion.9), channel_id=1, source_target_pairs={{1,0},{2,1},{3,2},{0,3},{5,4},{6,5},{7,6},{4,7},{9,8},{10,9},{11,1... | collective-permute-start | bytes 1179656 | tf_op jit(solution)/shard_map/ppermute | solution.py:20
  157.2 12.3 %collective-permute-start.16 = (bf16[1,1,4,4,64,64]{4,5,3,2,1,0:T(8,128)(2,1)S(1)}, bf16[1,1,4,4,64,64]{4,5,3,2,1,0:T(8,128)(2,1)S(1)}, u32[]{:S(2)}, u32[]{:S(2)}) collective-permute-start(bf16[1,1,4,4,64,64]{4,5,3,2,1,0:T(8,128)(2,1)S(1)} %fusion.34), channel_id=1, source_target_pairs={{0,4},{4,8},{8,12},{12,16},{16,20},{20,24},{24,28},{28,0},{1,5},{5... | collective-permute-start | bytes 393224 | tf_op jit(solution)/shard_map/ppermute | solution.py:17
  157.3 15.1 %collective-permute-start.17 = (bf16[1,1,4,4,64,64]{4,5,3,2,1,0:T(8,128)(2,1)S(1)}, bf16[1,1,4,4,64,64]{4,5,3,2,1,0:T(8,128)(2,1)S(1)}, u32[]{:S(2)}, u32[]{:S(2)}) collective-permute-start(bf16[1,1,4,4,64,64]{4,5,3,2,1,0:T(8,128)(2,1)S(1)} %fusion.34), channel_id=1, source_target_pairs={{4,0},{8,4},{12,8},{16,12},{20,16},{24,20},{28,24},{0,28},{5,1},{9... | collective-permute-start | bytes 393224 | tf_op jit(solution)/shard_map/ppermute | solution.py:20
  172.6 18.0 %collective-permute-start.18 = (bf16[1,3,4,4,64,64]{4,5,3,2,1,0:T(8,128)(2,1)S(1)}, bf16[1,3,4,4,64,64]{4,5,3,2,1,0:T(8,128)(2,1)S(1)}, u32[]{:S(2)}, u32[]{:S(2)}) collective-permute-start(bf16[1,3,4,4,64,64]{4,5,3,2,1,0:T(8,128)(2,1)S(1)} %pad_maximum_fusion.10), channel_id=1, source_target_pairs={{0,1},{1,2},{2,3},{3,0},{4,5},{5,6},{6,7},{7,4},{8,9},{9,10},{10,1... | collective-permute-start | bytes 1179656 | tf_op jit(solution)/shard_map/ppermute | solution.py:17
  172.7 18.9 %collective-permute-start.19 = (bf16[1,3,4,4,64,64]{4,5,3,2,1,0:T(8,128)(2,1)S(1)}, bf16[1,3,4,4,64,64]{4,5,3,2,1,0:T(8,128)(2,1)S(1)}, u32[]{:S(2)}, u32[]{:S(2)}) collective-permute-start(bf16[1,3,4,4,64,64]{4,5,3,2,1,0:T(8,128)(2,1)S(1)} %pad_maximum_fusion.10), channel_id=1, source_target_pairs={{1,0},{2,1},{3,2},{0,3},{5,4},{6,5},{7,6},{4,7},{9,8},{10,9},{11,1... | collective-permute-start | bytes 1179656 | tf_op jit(solution)/shard_map/ppermute | solution.py:20
  194.2 12.3 %collective-permute-start.20 = (bf16[1,1,4,4,64,64]{4,5,3,2,1,0:T(8,128)(2,1)S(1)}, bf16[1,1,4,4,64,64]{4,5,3,2,1,0:T(8,128)(2,1)S(1)}, u32[]{:S(2)}, u32[]{:S(2)}) collective-permute-start(bf16[1,1,4,4,64,64]{4,5,3,2,1,0:T(8,128)(2,1)S(1)} %fusion.35), channel_id=1, source_target_pairs={{0,4},{4,8},{8,12},{12,16},{16,20},{20,24},{24,28},{28,0},{1,5},{5... | collective-permute-start | bytes 393224 | tf_op jit(solution)/shard_map/ppermute | solution.py:17
  194.3 15.0 %collective-permute-start.21 = (bf16[1,1,4,4,64,64]{4,5,3,2,1,0:T(8,128)(2,1)S(1)}, bf16[1,1,4,4,64,64]{4,5,3,2,1,0:T(8,128)(2,1)S(1)}, u32[]{:S(2)}, u32[]{:S(2)}) collective-permute-start(bf16[1,1,4,4,64,64]{4,5,3,2,1,0:T(8,128)(2,1)S(1)} %fusion.35), channel_id=1, source_target_pairs={{4,0},{8,4},{12,8},{16,12},{20,16},{24,20},{28,24},{0,28},{5,1},{9... | collective-permute-start | bytes 393224 | tf_op jit(solution)/shard_map/ppermute | solution.py:20
  209.4 18.0 %collective-permute-start.22 = (bf16[1,3,4,4,64,64]{4,5,3,2,1,0:T(8,128)(2,1)S(1)}, bf16[1,3,4,4,64,64]{4,5,3,2,1,0:T(8,128)(2,1)S(1)}, u32[]{:S(2)}, u32[]{:S(2)}) collective-permute-start(bf16[1,3,4,4,64,64]{4,5,3,2,1,0:T(8,128)(2,1)S(1)} %pad_maximum_fusion.11), channel_id=1, source_target_pairs={{0,1},{1,2},{2,3},{3,0},{4,5},{5,6},{6,7},{7,4},{8,9},{9,10},{10,1... | collective-permute-start | bytes 1179656 | tf_op jit(solution)/shard_map/ppermute | solution.py:17
  209.5 18.9 %collective-permute-start.23 = (bf16[1,3,4,4,64,64]{4,5,3,2,1,0:T(8,128)(2,1)S(1)}, bf16[1,3,4,4,64,64]{4,5,3,2,1,0:T(8,128)(2,1)S(1)}, u32[]{:S(2)}, u32[]{:S(2)}) collective-permute-start(bf16[1,3,4,4,64,64]{4,5,3,2,1,0:T(8,128)(2,1)S(1)} %pad_maximum_fusion.11), channel_id=1, source_target_pairs={{1,0},{2,1},{3,2},{0,3},{5,4},{6,5},{7,6},{4,7},{9,8},{10,9},{11,1... | collective-permute-start | bytes 1179656 | tf_op jit(solution)/shard_map/ppermute | solution.py:20
  (11 other events, 88.5 us)
where the time goes:
time: 273 us
  waiting for transfers between devices  152 us (56%)
  starting transfers between devices  40.7 us (15%)
  blocking collectives  39.7 us (15%)
  matrix products  19.6 us (7%)
  other arithmetic  10.9 us (4%)
  local copies, waits for them, and re-layouts  8.35 us (3%)
    ppermute x12, waiting for transfers between devices, padded(): lax.ppermute(lax.slice_in_dim(block, block.shape[dim] - width, None, axis...  129 us
    psum x1, blocking collectives, body(): summed = lax.psum(jnp.stack([real_sum, imag_sum]), ('space', 'tm'))  39.7 us
    ppermute x12, starting transfers between devices, padded(): lax.ppermute(lax.slice_in_dim(block, 0, width, axis=dim), axis, backward)  36.8 us
    ppermute x12, waiting for transfers between devices, padded(): lax.ppermute(lax.slice_in_dim(block, 0, width, axis=dim), axis, backward)  22.9 us
    dot_general x57, matrix products, apply_wide(): jnp.einsum('tzxyij,tzxyjk->tzxyik', blocks, widened, preferred_element_ty...  19.3 us
  transfers between devices with their start and end apart: 24, of which 24 were waited for; matrix products, arithmetic and copies ran while one was open for 5% of the time, Pallas kernels for 0%

commit v1 on v0

v1 whole, which is shorter than its diff:
```python
import functools
import math

import jax
import jax.numpy as jnp
from jax import lax
from jax.experimental import pallas as pl
from jax.experimental.pallas import tpu as pltpu
from jax.sharding import PartitionSpec as P

SWEEPS = 4
F32 = jnp.float32
VMEM = pl.BlockSpec(memory_space=pltpu.VMEM)
SMEM = pl.BlockSpec(memory_space=pltpu.SMEM)


def dot(a, b):
    return jnp.dot(a, b, preferred_element_type=F32)


def widen(field):
    half = field.shape[1] // 2
    re, im = field[:, :half], field[:, half:]
    return jnp.concatenate(
        [field, jnp.concatenate([-im, re], axis=1)], axis=0
    )


def pick(product, sites):
    rows = product.shape[0] // sites
    half = product.shape[1] // 2
    lane = lax.broadcasted_iota(jnp.int32, (rows, 2 * half), 1) % half
    out = product[:rows]
    for y in range(1, sites):
        out = jnp.where(lane >= y * (half // sites), product[y * rows : (y + 1) * rows], out)
    return out


def turn(field, shift):
    half = field.shape[1] // 2
    re, im = field[:, :half].astype(F32), field[:, half:].astype(F32)
    return jnp.concatenate(
        [pltpu.roll(re, shift % half, 1), pltpu.roll(im, shift % half, 1)], axis=1
    ).astype(field.dtype)


def first_kernel(order, rhs, diag, source, out):
    lx, ly = rhs.shape[0], rhs.shape[1]
    cols = order.shape[1]
    half = ly * cols
    row = lax.broadcasted_iota(jnp.int32, (2 * cols, 2 * half), 0)
    lane = lax.broadcasted_iota(jnp.int32, (2 * cols, 2 * half), 1)
    wanted = jnp.concatenate([order[...]] * (2 * ly), axis=1)
    wanted = wanted + jnp.where(lane >= half, cols, 0)
    site = (lane % half) // cols
    hot = row == wanted
    places = [jnp.where(hot & (site == y), 1.0, 0.0).astype(jnp.bfloat16) for y in range(ly)]
    for x in range(lx):
        field = dot(rhs[x, 0], places[0])
        for y in range(1, ly):
            field = field + dot(rhs[x, y], places[y])
        field = field.astype(jnp.bfloat16)
        source[x] = field
        out[x] = pick(dot(diag[x], widen(field)), ly).astype(jnp.bfloat16)


def local_kernel(sites, hops, source, field, total):
    lx = field.shape[0]
    cols = field.shape[2] // (2 * sites)
    for x in range(lx):
        here = field[x]
        right = jnp.concatenate(
            [
                widen(field[(x + 1) % lx]),
                widen(field[(x - 1) % lx]),
                widen(turn(here, -cols)),
                widen(turn(here, cols)),
            ],
            axis=0,
        )
        left = jnp.concatenate([hops[e, x] for e in range(4)], axis=1)
        total[x] = source[x].astype(F32) + pick(dot(left, right), sites)


def remote_kernel(sites, which, hops, diag, total, *refs):
    fields, out = refs[:-1], refs[-1]
    lx = out.shape[0]
    for x in range(lx):
        right = jnp.concatenate([widen(f[x]) for f in fields], axis=0)
        left = jnp.concatenate([hops[which[n], x] for n in range(len(fields))], axis=1)
        residue = (total[x] + pick(dot(left, right), sites)).astype(jnp.bfloat16)
        out[x] = pick(dot(diag[x], widen(residue)), sites).astype(jnp.bfloat16)


def insert_kernel(sites, current, diag, field, source, out):
    lx = out.shape[0]
    for x in range(lx):
        inserted = pick(dot(current[x], widen(field[x])), sites).astype(jnp.bfloat16)
        source[x] = inserted
        out[x] = pick(dot(diag[x], widen(inserted)), sites).astype(jnp.bfloat16)


def leave_kernel(field, out):
    lx, ly = out.shape[0], out.shape[1]
    half = field.shape[2] // 2
    cols = half // ly
    row = lax.broadcasted_iota(jnp.int32, (2 * half, 2 * cols), 0)
    lane = lax.broadcasted_iota(jnp.int32, (2 * half, 2 * cols), 1)
    for y in range(ly):
        start = jnp.where(lane >= cols, half - cols, 0) + y * cols
        place = jnp.where(row == lane + start, 1.0, 0.0).astype(jnp.bfloat16)
        for x in range(lx):
            out[x, y] = dot(field[x], place).astype(jnp.bfloat16)


def gram_kernel(sites, left, right, out):
    lx, comps, width = left.shape
    half = width // 2
    cols = half // sites
    a = left[...].reshape(lx * comps, width)
    b = right[...].reshape(lx * comps, width)
    full = lax.dot_general(a, b, (((0,), (0,)), ((), ())), preferred_element_type=F32)
    real = full[:half, :half] + full[half:, half:]
    imag = full[:half, half:] - full[half:, :half]
    lane = lax.broadcasted_iota(jnp.int32, (cols, half), 1) // cols
    parts = []
    for m in (real, imag):
        folded = m[:cols]
        for y in range(1, sites):
            folded = jnp.where(lane == y, m[y * cols : (y + 1) * cols], folded)
        parts.append(folded)
    out[0] = parts[0]
    out[1] = parts[1]


def call(kernel, outs, cost, *args, smem=()):
    flops, moved = cost
    return pl.pallas_call(
        kernel,
        out_shape=outs,
        in_specs=[SMEM if i in smem else VMEM for i in range(len(args))],
        out_specs=jax.tree.map(lambda _: VMEM, outs),
        compiler_params=pltpu.CompilerParams(vmem_limit_bytes=24 * 2**20),
        cost_estimate=pl.CostEstimate(flops=flops, bytes_accessed=moved, transcendentals=0),
    )(*args)


def swaps(axis):
    count = lax.axis_size(axis)
    if count % 2:
        return (
            [(i, (i - 1) % count) for i in range(count)],
            [(i, (i + 1) % count) for i in range(count)],
        )
    near = [(i, i ^ 1) for i in range(count)]
    far = [(i, (i + 1 if i % 2 else i - 1) % count) for i in range(count)]
    return near, far


def parity(axis):
    return lax.axis_index(axis) % 2 if lax.axis_size(axis) % 2 == 0 else jnp.int32(0)


def exchange(field):
    near_s, far_s = swaps("space")
    near_t, far_t = swaps("tm")
    y = lax.ppermute(field, "tm", far_t)
    c = lax.ppermute(field, "tm", near_t)
    w = lax.ppermute(field, "space", far_s)
    e = lax.ppermute(field, "space", near_s)
    return e, w, c, y


def total_sum(value):
    for axis in ("tm", "space"):
        count = lax.axis_size(axis)
        if count & (count - 1):
            value = lax.psum(value, axis)
            continue
        step = 1
        while step < count:
            value = value + lax.ppermute(value, axis, [(i, i ^ step) for i in range(count)])
            step *= 2
    return value


def body(right_side, batch_order, light_diag, light_hops, charm_diag, charm_hops, current_blocks):
    lt, lz, lx, ly, comps, wide = right_side.shape
    assert lt == 1 and lz == 1
    cols = wide // 2
    rows = ly * comps
    rhs = right_side.reshape(lx, ly, comps, wide)
    order = batch_order.reshape(1, cols)
    light_p, charm_p, current = (a.reshape(lx, rows, 2 * comps) for a in (light_diag, charm_diag, current_blocks))
    light_h, charm_h = (a.reshape(8, lx, rows, 2 * comps) for a in (light_hops, charm_hops))
    shape = (lx, comps, 2 * ly * cols)
    field_t = jax.ShapeDtypeStruct(shape, jnp.bfloat16)
    total_t = jax.ShapeDtypeStruct(shape, F32)
    odd_s, odd_t = parity("space"), parity("tm")
    which = jnp.stack([4 + odd_s, 5 - odd_s, 6 + odd_t, 7 - odd_t]).astype(jnp.int32)
    unit = 2 * lx * rows * 2 * comps * 2 * ly * cols

    def sweeps(hops, diag, source, field):
        for _ in range(SWEEPS - 1):
            got = exchange(field)
            total = call(
                functools.partial(local_kernel, ly), total_t, (4 * unit, 2 * 2**20), hops, source, field
            )
            field = call(
                functools.partial(remote_kernel, ly), field_t, (5 * unit, 2 * 2**20), which, hops, diag, total, *got,
                smem=(0,),
            )
        return field

    source, field = call(first_kernel, (field_t, field_t), (2 * unit, 2**20), order, rhs, light_p)
    light = sweeps(light_h, light_p, source, field)
    inserted, field = call(
        functools.partial(insert_kernel, ly), (field_t, field_t), (2 * unit, 2**20), current, charm_p, light
    )
    seq = sweeps(charm_h, charm_p, inserted, field)
    part = call(
        functools.partial(gram_kernel, ly),
        jax.ShapeDtypeStruct((2, cols, ly * cols), F32),
        (unit, 2**20),
        light,
        seq,
    )
    out_t = jax.ShapeDtypeStruct((lx, ly, comps, wide), jnp.bfloat16)
    light_out = call(leave_kernel, out_t, (unit, 2**20), light)
    seq_out = call(leave_kernel, out_t, (unit, 2**20), seq)
    summed = total_sum(part.reshape(2, cols, ly, cols).sum(axis=2))
    site_count = lx * ly * lax.axis_size("space") * lax.axis_size("tm")
    return (
        light_out.reshape(right_side.shape),
        seq_out.reshape(right_side.shape),
        summed * (1.0 / math.sqrt(site_count * comps)),
    )


def solution(mesh):
    site = P("tm", "space", None, None, None, None)
    hops = P(None, "tm", "space", None, None, None, None)
    return jax.shard_map(
        body,
        mesh=mesh,
        in_specs=(site, P(), site, hops, site, hops, site),
        out_specs=(site, site, P()),
        check_vma=False,
    )
```

time: 273 us -> 89.8 us (0.33)
  waiting for transfers between devices: 152 us -> 37.2 us
  blocking collectives: 39.7 us -> 0 us
  matrix products: 19.6 us -> 0 us
  Pallas kernels: 0 us -> 17.2 us
  starting transfers between devices: 40.7 us -> 29.2 us
  other arithmetic: 10.9 us -> 0.81 us
  local copies, waits for them, and re-layouts: 8.35 us -> 4.28 us
    ppermute x24 -> x29, waiting for transfers between devices: 152 us -> 37.2 us  [the longest x5 12.7 us: total_sum(): lax.ppermute(value, axis, [(i, i ^ step) for i in range(count)])]
    psum x1 -> x0, blocking collectives: 39.7 us -> none  [body(): summed = lax.psum(jnp.stack([real_sum, imag_sum]), ('space', 'tm'))]
    dot_general x58 -> x0, matrix products: 19.6 us -> none  [the longest x57 19.3 us: apply_wide(): jnp.einsum('tzxyij,tzxyjk->tzxyik', blocks, widened, preferred_element_ty...]
    pallas_call x0 -> x17, Pallas kernels: none -> 17.2 us  [call(): pl.pallas_call(kernel, out_shape=outs, in_specs=[SMEM if i in smem else V...]
    ppermute x24 -> x29, starting transfers between devices: 40.7 us -> 29.2 us  [the longest x6 15 us: exchange(): w = lax.ppermute(field, 'space', far_s)]
    concatenate x19 -> x0, other arithmetic: 6.87 us -> none  [the longest x12 5.25 us: padded(): block = jnp.concatenate([low, block, high], axis=dim)]
  transfers between devices with their start and end apart: 24 -> 29, of which waited for: 24 -> 18; matrix products, arithmetic and copies ran while one was open for 5% -> 0% of each run, Pallas kernels for 0% -> 5%
where the time goes in v1:
time: 89.8 us; the launch traced here: 89.6 us
  waiting for transfers between devices  37.2 us (41%)
  starting transfers between devices  29.2 us (33%)
  Pallas kernels  17.2 us (19%)
  local copies, waits for them, and re-layouts  4.28 us (5%)
    pallas_call x17, Pallas kernels, call(): pl.pallas_call(kernel, out_shape=outs, in_specs=[SMEM if i in smem else V...  17.2 us
    ppermute x6, starting transfers between devices, exchange(): w = lax.ppermute(field, 'space', far_s)  15 us
    ppermute x5, waiting for transfers between devices, total_sum(): lax.ppermute(value, axis, [(i, i ^ step) for i in range(count)])  12.7 us
    ppermute x6, waiting for transfers between devices, exchange(): e = lax.ppermute(field, 'space', near_s)  12 us
    ppermute x6, waiting for transfers between devices, exchange(): w = lax.ppermute(field, 'space', far_s)  10.5 us
    ppermute x6, starting transfers between devices, exchange(): y = lax.ppermute(field, 'tm', far_t)  6.51 us
    ppermute x6, starting transfers between devices, exchange(): e = lax.ppermute(field, 'space', near_s)  4.28 us
    unnamed x18, local copies, waits for them, and re-layouts  4.17 us
  transfers between devices with their start and end apart: 29, of which 18 were waited for; matrix products, arithmetic and copies ran while one was open for 0% of the time, Pallas kernels for 5%

profile of v1, /device:TPU:0, one launch (start us, length us, event | category | flops | bytes accessed | tf_op | source)
XLA Modules:
  0.0 89.6 jit_solution(17702486920062487698)
XLA Ops:
  3.9 3.0 %collective-permute-start = (bf16[4,64,256]{2,1,0:T(8,128)(2,1)S(1)}, bf16[4,64,256]{2,1,0:T(8,128)(2,1)S(1)}, u32[]{:S(2)}, u32[]{:S(2)}) collective-permute-start(bf16[4,64,256]{2,1,0:T(8,128)(2,1)S(1)} %get-tuple-element.8.field), channel_id=1, source_target_pairs={{0,4},{4,0},{8,12},{12,8},{16,20},{20,16},{24,28},{28,24},{1,5},{5... | collective-permute-start | bytes 393224 | tf_op jit(solution)/shard_map/ppermute | solution.py:170
  6.9 3.6 %collective-permute-start.1 = (bf16[4,64,256]{2,1,0:T(8,128)(2,1)S(1)}, bf16[4,64,256]{2,1,0:T(8,128)(2,1)S(1)}, u32[]{:S(2)}, u32[]{:S(2)}) collective-permute-start(bf16[4,64,256]{2,1,0:T(8,128)(2,1)S(1)} %get-tuple-element.8.field), channel_id=1, source_target_pairs={{0,28},{4,8},{8,4},{12,16},{16,12},{20,24},{24,20},{28,0},{1,29},{... | collective-permute-start | bytes 393224 | tf_op jit(solution)/shard_map/ppermute | solution.py:169
  15.6 1.8 %shard_map.96.field = bf16[4,64,256]{2,1,0:T(8,128)(2,1)S(1)} custom-call(s32[4]{0:T(128)S(1)} %pad_add_fusion.which, bf16[8,4,256,128]{3,2,1,0:T(8,128)(2,1)S(1)} %bitcast.14, bf16[4,256,128]{2,1,0:T(8,128)(2,1)S(1)} %bitcast.26, f32[4,64,256]{2,1,0:T(8,128)S(1)} %shard_map.95.total, bf16[4,64,256]{2,1,0:T(8,128)(2,1)S(1)} %collective-permute-done.refs_0_, ...), custom_call_target="tpu_custom_call" | custom-call | flops 335544320 | bytes 2097152 | tf_op jit(solution)/shard_map/pallas_call | solution.py:138
  17.5 2.9 %collective-permute-start.5 = (bf16[4,64,256]{2,1,0:T(8,128)(2,1)S(1)}, bf16[4,64,256]{2,1,0:T(8,128)(2,1)S(1)}, u32[]{:S(2)}, u32[]{:S(2)}) collective-permute-start(bf16[4,64,256]{2,1,0:T(8,128)(2,1)S(1)} %shard_map.96.field), channel_id=1, source_target_pairs={{0,28},{4,8},{8,4},{12,16},{16,12},{20,24},{24,20},{28,0},{1,29},{... | collective-permute-start | bytes 393224 | tf_op jit(solution)/shard_map/ppermute | solution.py:169
  24.0 2.2 %collective-permute-done.5.refs_1_ = bf16[4,64,256]{2,1,0:T(8,128)(2,1)S(1)} collective-permute-done((bf16[4,64,256]{2,1,0:T(8,128)(2,1)S(1)}, bf16[4,64,256]{2,1,0:T(8,128)(2,1)S(1)}, u32[]{:S(2)}, u32[]{:S(2)}) %collective-permute-start.5) | collective-permute-done | bytes 131104 | tf_op jit(solution)/shard_map/ppermute | solution.py:169
  26.2 1.8 %shard_map.98.field = bf16[4,64,256]{2,1,0:T(8,128)(2,1)S(1)} custom-call(s32[4]{0:T(128)S(1)} %pad_add_fusion.which, bf16[8,4,256,128]{3,2,1,0:T(8,128)(2,1)S(1)} %bitcast.16, bf16[4,256,128]{2,1,0:T(8,128)(2,1)S(1)} %bitcast.27, f32[4,64,256]{2,1,0:T(8,128)S(1)} %shard_map.97.total, bf16[4,64,256]{2,1,0:T(8,128)(2,1)S(1)} %collective-permute-done.4.refs_0_, ...), custom_call_target="tpu_custom_call" | custom-call | flops 335544320 | bytes 2097152 | tf_op jit(solution)/shard_map/pallas_call | solution.py:138
  30.0 1.9 %collective-permute-start.9 = (bf16[4,64,256]{2,1,0:T(8,128)(2,1)S(1)}, bf16[4,64,256]{2,1,0:T(8,128)(2,1)S(1)}, u32[]{:S(2)}, u32[]{:S(2)}) collective-permute-start(bf16[4,64,256]{2,1,0:T(8,128)(2,1)S(1)} %shard_map.98.field), channel_id=1, source_target_pairs={{0,28},{4,8},{8,4},{12,16},{16,12},{20,24},{24,20},{28,0},{1,29},{... | collective-permute-start | bytes 393224 | tf_op jit(solution)/shard_map/ppermute | solution.py:169
  33.4 2.5 %collective-permute-done.8.refs_0_ = bf16[4,64,256]{2,1,0:T(8,128)(2,1)S(1)} collective-permute-done((bf16[4,64,256]{2,1,0:T(8,128)(2,1)S(1)}, bf16[4,64,256]{2,1,0:T(8,128)(2,1)S(1)}, u32[]{:S(2)}, u32[]{:S(2)}) %collective-permute-start.8) | collective-permute-done | bytes 131104 | tf_op jit(solution)/shard_map/ppermute | solution.py:170
  35.8 2.2 %collective-permute-done.9.refs_1_ = bf16[4,64,256]{2,1,0:T(8,128)(2,1)S(1)} collective-permute-done((bf16[4,64,256]{2,1,0:T(8,128)(2,1)S(1)}, bf16[4,64,256]{2,1,0:T(8,128)(2,1)S(1)}, u32[]{:S(2)}, u32[]{:S(2)}) %collective-permute-start.9) | collective-permute-done | bytes 131104 | tf_op jit(solution)/shard_map/ppermute | solution.py:169
  38.0 1.8 %shard_map.100.field.left = bf16[4,64,256]{2,1,0:T(8,128)(2,1)S(1)} custom-call(s32[4]{0:T(128)S(1)} %pad_add_fusion.which, bf16[8,4,256,128]{3,2,1,0:T(8,128)(2,1)S(1)} %bitcast.18, bf16[4,256,128]{2,1,0:T(8,128)(2,1)S(1)} %bitcast.28, f32[4,64,256]{2,1,0:T(8,128)S(1)} %shard_map.99.total, bf16[4,64,256]{2,1,0:T(8,128)(2,1)S(1)} %collective-permute-done.8.refs_0_, ...), custom_call_target="tpu_custom_call" | custom-call | flops 335544320 | bytes 2097152 | tf_op jit(solution)/shard_map/pallas_call | solution.py:138
  40.8 1.9 %collective-permute-start.13 = (bf16[4,64,256]{2,1,0:T(8,128)(2,1)S(1)}, bf16[4,64,256]{2,1,0:T(8,128)(2,1)S(1)}, u32[]{:S(2)}, u32[]{:S(2)}) collective-permute-start(bf16[4,64,256]{2,1,0:T(8,128)(2,1)S(1)} %get-tuple-element.10.field), channel_id=1, source_target_pairs={{0,28},{4,8},{8,4},{12,16},{16,12},{20,24},{24,20},{28,0},{1,29},{... | collective-permute-start | bytes 393224 | tf_op jit(solution)/shard_map/ppermute | solution.py:169
  43.8 3.1 %collective-permute-done.12.refs_0_ = bf16[4,64,256]{2,1,0:T(8,128)(2,1)S(1)} collective-permute-done((bf16[4,64,256]{2,1,0:T(8,128)(2,1)S(1)}, bf16[4,64,256]{2,1,0:T(8,128)(2,1)S(1)}, u32[]{:S(2)}, u32[]{:S(2)}) %collective-permute-start.12) | collective-permute-done | bytes 131104 | tf_op jit(solution)/shard_map/ppermute | solution.py:170
  48.5 1.8 %shard_map.104.field = bf16[4,64,256]{2,1,0:T(8,128)(2,1)S(1)} custom-call(s32[4]{0:T(128)S(1)} %pad_add_fusion.which, bf16[8,4,256,128]{3,2,1,0:T(8,128)(2,1)S(1)} %bitcast.20, bf16[4,256,128]{2,1,0:T(8,128)(2,1)S(1)} %bitcast.30, f32[4,64,256]{2,1,0:T(8,128)S(1)} %shard_map.103.total, bf16[4,64,256]{2,1,0:T(8,128)(2,1)S(1)} %collective-permute-done.12.refs_0_, ...), custom_call_target="tpu_custom_call" | custom-call | flops 335544320 | bytes 2097152 | tf_op jit(solution)/shard_map/pallas_call | solution.py:138
  50.5 2.2 %collective-permute-start.17 = (bf16[4,64,256]{2,1,0:T(8,128)(2,1)S(1)}, bf16[4,64,256]{2,1,0:T(8,128)(2,1)S(1)}, u32[]{:S(2)}, u32[]{:S(2)}) collective-permute-start(bf16[4,64,256]{2,1,0:T(8,128)(2,1)S(1)} %shard_map.104.field), channel_id=1, source_target_pairs={{0,28},{4,8},{8,4},{12,16},{16,12},{20,24},{24,20},{28,0},{1,29},{... | collective-permute-start | bytes 393224 | tf_op jit(solution)/shard_map/ppermute | solution.py:169
  53.7 2.8 %collective-permute-done.16.refs_0_ = bf16[4,64,256]{2,1,0:T(8,128)(2,1)S(1)} collective-permute-done((bf16[4,64,256]{2,1,0:T(8,128)(2,1)S(1)}, bf16[4,64,256]{2,1,0:T(8,128)(2,1)S(1)}, u32[]{:S(2)}, u32[]{:S(2)}) %collective-permute-start.16) | collective-permute-done | bytes 131104 | tf_op jit(solution)/shard_map/ppermute | solution.py:170
  56.5 2.2 %collective-permute-done.17.refs_1_ = bf16[4,64,256]{2,1,0:T(8,128)(2,1)S(1)} collective-permute-done((bf16[4,64,256]{2,1,0:T(8,128)(2,1)S(1)}, bf16[4,64,256]{2,1,0:T(8,128)(2,1)S(1)}, u32[]{:S(2)}, u32[]{:S(2)}) %collective-permute-start.17) | collective-permute-done | bytes 131104 | tf_op jit(solution)/shard_map/ppermute | solution.py:169
  58.7 1.8 %shard_map.106.field = bf16[4,64,256]{2,1,0:T(8,128)(2,1)S(1)} custom-call(s32[4]{0:T(128)S(1)} %pad_add_fusion.which, bf16[8,4,256,128]{3,2,1,0:T(8,128)(2,1)S(1)} %bitcast.22, bf16[4,256,128]{2,1,0:T(8,128)(2,1)S(1)} %bitcast.31, f32[4,64,256]{2,1,0:T(8,128)S(1)} %shard_map.105.total, bf16[4,64,256]{2,1,0:T(8,128)(2,1)S(1)} %collective-permute-done.16.refs_0_, ...), custom_call_target="tpu_custom_call" | custom-call | flops 335544320 | bytes 2097152 | tf_op jit(solution)/shard_map/pallas_call | solution.py:138
  60.9 2.6 %collective-permute-start.21 = (bf16[4,64,256]{2,1,0:T(8,128)(2,1)S(1)}, bf16[4,64,256]{2,1,0:T(8,128)(2,1)S(1)}, u32[]{:S(2)}, u32[]{:S(2)}) collective-permute-start(bf16[4,64,256]{2,1,0:T(8,128)(2,1)S(1)} %shard_map.106.field), channel_id=1, source_target_pairs={{0,28},{4,8},{8,4},{12,16},{16,12},{20,24},{24,20},{28,0},{1,29},{... | collective-permute-start | bytes 393224 | tf_op jit(solution)/shard_map/ppermute | solution.py:169
  64.5 2.2 %collective-permute-done.20.refs_0_ = bf16[4,64,256]{2,1,0:T(8,128)(2,1)S(1)} collective-permute-done((bf16[4,64,256]{2,1,0:T(8,128)(2,1)S(1)}, bf16[4,64,256]{2,1,0:T(8,128)(2,1)S(1)}, u32[]{:S(2)}, u32[]{:S(2)}) %collective-permute-start.20) | collective-permute-done | bytes 131104 | tf_op jit(solution)/shard_map/ppermute | solution.py:170
  66.7 2.2 %collective-permute-done.21.refs_1_ = bf16[4,64,256]{2,1,0:T(8,128)(2,1)S(1)} collective-permute-done((bf16[4,64,256]{2,1,0:T(8,128)(2,1)S(1)}, bf16[4,64,256]{2,1,0:T(8,128)(2,1)S(1)}, u32[]{:S(2)}, u32[]{:S(2)}) %collective-permute-start.21) | collective-permute-done | bytes 131104 | tf_op jit(solution)/shard_map/ppermute | solution.py:169
  68.9 1.8 %shard_map.108.field.right = bf16[4,64,256]{2,1,0:T(8,128)(2,1)S(1)} custom-call(s32[4]{0:T(128)S(1)} %pad_add_fusion.which, bf16[8,4,256,128]{3,2,1,0:T(8,128)(2,1)S(1)} %bitcast.24, bf16[4,256,128]{2,1,0:T(8,128)(2,1)S(1)} %bitcast.32, f32[4,64,256]{2,1,0:T(8,128)S(1)} %shard_map.107.total, bf16[4,64,256]{2,1,0:T(8,128)(2,1)S(1)} %collective-permute-done.20.refs_0_, ...), custom_call_target="tpu_custom_call" | custom-call | flops 335544320 | bytes 2097152 | tf_op jit(solution)/shard_map/pallas_call | solution.py:138
  72.9 3.4 %collective-permute-done.25 = f32[2,32,32]{2,1,0:T(8,128)S(1)} collective-permute-done((f32[2,32,32]{2,1,0:T(8,128)S(1)}, f32[2,32,32]{2,1,0:T(8,128)S(1)}, u32[]{:S(2)}, u32[]{:S(2)}) %collective-permute-start.25) | collective-permute-done | bytes 8224 | tf_op jit(solution)/shard_map/ppermute | solution.py:182
  76.6 3.6 %collective-permute-done.26 = f32[2,32,32]{2,1,0:T(8,128)S(1)} collective-permute-done((f32[2,32,32]{2,1,0:T(8,128)S(1)}, f32[2,32,32]{2,1,0:T(8,128)S(1)}, u32[]{:S(2)}, u32[]{:S(2)}) %collective-permute-start.26) | collective-permute-done | bytes 8224 | tf_op jit(solution)/shard_map/ppermute | solution.py:182
  81.3 2.9 %collective-permute-done.27 = f32[2,32,32]{2,1,0:T(8,128)S(1)} collective-permute-done((f32[2,32,32]{2,1,0:T(8,128)S(1)}, f32[2,32,32]{2,1,0:T(8,128)S(1)}, u32[]{:S(2)}, u32[]{:S(2)}) %collective-permute-start.27) | collective-permute-done | bytes 8224 | tf_op jit(solution)/shard_map/ppermute | solution.py:182
  (77 shorter events, 30.8 us)
Async XLA Ops:
  3.9 10.4 %collective-permute-start = (bf16[4,64,256]{2,1,0:T(8,128)(2,1)S(1)}, bf16[4,64,256]{2,1,0:T(8,128)(2,1)S(1)}, u32[]{:S(2)}, u32[]{:S(2)}) collective-permute-start(bf16[4,64,256]{2,1,0:T(8,128)(2,1)S(1)} %get-tuple-element.8.field), channel_id=1, source_target_pairs={{0,4},{4,0},{8,12},{12,8},{16,20},{20,16},{24,28},{28,24},{1,5},{5... | collective-permute-start | bytes 393224 | tf_op jit(solution)/shard_map/ppermute | solution.py:170
  6.9 7.7 %collective-permute-start.1 = (bf16[4,64,256]{2,1,0:T(8,128)(2,1)S(1)}, bf16[4,64,256]{2,1,0:T(8,128)(2,1)S(1)}, u32[]{:S(2)}, u32[]{:S(2)}) collective-permute-start(bf16[4,64,256]{2,1,0:T(8,128)(2,1)S(1)} %get-tuple-element.8.field), channel_id=1, source_target_pairs={{0,28},{4,8},{8,4},{12,16},{16,12},{20,24},{24,20},{28,0},{1,29},{... | collective-permute-start | bytes 393224 | tf_op jit(solution)/shard_map/ppermute | solution.py:169
  10.4 5.2 %collective-permute-start.3 = (bf16[4,64,256]{2,1,0:T(8,128)(2,1)S(1)}, bf16[4,64,256]{2,1,0:T(8,128)(2,1)S(1)}, u32[]{:S(2)}, u32[]{:S(2)}) collective-permute-start(bf16[4,64,256]{2,1,0:T(8,128)(2,1)S(1)} %get-tuple-element.8.field), channel_id=1, source_target_pairs={{0,3},{1,2},{2,1},{3,0},{4,7},{5,6},{6,5},{7,4},{8,11},{9,10},{10,... | collective-permute-start | bytes 393224 | tf_op jit(solution)/shard_map/ppermute | solution.py:167
  17.4 6.6 %collective-permute-start.4 = (bf16[4,64,256]{2,1,0:T(8,128)(2,1)S(1)}, bf16[4,64,256]{2,1,0:T(8,128)(2,1)S(1)}, u32[]{:S(2)}, u32[]{:S(2)}) collective-permute-start(bf16[4,64,256]{2,1,0:T(8,128)(2,1)S(1)} %shard_map.96.field), channel_id=1, source_target_pairs={{0,4},{4,0},{8,12},{12,8},{16,20},{20,16},{24,28},{28,24},{1,5},{5... | collective-permute-start | bytes 393224 | tf_op jit(solution)/shard_map/ppermute | solution.py:170
  17.5 8.7 %collective-permute-start.5 = (bf16[4,64,256]{2,1,0:T(8,128)(2,1)S(1)}, bf16[4,64,256]{2,1,0:T(8,128)(2,1)S(1)}, u32[]{:S(2)}, u32[]{:S(2)}) collective-permute-start(bf16[4,64,256]{2,1,0:T(8,128)(2,1)S(1)} %shard_map.96.field), channel_id=1, source_target_pairs={{0,28},{4,8},{8,4},{12,16},{16,12},{20,24},{24,20},{28,0},{1,29},{... | collective-permute-start | bytes 393224 | tf_op jit(solution)/shard_map/ppermute | solution.py:169
  20.4 5.8 %collective-permute-start.6 = (bf16[4,64,256]{2,1,0:T(8,128)(2,1)S(1)}, bf16[4,64,256]{2,1,0:T(8,128)(2,1)S(1)}, u32[]{:S(2)}, u32[]{:S(2)}) collective-permute-start(bf16[4,64,256]{2,1,0:T(8,128)(2,1)S(1)} %shard_map.96.field), channel_id=1, source_target_pairs={{0,1},{1,0},{2,3},{3,2},{4,5},{5,4},{6,7},{7,6},{8,9},{9,8},{10,11... | collective-permute-start | bytes 393224 | tf_op jit(solution)/shard_map/ppermute | solution.py:168
  20.4 5.8 %collective-permute-start.7 = (bf16[4,64,256]{2,1,0:T(8,128)(2,1)S(1)}, bf16[4,64,256]{2,1,0:T(8,128)(2,1)S(1)}, u32[]{:S(2)}, u32[]{:S(2)}) collective-permute-start(bf16[4,64,256]{2,1,0:T(8,128)(2,1)S(1)} %shard_map.96.field), channel_id=1, source_target_pairs={{0,3},{1,2},{2,1},{3,0},{4,7},{5,6},{6,5},{7,4},{8,11},{9,10},{10,... | collective-permute-start | bytes 393224 | tf_op jit(solution)/shard_map/ppermute | solution.py:167
  28.0 4.4 %collective-permute-start.10 = (bf16[4,64,256]{2,1,0:T(8,128)(2,1)S(1)}, bf16[4,64,256]{2,1,0:T(8,128)(2,1)S(1)}, u32[]{:S(2)}, u32[]{:S(2)}) collective-permute-start(bf16[4,64,256]{2,1,0:T(8,128)(2,1)S(1)} %shard_map.98.field), channel_id=1, source_target_pairs={{0,1},{1,0},{2,3},{3,2},{4,5},{5,4},{6,7},{7,6},{8,9},{9,8},{10,11... | collective-permute-start | bytes 393224 | tf_op jit(solution)/shard_map/ppermute | solution.py:168
  28.1 5.2 %collective-permute-start.11 = (bf16[4,64,256]{2,1,0:T(8,128)(2,1)S(1)}, bf16[4,64,256]{2,1,0:T(8,128)(2,1)S(1)}, u32[]{:S(2)}, u32[]{:S(2)}) collective-permute-start(bf16[4,64,256]{2,1,0:T(8,128)(2,1)S(1)} %shard_map.98.field), channel_id=1, source_target_pairs={{0,3},{1,2},{2,1},{3,0},{4,7},{5,6},{6,5},{7,4},{8,11},{9,10},{10,... | collective-permute-start | bytes 393224 | tf_op jit(solution)/shard_map/ppermute | solution.py:167
  29.7 6.1 %collective-permute-start.8 = (bf16[4,64,256]{2,1,0:T(8,128)(2,1)S(1)}, bf16[4,64,256]{2,1,0:T(8,128)(2,1)S(1)}, u32[]{:S(2)}, u32[]{:S(2)}) collective-permute-start(bf16[4,64,256]{2,1,0:T(8,128)(2,1)S(1)} %shard_map.98.field), channel_id=1, source_target_pairs={{0,4},{4,0},{8,12},{12,8},{16,20},{20,16},{24,28},{28,24},{1,5},{5... | collective-permute-start | bytes 393224 | tf_op jit(solution)/shard_map/ppermute | solution.py:170
  30.0 8.0 %collective-permute-start.9 = (bf16[4,64,256]{2,1,0:T(8,128)(2,1)S(1)}, bf16[4,64,256]{2,1,0:T(8,128)(2,1)S(1)}, u32[]{:S(2)}, u32[]{:S(2)}) collective-permute-start(bf16[4,64,256]{2,1,0:T(8,128)(2,1)S(1)} %shard_map.98.field), channel_id=1, source_target_pairs={{0,28},{4,8},{8,4},{12,16},{16,12},{20,24},{24,20},{28,0},{1,29},{... | collective-permute-start | bytes 393224 | tf_op jit(solution)/shard_map/ppermute | solution.py:169
  40.4 6.4 %collective-permute-start.12 = (bf16[4,64,256]{2,1,0:T(8,128)(2,1)S(1)}, bf16[4,64,256]{2,1,0:T(8,128)(2,1)S(1)}, u32[]{:S(2)}, u32[]{:S(2)}) collective-permute-start(bf16[4,64,256]{2,1,0:T(8,128)(2,1)S(1)} %get-tuple-element.10.field), channel_id=1, source_target_pairs={{0,4},{4,0},{8,12},{12,8},{16,20},{20,16},{24,28},{28,24},{1,5},{5... | collective-permute-start | bytes 393224 | tf_op jit(solution)/shard_map/ppermute | solution.py:170
  40.8 7.7 %collective-permute-start.13 = (bf16[4,64,256]{2,1,0:T(8,128)(2,1)S(1)}, bf16[4,64,256]{2,1,0:T(8,128)(2,1)S(1)}, u32[]{:S(2)}, u32[]{:S(2)}) collective-permute-start(bf16[4,64,256]{2,1,0:T(8,128)(2,1)S(1)} %get-tuple-element.10.field), channel_id=1, source_target_pairs={{0,28},{4,8},{8,4},{12,16},{16,12},{20,24},{24,20},{28,0},{1,29},{... | collective-permute-start | bytes 393224 | tf_op jit(solution)/shard_map/ppermute | solution.py:169
  42.7 5.7 %collective-permute-start.14 = (bf16[4,64,256]{2,1,0:T(8,128)(2,1)S(1)}, bf16[4,64,256]{2,1,0:T(8,128)(2,1)S(1)}, u32[]{:S(2)}, u32[]{:S(2)}) collective-permute-start(bf16[4,64,256]{2,1,0:T(8,128)(2,1)S(1)} %get-tuple-element.10.field), channel_id=1, source_target_pairs={{0,1},{1,0},{2,3},{3,2},{4,5},{5,4},{6,7},{7,6},{8,9},{9,8},{10,11... | collective-permute-start | bytes 393224 | tf_op jit(solution)/shard_map/ppermute | solution.py:168
  42.7 5.7 %collective-permute-start.15 = (bf16[4,64,256]{2,1,0:T(8,128)(2,1)S(1)}, bf16[4,64,256]{2,1,0:T(8,128)(2,1)S(1)}, u32[]{:S(2)}, u32[]{:S(2)}) collective-permute-start(bf16[4,64,256]{2,1,0:T(8,128)(2,1)S(1)} %get-tuple-element.10.field), channel_id=1, source_target_pairs={{0,3},{1,2},{2,1},{3,0},{4,7},{5,6},{6,5},{7,4},{8,11},{9,10},{10,... | collective-permute-start | bytes 393224 | tf_op jit(solution)/shard_map/ppermute | solution.py:167
  50.3 6.2 %collective-permute-start.16 = (bf16[4,64,256]{2,1,0:T(8,128)(2,1)S(1)}, bf16[4,64,256]{2,1,0:T(8,128)(2,1)S(1)}, u32[]{:S(2)}, u32[]{:S(2)}) collective-permute-start(bf16[4,64,256]{2,1,0:T(8,128)(2,1)S(1)} %shard_map.104.field), channel_id=1, source_target_pairs={{0,4},{4,0},{8,12},{12,8},{16,20},{20,16},{24,28},{28,24},{1,5},{5... | collective-permute-start | bytes 393224 | tf_op jit(solution)/shard_map/ppermute | solution.py:170
  50.5 8.2 %collective-permute-start.17 = (bf16[4,64,256]{2,1,0:T(8,128)(2,1)S(1)}, bf16[4,64,256]{2,1,0:T(8,128)(2,1)S(1)}, u32[]{:S(2)}, u32[]{:S(2)}) collective-permute-start(bf16[4,64,256]{2,1,0:T(8,128)(2,1)S(1)} %shard_map.104.field), channel_id=1, source_target_pairs={{0,28},{4,8},{8,4},{12,16},{16,12},{20,24},{24,20},{28,0},{1,29},{... | collective-permute-start | bytes 393224 | tf_op jit(solution)/shard_map/ppermute | solution.py:169
  52.6 6.0 %collective-permute-start.18 = (bf16[4,64,256]{2,1,0:T(8,128)(2,1)S(1)}, bf16[4,64,256]{2,1,0:T(8,128)(2,1)S(1)}, u32[]{:S(2)}, u32[]{:S(2)}) collective-permute-start(bf16[4,64,256]{2,1,0:T(8,128)(2,1)S(1)} %shard_map.104.field), channel_id=1, source_target_pairs={{0,1},{1,0},{2,3},{3,2},{4,5},{5,4},{6,7},{7,6},{8,9},{9,8},{10,11... | collective-permute-start | bytes 393224 | tf_op jit(solution)/shard_map/ppermute | solution.py:168
  52.8 5.9 %collective-permute-start.19 = (bf16[4,64,256]{2,1,0:T(8,128)(2,1)S(1)}, bf16[4,64,256]{2,1,0:T(8,128)(2,1)S(1)}, u32[]{:S(2)}, u32[]{:S(2)}) collective-permute-start(bf16[4,64,256]{2,1,0:T(8,128)(2,1)S(1)} %shard_map.104.field), channel_id=1, source_target_pairs={{0,3},{1,2},{2,1},{3,0},{4,7},{5,6},{6,5},{7,4},{8,11},{9,10},{10,... | collective-permute-start | bytes 393224 | tf_op jit(solution)/shard_map/ppermute | solution.py:167
  60.5 6.2 %collective-permute-start.20 = (bf16[4,64,256]{2,1,0:T(8,128)(2,1)S(1)}, bf16[4,64,256]{2,1,0:T(8,128)(2,1)S(1)}, u32[]{:S(2)}, u32[]{:S(2)}) collective-permute-start(bf16[4,64,256]{2,1,0:T(8,128)(2,1)S(1)} %shard_map.106.field), channel_id=1, source_target_pairs={{0,4},{4,0},{8,12},{12,8},{16,20},{20,16},{24,28},{28,24},{1,5},{5... | collective-permute-start | bytes 393224 | tf_op jit(solution)/shard_map/ppermute | solution.py:170
  60.9 8.0 %collective-permute-start.21 = (bf16[4,64,256]{2,1,0:T(8,128)(2,1)S(1)}, bf16[4,64,256]{2,1,0:T(8,128)(2,1)S(1)}, u32[]{:S(2)}, u32[]{:S(2)}) collective-permute-start(bf16[4,64,256]{2,1,0:T(8,128)(2,1)S(1)} %shard_map.106.field), channel_id=1, source_target_pairs={{0,28},{4,8},{8,4},{12,16},{16,12},{20,24},{24,20},{28,0},{1,29},{... | collective-permute-start | bytes 393224 | tf_op jit(solution)/shard_map/ppermute | solution.py:169
  63.4 5.4 %collective-permute-start.22 = (bf16[4,64,256]{2,1,0:T(8,128)(2,1)S(1)}, bf16[4,64,256]{2,1,0:T(8,128)(2,1)S(1)}, u32[]{:S(2)}, u32[]{:S(2)}) collective-permute-start(bf16[4,64,256]{2,1,0:T(8,128)(2,1)S(1)} %shard_map.106.field), channel_id=1, source_target_pairs={{0,1},{1,0},{2,3},{3,2},{4,5},{5,4},{6,7},{7,6},{8,9},{9,8},{10,11... | collective-permute-start | bytes 393224 | tf_op jit(solution)/shard_map/ppermute | solution.py:168
  63.4 5.4 %collective-permute-start.23 = (bf16[4,64,256]{2,1,0:T(8,128)(2,1)S(1)}, bf16[4,64,256]{2,1,0:T(8,128)(2,1)S(1)}, u32[]{:S(2)}, u32[]{:S(2)}) collective-permute-start(bf16[4,64,256]{2,1,0:T(8,128)(2,1)S(1)} %shard_map.106.field), channel_id=1, source_target_pairs={{0,3},{1,2},{2,1},{3,0},{4,7},{5,6},{6,5},{7,4},{8,11},{9,10},{10,... | collective-permute-start | bytes 393224 | tf_op jit(solution)/shard_map/ppermute | solution.py:167
  84.2 4.8 %collective-permute-start.28 = (f32[2,32,32]{2,1,0:T(8,128)S(1)}, f32[2,32,32]{2,1,0:T(8,128)S(1)}, u32[]{:S(2)}, u32[]{:S(2)}) collective-permute-start(f32[2,32,32]{2,1,0:T(8,128)S(1)} %add.27), channel_id=1, source_target_pairs={{0,16},{4,20},{8,24},{12,28},{16,0},{20,4},{24,8},{28,12},{1,17},{... | collective-permute-start | bytes 24584 | tf_op jit(solution)/shard_map/ppermute | solution.py:182
  (14 other events, 67.3 us)

commit v2 on v1

v2 whole, which is shorter than its diff:
```python
import functools
import math

import jax
import jax.numpy as jnp
from jax import lax
from jax.experimental import pallas as pl
from jax.experimental.pallas import tpu as pltpu
from jax.sharding import PartitionSpec as P

SWEEPS = 4
F32 = jnp.float32
BF16 = jnp.bfloat16
VMEM = pl.BlockSpec(memory_space=pltpu.VMEM)
HBM = pl.BlockSpec(memory_space=pltpu.HBM)


def dot(a, b):
    return jnp.dot(a, b, preferred_element_type=F32)


def widen(field):
    half = field.shape[1] // 2
    re, im = field[:, :half], field[:, half:]
    return jnp.concatenate(
        [field, jnp.concatenate([-im, re], axis=1)], axis=0
    )


def pick(product, sites):
    rows = product.shape[0] // sites
    half = product.shape[1] // 2
    lane = lax.broadcasted_iota(jnp.int32, (rows, 2 * half), 1) % half
    out = product[:rows]
    for y in range(1, sites):
        out = jnp.where(lane >= y * (half // sites), product[y * rows : (y + 1) * rows], out)
    return out


def turn(field, shift):
    half = field.shape[1] // 2
    re, im = field[:, :half].astype(F32), field[:, half:].astype(F32)
    return jnp.concatenate(
        [pltpu.roll(re, shift % half, 1), pltpu.roll(im, shift % half, 1)], axis=1
    ).astype(field.dtype)


def toward(axes):
    odd = [lax.rem(lax.axis_index(name), 2) if paired else 0 for name, paired in axes]
    return 4 + odd[0], 5 - odd[0], 6 + odd[1], 7 - odd[1]


def hop_loads(axes, hops, local, remote, sems):
    loads = [pltpu.make_async_copy(hops.at[e], local.at[e], sems.at[e]) for e in range(4)]
    return loads + [
        pltpu.make_async_copy(hops.at[e], remote.at[n], sems.at[4 + n]) for n, e in enumerate(toward(axes))
    ]


def load_kernel(axes, hops, local, remote, sems):
    loads = hop_loads(axes, hops, local, remote, sems)
    for load in loads:
        load.start()
    for load in loads:
        load.wait()


def first_kernel(
    axes, order_hbm, rhs_hbm, diag_hbm, hops, source, out, diag, local, remote, order, rhs, sems, hop_sems
):
    copies = [
        pltpu.make_async_copy(order_hbm, order, sems.at[0]),
        pltpu.make_async_copy(rhs_hbm, rhs, sems.at[1]),
        pltpu.make_async_copy(diag_hbm, diag, sems.at[2]),
    ]
    loads = hop_loads(axes, hops, local, remote, hop_sems)
    for copy in copies + loads:
        copy.start()
    lx, ly = rhs.shape[0], rhs.shape[1]
    cols = order.shape[1]
    half = ly * cols
    row = lax.broadcasted_iota(jnp.int32, (2 * cols, 2 * half), 0)
    lane = lax.broadcasted_iota(jnp.int32, (2 * cols, 2 * half), 1)
    copies[0].wait()
    wanted = jnp.concatenate([order[...]] * (2 * ly), axis=1)
    wanted = wanted + jnp.where(lane >= half, cols, 0)
    site = (lane % half) // cols
    hot = row == wanted
    places = [jnp.where(hot & (site == y), 1.0, 0.0).astype(BF16) for y in range(ly)]
    copies[1].wait()
    fields = []
    for x in range(lx):
        field = dot(rhs[x, 0], places[0])
        for y in range(1, ly):
            field = field + dot(rhs[x, y], places[y])
        fields.append(field.astype(BF16))
        source[x] = fields[x]
    copies[2].wait()
    for x in range(lx):
        out[x] = pick(dot(diag[x], widen(fields[x])), ly).astype(BF16)
    for load in loads:
        load.wait()


def local_kernel(sites, hops, source, field, residue):
    lx = field.shape[0]
    cols = field.shape[2] // (2 * sites)
    for x in range(lx):
        here = field[x]
        right = jnp.concatenate(
            [
                widen(field[(x + 1) % lx]),
                widen(field[(x - 1) % lx]),
                widen(turn(here, -cols)),
                widen(turn(here, cols)),
            ],
            axis=0,
        )
        left = jnp.concatenate([hops[e, x] for e in range(4)], axis=1)
        residue[x] = (source[x].astype(F32) + pick(dot(left, right), sites)).astype(BF16)


def blend_kernel(sites, remote, diag, out):
    lx, rows, wide = diag.shape
    comps = rows // sites
    row = lax.broadcasted_iota(jnp.int32, (wide, wide), 0)
    lane = lax.broadcasted_iota(jnp.int32, (wide, wide), 1)
    move = jnp.where(row == lane - comps, 1.0, jnp.where(row == lane + comps, -1.0, 0.0)).astype(BF16)
    for e in range(0, 4, 2):
        for x in range(lx):
            first, second = remote[e, x], remote[e + 1, x]
            low_first, low_second = dot(first, move).astype(BF16), dot(second, move).astype(BF16)
            for y in range(sites):
                at = slice(y * comps, (y + 1) * comps)
                right = jnp.concatenate(
                    [
                        jnp.concatenate([first[at], second[at]], axis=1),
                        jnp.concatenate([low_first[at], low_second[at]], axis=1),
                    ],
                    axis=0,
                )
                both = dot(diag[x, at], right).astype(BF16)
                out[e, x, at] = both[:, :wide]
                out[e + 1, x, at] = both[:, wide:]


def settle_kernel(sites, diag, residue, total):
    for x in range(residue.shape[0]):
        total[x] = pick(dot(diag[x], widen(residue[x])), sites)


def after_kernel(_, token, out):
    out[...] = token[...]


def add_kernel(sites, places, blended, token, total, *refs):
    fields, out = refs[:-1], refs[-1]
    for x in range(out.shape[0]):
        right = jnp.concatenate([widen(f[x]) for f in fields], axis=0)
        left = jnp.concatenate([blended[n, x] for n in places], axis=1)
        out[x] = (total[x] + pick(dot(left, right), sites)).astype(out.dtype)


def insert_kernel(sites, current, diag, field, source, out):
    lx = out.shape[0]
    inserted = [pick(dot(current[x], widen(field[x])), sites).astype(BF16) for x in range(lx)]
    for x in range(lx):
        source[x] = inserted[x]
        out[x] = pick(dot(diag[x], widen(inserted[x])), sites).astype(BF16)


def leave_kernel(*refs):
    refs, token = refs[:-1], refs[-1]
    token[...] = jnp.zeros_like(token)
    count = len(refs) // 2
    lx, ly, comps, wide = refs[count].shape
    half = refs[0].shape[2] // 2
    cols = wide // 2
    row = lax.broadcasted_iota(jnp.int32, (2 * half, wide), 0)
    lane = lax.broadcasted_iota(jnp.int32, (2 * half, wide), 1)
    start = jnp.where(lane >= cols, half - cols, 0)
    for field, out in zip(refs[:count], refs[count:], strict=True):
        whole = field[...].reshape(lx * comps, 2 * half)
        for y in range(ly):
            place = jnp.where(row == lane + start + y * cols, 1.0, 0.0).astype(BF16)
            out[:, y] = dot(whole, place).astype(BF16).reshape(lx, comps, wide)


def gram_kernel(sites, left, right, out):
    lx, comps, width = left.shape
    half = width // 2
    cols = half // sites
    a = left[...].reshape(lx * comps, width)
    b = right[...].reshape(lx * comps, width)
    full = lax.dot_general(a, b, (((0,), (0,)), ((), ())), preferred_element_type=F32)
    real = full[:half, :half] + full[half:, half:]
    imag = full[:half, half:] - full[half:, :half]
    group = lax.broadcasted_iota(jnp.int32, (cols, half), 1) // cols
    sums = []
    for m in (real, imag):
        folded = m[:cols]
        for y in range(1, sites):
            folded = jnp.where(group == y, m[y * cols : (y + 1) * cols], folded)
        total = folded
        for y in range(1, sites):
            total = total + pltpu.roll(folded, y * cols, 1)
        sums.append(total)
    out[...] = jnp.where(group == 0, sums[0], jnp.where(group == 1, sums[1], 0.0))


def margin_kernel(factor, summed, _, out):
    cols = out.shape[1]
    scaled = summed[...] * factor
    out[0] = scaled[:, :cols]
    out[1] = pltpu.roll(scaled, scaled.shape[1] - cols, 1)[:, :cols]


def call(kernel, outs, cost, *args, far=(), scratch=()):
    flops, moved = cost
    args = [pltpu.with_memory_space_constraint(a, pltpu.HBM) if i in far else a for i, a in enumerate(args)]
    return pl.pallas_call(
        kernel,
        out_shape=outs,
        in_specs=[HBM if i in far else VMEM for i in range(len(args))],
        out_specs=jax.tree.map(lambda _: VMEM, outs),
        scratch_shapes=scratch,
        compiler_params=pltpu.CompilerParams(vmem_limit_bytes=24 * 2**20),
        cost_estimate=pl.CostEstimate(flops=flops, bytes_accessed=moved, transcendentals=0),
    )(*args)


def swaps(axis):
    count = lax.axis_size(axis)
    if count % 2:
        return (
            [(i, (i - 1) % count) for i in range(count)],
            [(i, (i + 1) % count) for i in range(count)],
        )
    near = [(i, i ^ 1) for i in range(count)]
    far = [(i, (i + 1 if i % 2 else i - 1) % count) for i in range(count)]
    return near, far


def total_sum(value):
    spaces, times = lax.axis_size("space"), lax.axis_size("tm")
    if (spaces & (spaces - 1)) or (times & (times - 1)):
        return lax.psum(value, ("space", "tm"))

    def swap(mask):
        target = [(s ^ mask[0]) * times + (t ^ mask[1]) for s in range(spaces) for t in range(times)]
        return lax.ppermute(value, ("space", "tm"), list(enumerate(target)))

    cross = 1 if times > 1 else 0
    steps = [(0, 1 << k) for k in range(1, times.bit_length() - 1)]
    steps[1:1] = [(1 << k, 0) for k in range(spaces.bit_length() - 1)]
    if cross:
        value = value + swap((0, 1))
    for k in range(0, len(steps), 2):
        pair = steps[k : k + 2]
        if len(pair) == 2:
            pair.append((pair[0][0] ^ pair[1][0], pair[0][1] ^ pair[1][1]))
        value = sum([swap((s, t ^ cross)) for s, t in pair], value)
    return value


def body(right_side, batch_order, light_diag, light_hops, charm_diag, charm_hops, current_blocks):
    lt, lz, lx, ly, comps, wide = right_side.shape
    assert lt == 1 and lz == 1
    cols = wide // 2
    rows = ly * comps
    rhs = right_side.reshape(lx, ly, comps, wide)
    order = batch_order.reshape(1, cols)
    light_p, charm_p, current = (a.reshape(lx, rows, 2 * comps) for a in (light_diag, charm_diag, current_blocks))
    light_h, charm_h = (a.reshape(8, lx, rows, 2 * comps) for a in (light_hops, charm_hops))
    shape = (lx, comps, 2 * ly * cols)
    field_t = jax.ShapeDtypeStruct(shape, BF16)
    total_t = jax.ShapeDtypeStruct(shape, F32)
    axes = tuple((name, lax.axis_size(name) % 2 == 0) for name in ("space", "tm"))
    unit = 2 * lx * rows * 2 * comps * 2 * ly * cols

    blended_t = jax.ShapeDtypeStruct((4, lx, rows, 2 * comps), BF16)
    near_s, far_s = swaps("space")
    near_t, far_t = swaps("tm")

    token_t = jax.ShapeDtypeStruct((8, 128), F32)

    def sweeps(local, remote, diag, source, field):
        blended = call(functools.partial(blend_kernel, ly), blended_t, (4 * unit, 2**22), remote, diag)
        token = jnp.zeros(token_t.shape, F32)
        for _ in range(SWEEPS - 1):
            y = lax.ppermute(field, "tm", far_t)
            c = lax.ppermute(field, "tm", near_t)
            w = lax.ppermute(field, "space", far_s)
            e = lax.ppermute(field, "space", near_s)
            residue = call(functools.partial(local_kernel, ly), field_t, (4 * unit, 2**21), local, source, field)
            total = call(functools.partial(settle_kernel, ly), total_t, (unit, 2**20), diag, residue)
            for arrived in (e, w):
                token = call(after_kernel, token_t, (0, 2**24), arrived, token)
            field = call(
                functools.partial(add_kernel, ly, (0, 1, 3, 2)), field_t, (4 * unit, 2**20), blended, token, total, e, w, y, c
            )
        return field

    results = (field_t, field_t, jax.ShapeDtypeStruct(light_p.shape, BF16), blended_t, blended_t)
    source, field, light_p, local, remote = call(
        functools.partial(first_kernel, axes), results, (2 * unit, 2**20), order, rhs, light_p, light_h,
        far=(0, 1, 2, 3),
        scratch=(
            pltpu.VMEM(order.shape, jnp.int32),
            pltpu.VMEM(rhs.shape, BF16),
            pltpu.SemaphoreType.DMA((3,)),
            pltpu.SemaphoreType.DMA((8,)),
        ),
    )
    light = sweeps(local, remote, light_p, source, field)
    local, remote = call(
        functools.partial(load_kernel, axes), (blended_t, blended_t), (0, 2**22), charm_h, far=(0,),
        scratch=(pltpu.SemaphoreType.DMA((8,)),),
    )
    inserted, field = call(
        functools.partial(insert_kernel, ly), (field_t, field_t), (2 * unit, 2**20), current, charm_p, light
    )
    seq = sweeps(local, remote, charm_p, inserted, field)
    part = call(
        functools.partial(gram_kernel, ly), jax.ShapeDtypeStruct((cols, ly * cols), F32), (unit, 2**20), light, seq
    )
    out_t = jax.ShapeDtypeStruct((lx, ly, comps, wide), BF16)
    light_out, seq_out, token = call(leave_kernel, (out_t, out_t, token_t), (unit, 2**22), light, seq)
    summed = total_sum(part)
    site_count = lx * ly * lax.axis_size("space") * lax.axis_size("tm")
    factor = 1.0 / math.sqrt(site_count * comps)
    margin = call(
        functools.partial(margin_kernel, factor), jax.ShapeDtypeStruct((2, cols, cols), F32), (2**14, 2**14), summed, token
    )
    return light_out.reshape(right_side.shape), seq_out.reshape(right_side.shape), margin


def solution(mesh):
    site = P("tm", "space", None, None, None, None)
    hops = P(None, "tm", "space", None, None, None, None)
    return jax.shard_map(
        body,
        mesh=mesh,
        in_specs=(site, P(), site, hops, site, hops, site),
        out_specs=(site, site, P()),
        check_vma=False,
    )
```

time: 89.8 us -> 73.1 us (0.81)
  waiting for transfers between devices: 37.2 us -> 21.6 us
  starting transfers between devices: 29.2 us -> 33.7 us
  local copies, waits for them, and re-layouts: 4.28 us -> 0.02 us
    ppermute x29 -> x31, waiting for transfers between devices: 37.2 us -> 21.6 us  [the longest x6 9.04 us: sweeps(): w = lax.ppermute(field, 'space', far_s)]
    ppermute x29 -> x31, starting transfers between devices: 29.2 us -> 33.7 us  [the longest x6 14.9 us: sweeps(): w = lax.ppermute(field, 'space', far_s)]
    unnamed x18 -> x4, local copies, waits for them, and re-layouts: 4.17 us -> 0.01 us
    pallas_call x17 -> x38, Pallas kernels: 17.2 us -> 16.5 us  [call(): pl.pallas_call(kernel, out_shape=outs, in_specs=[HBM if i in far else VME...]
  transfers between devices with their start and end apart: 29 -> 31, of which waited for: 18 -> 15; matrix products, arithmetic and copies ran while one was open for 0% -> 0% of each run, Pallas kernels for 5% -> 14%
where the time goes in v2:
time: 73.1 us; the launch traced here: 72.9 us
  starting transfers between devices  33.7 us (46%)
  waiting for transfers between devices  21.6 us (30%)
  Pallas kernels  16.5 us (23%)
  between operations  0.96 us (1%)
    pallas_call x38, Pallas kernels, call(): pl.pallas_call(kernel, out_shape=outs, in_specs=[HBM if i in far else VME...  16.5 us
    ppermute x6, starting transfers between devices, sweeps(): w = lax.ppermute(field, 'space', far_s)  14.9 us
    ppermute x6, waiting for transfers between devices, sweeps(): w = lax.ppermute(field, 'space', far_s)  9.04 us
    ppermute x7, starting transfers between devices, swap(): return lax.ppermute(value, ('space', 'tm'), list(enumerate(target)))  6.93 us
    ppermute x6, starting transfers between devices, sweeps(): c = lax.ppermute(field, 'tm', near_t)  6.75 us
    ppermute x6, waiting for transfers between devices, sweeps(): e = lax.ppermute(field, 'space', near_s)  6.46 us
    ppermute x7, waiting for transfers between devices, swap(): return lax.ppermute(value, ('space', 'tm'), list(enumerate(target)))  4.47 us
    ppermute x6, starting transfers between devices, sweeps(): e = lax.ppermute(field, 'space', near_s)  4.45 us
  transfers between devices with their start and end apart: 31, of which 15 were waited for; matrix products, arithmetic and copies ran while one was open for 0% of the time, Pallas kernels for 14%

profile of v2, /device:TPU:0, one launch (start us, length us, event | category | flops | bytes accessed | tf_op | source)
XLA Modules:
  0.0 72.9 jit_solution(2045210325461941653)
XLA Ops:
  0.6 1.9 %shard_map.94 = (bf16[4,64,256]{2,1,0:T(8,128)(2,1)S(1)}, bf16[4,64,256]{2,1,0:T(8,128)(2,1)S(1)}, bf16[4,256,128]{2,1,0:T(8,128)(2,1)S(1)}, bf16[4,4,256,128]{3...) custom-call(s32[1,32]{1,0:T(1,128)} %bitcast.19, bf16[4,4,64,64]{3,2,1,0:T(8,128)(2,1)} %bitcast.17, ...), custom_call_target="tpu_custom_call" | custom-call | flops 134217728 | bytes 1048576 | tf_op jit(solution)/shard_map/pallas_call | solution.py:221
  2.6 3.0 %collective-permute-start.1 = (bf16[4,64,256]{2,1,0:T(8,128)(2,1)S(1)}, bf16[4,64,256]{2,1,0:T(8,128)(2,1)S(1)}, u32[]{:S(2)}, u32[]{:S(2)}) collective-permute-start(bf16[4,64,256]{2,1,0:T(8,128)(2,1)S(1)} %get-tuple-element.17.field), channel_id=1, source_target_pairs={{0,4},{4,0},{8,12},{12,8},{16,20},{20,16},{24,28},{28,24},{1,5},{5... | collective-permute-start | bytes 393224 | tf_op jit(solution)/shard_map/ppermute | solution.py:294
  5.6 3.6 %collective-permute-start = (bf16[4,64,256]{2,1,0:T(8,128)(2,1)S(1)}, bf16[4,64,256]{2,1,0:T(8,128)(2,1)S(1)}, u32[]{:S(2)}, u32[]{:S(2)}) collective-permute-start(bf16[4,64,256]{2,1,0:T(8,128)(2,1)S(1)} %get-tuple-element.17.field), channel_id=1, source_target_pairs={{0,28},{4,8},{8,4},{12,16},{16,12},{20,24},{24,20},{28,0},{1,29},{... | collective-permute-start | bytes 393224 | tf_op jit(solution)/shard_map/ppermute | solution.py:293
  11.6 1.6 %shard_map.95.blended = bf16[4,4,256,128]{3,2,1,0:T(8,128)(2,1)S(1)} custom-call(bf16[4,4,256,128]{3,2,1,0:T(8,128)(2,1)S(1)} %get-tuple-element.15.remote, bf16[4,256,128]{2,1,0:T(8,128)(2,1)S(1)} %get-tuple-element.16.diag), custom_call_target="tpu_custom_call" | custom-call | flops 268435456 | bytes 4194304 | tf_op jit(solution)/shard_map/pallas_call | solution.py:221
  13.3 1.6 %collective-permute-done.2.refs_2_ = bf16[4,64,256]{2,1,0:T(8,128)(2,1)S(1)} collective-permute-done((bf16[4,64,256]{2,1,0:T(8,128)(2,1)S(1)}, bf16[4,64,256]{2,1,0:T(8,128)(2,1)S(1)}, u32[]{:S(2)}, u32[]{:S(2)}) %collective-permute-start.2) | collective-permute-done | bytes 131104 | tf_op jit(solution)/shard_map/ppermute | solution.py:291
  15.4 2.3 %collective-permute-start.4 = (bf16[4,64,256]{2,1,0:T(8,128)(2,1)S(1)}, bf16[4,64,256]{2,1,0:T(8,128)(2,1)S(1)}, u32[]{:S(2)}, u32[]{:S(2)}) collective-permute-start(bf16[4,64,256]{2,1,0:T(8,128)(2,1)S(1)} %shard_map.100.field), channel_id=1, source_target_pairs={{0,28},{4,8},{8,4},{12,16},{16,12},{20,24},{24,20},{28,0},{1,29},{... | collective-permute-start | bytes 393224 | tf_op jit(solution)/shard_map/ppermute | solution.py:293
  17.8 1.6 %collective-permute-start.7 = (bf16[4,64,256]{2,1,0:T(8,128)(2,1)S(1)}, bf16[4,64,256]{2,1,0:T(8,128)(2,1)S(1)}, u32[]{:S(2)}, u32[]{:S(2)}) collective-permute-start(bf16[4,64,256]{2,1,0:T(8,128)(2,1)S(1)} %shard_map.100.field), channel_id=1, source_target_pairs={{0,1},{1,0},{2,3},{3,2},{4,5},{5,4},{6,7},{7,6},{8,9},{9,8},{10,11... | collective-permute-start | bytes 393224 | tf_op jit(solution)/shard_map/ppermute | solution.py:292
  20.2 1.4 %collective-permute-done.5._.refs_0_ = bf16[4,64,256]{2,1,0:T(8,128)(2,1)S(1)} collective-permute-done((bf16[4,64,256]{2,1,0:T(8,128)(2,1)S(1)}, bf16[4,64,256]{2,1,0:T(8,128)(2,1)S(1)}, u32[]{:S(2)}, u32[]{:S(2)}) %collective-permute-start.5) | collective-permute-done | bytes 131104 | tf_op jit(solution)/shard_map/ppermute | solution.py:294
  21.6 2.2 %collective-permute-done.4._.refs_1_ = bf16[4,64,256]{2,1,0:T(8,128)(2,1)S(1)} collective-permute-done((bf16[4,64,256]{2,1,0:T(8,128)(2,1)S(1)}, bf16[4,64,256]{2,1,0:T(8,128)(2,1)S(1)}, u32[]{:S(2)}, u32[]{:S(2)}) %collective-permute-start.4) | collective-permute-done | bytes 131104 | tf_op jit(solution)/shard_map/ppermute | solution.py:293
  24.6 2.0 %collective-permute-start.8 = (bf16[4,64,256]{2,1,0:T(8,128)(2,1)S(1)}, bf16[4,64,256]{2,1,0:T(8,128)(2,1)S(1)}, u32[]{:S(2)}, u32[]{:S(2)}) collective-permute-start(bf16[4,64,256]{2,1,0:T(8,128)(2,1)S(1)} %shard_map.105.field), channel_id=1, source_target_pairs={{0,28},{4,8},{8,4},{12,16},{16,12},{20,24},{24,20},{28,0},{1,29},{... | collective-permute-start | bytes 393224 | tf_op jit(solution)/shard_map/ppermute | solution.py:293
  28.5 1.8 %collective-permute-done.9._.refs_0_ = bf16[4,64,256]{2,1,0:T(8,128)(2,1)S(1)} collective-permute-done((bf16[4,64,256]{2,1,0:T(8,128)(2,1)S(1)}, bf16[4,64,256]{2,1,0:T(8,128)(2,1)S(1)}, u32[]{:S(2)}, u32[]{:S(2)}) %collective-permute-start.9) | collective-permute-done | bytes 131104 | tf_op jit(solution)/shard_map/ppermute | solution.py:294
  30.3 2.2 %collective-permute-done.8._.refs_1_ = bf16[4,64,256]{2,1,0:T(8,128)(2,1)S(1)} collective-permute-done((bf16[4,64,256]{2,1,0:T(8,128)(2,1)S(1)}, bf16[4,64,256]{2,1,0:T(8,128)(2,1)S(1)}, u32[]{:S(2)}, u32[]{:S(2)}) %collective-permute-start.8) | collective-permute-done | bytes 131104 | tf_op jit(solution)/shard_map/ppermute | solution.py:293
  33.8 2.4 %collective-permute-start.12 = (bf16[4,64,256]{2,1,0:T(8,128)(2,1)S(1)}, bf16[4,64,256]{2,1,0:T(8,128)(2,1)S(1)}, u32[]{:S(2)}, u32[]{:S(2)}) collective-permute-start(bf16[4,64,256]{2,1,0:T(8,128)(2,1)S(1)} %get-tuple-element.21.field), channel_id=1, source_target_pairs={{0,28},{4,8},{8,4},{12,16},{16,12},{20,24},{24,20},{28,0},{1,29},{... | collective-permute-start | bytes 393224 | tf_op jit(solution)/shard_map/ppermute | solution.py:293
  36.9 1.6 %shard_map.111 = (bf16[4,4,256,128]{3,2,1,0:T(8,128)(2,1)S(1)}, bf16[4,4,256,128]{3,2,1,0:T(8,128)(2,1)S(1)}) custom-call(bf16[8,4,256,128]{3,2,1,0:T(8,128)(2,1)} %bitcast.16), custom_call_target="tpu_custom_call" | custom-call | bytes 4194304 | tf_op jit(solution)/shard_map/pallas_call | solution.py:221
  38.5 1.6 %shard_map.112.blended = bf16[4,4,256,128]{3,2,1,0:T(8,128)(2,1)S(1)} custom-call(bf16[4,4,256,128]{3,2,1,0:T(8,128)(2,1)S(1)} %get-tuple-element.20.remote, bf16[4,256,128]{2,1,0:T(8,128)(2,1)S(1)} %bitcast.10), custom_call_target="tpu_custom_call" | custom-call | flops 268435456 | bytes 4194304 | tf_op jit(solution)/shard_map/pallas_call | solution.py:221
  42.6 2.1 %collective-permute-start.16 = (bf16[4,64,256]{2,1,0:T(8,128)(2,1)S(1)}, bf16[4,64,256]{2,1,0:T(8,128)(2,1)S(1)}, u32[]{:S(2)}, u32[]{:S(2)}) collective-permute-start(bf16[4,64,256]{2,1,0:T(8,128)(2,1)S(1)} %shard_map.118.field), channel_id=1, source_target_pairs={{0,28},{4,8},{8,4},{12,16},{16,12},{20,24},{24,20},{28,0},{1,29},{... | collective-permute-start | bytes 393224 | tf_op jit(solution)/shard_map/ppermute | solution.py:293
  46.8 1.9 %collective-permute-done.17._.refs_0_ = bf16[4,64,256]{2,1,0:T(8,128)(2,1)S(1)} collective-permute-done((bf16[4,64,256]{2,1,0:T(8,128)(2,1)S(1)}, bf16[4,64,256]{2,1,0:T(8,128)(2,1)S(1)}, u32[]{:S(2)}, u32[]{:S(2)}) %collective-permute-start.17) | collective-permute-done | bytes 131104 | tf_op jit(solution)/shard_map/ppermute | solution.py:294
  48.7 1.6 %collective-permute-done.16._.refs_1_ = bf16[4,64,256]{2,1,0:T(8,128)(2,1)S(1)} collective-permute-done((bf16[4,64,256]{2,1,0:T(8,128)(2,1)S(1)}, bf16[4,64,256]{2,1,0:T(8,128)(2,1)S(1)}, u32[]{:S(2)}, u32[]{:S(2)}) %collective-permute-start.16) | collective-permute-done | bytes 131104 | tf_op jit(solution)/shard_map/ppermute | solution.py:293
  51.0 2.5 %collective-permute-start.20 = (bf16[4,64,256]{2,1,0:T(8,128)(2,1)S(1)}, bf16[4,64,256]{2,1,0:T(8,128)(2,1)S(1)}, u32[]{:S(2)}, u32[]{:S(2)}) collective-permute-start(bf16[4,64,256]{2,1,0:T(8,128)(2,1)S(1)} %shard_map.123.field), channel_id=1, source_target_pairs={{0,28},{4,8},{8,4},{12,16},{16,12},{20,24},{24,20},{28,0},{1,29},{... | collective-permute-start | bytes 393224 | tf_op jit(solution)/shard_map/ppermute | solution.py:293
  55.4 1.3 %collective-permute-done.21._.refs_0_ = bf16[4,64,256]{2,1,0:T(8,128)(2,1)S(1)} collective-permute-done((bf16[4,64,256]{2,1,0:T(8,128)(2,1)S(1)}, bf16[4,64,256]{2,1,0:T(8,128)(2,1)S(1)}, u32[]{:S(2)}, u32[]{:S(2)}) %collective-permute-start.21) | collective-permute-done | bytes 131104 | tf_op jit(solution)/shard_map/ppermute | solution.py:294
  56.7 2.2 %collective-permute-done.20._.refs_1_ = bf16[4,64,256]{2,1,0:T(8,128)(2,1)S(1)} collective-permute-done((bf16[4,64,256]{2,1,0:T(8,128)(2,1)S(1)}, bf16[4,64,256]{2,1,0:T(8,128)(2,1)S(1)}, u32[]{:S(2)}, u32[]{:S(2)}) %collective-permute-start.20) | collective-permute-done | bytes 131104 | tf_op jit(solution)/shard_map/ppermute | solution.py:293
  61.4 1.8 %collective-permute-start.26 = (f32[32,128]{1,0:T(8,128)S(1)}, f32[32,128]{1,0:T(8,128)S(1)}, u32[]{:S(2)}, u32[]{:S(2)}) collective-permute-start(f32[32,128]{1,0:T(8,128)S(1)} %add.21), channel_id=1, source_target_pairs={{0,5},{1,4},{2,7},{3,6},{4,1},{5,0},{6,3},{7,2},{8,13},{9,12},{10,... | collective-permute-start | bytes 49160 | tf_op jit(solution)/shard_map/ppermute | solution.py:251
  64.9 1.4 %collective-permute-done.25 = f32[32,128]{1,0:T(8,128)S(1)} collective-permute-done((f32[32,128]{1,0:T(8,128)S(1)}, f32[32,128]{1,0:T(8,128)S(1)}, u32[]{:S(2)}, u32[]{:S(2)}) %collective-permute-start.25) | collective-permute-done | bytes 16416 | tf_op jit(solution)/shard_map/ppermute | solution.py:251
  68.4 1.9 %collective-permute-start.28 = (f32[32,128]{1,0:T(8,128)S(1)}, f32[32,128]{1,0:T(8,128)S(1)}, u32[]{:S(2)}, u32[]{:S(2)}) collective-permute-start(f32[32,128]{1,0:T(8,128)S(1)} %add_add_fusion.1), channel_id=1, source_target_pairs={{0,9},{1,8},{2,11},{3,10},{4,13},{5,12},{6,15},{7,14},{8,1},{9,0},... | collective-permute-start | bytes 49160 | tf_op jit(solution)/shard_map/ppermute | solution.py:251
  (84 shorter events, 24.4 us)
Async XLA Ops:
  2.6 10.6 %collective-permute-start.1 = (bf16[4,64,256]{2,1,0:T(8,128)(2,1)S(1)}, bf16[4,64,256]{2,1,0:T(8,128)(2,1)S(1)}, u32[]{:S(2)}, u32[]{:S(2)}) collective-permute-start(bf16[4,64,256]{2,1,0:T(8,128)(2,1)S(1)} %get-tuple-element.17.field), channel_id=1, source_target_pairs={{0,4},{4,0},{8,12},{12,8},{16,20},{20,16},{24,28},{28,24},{1,5},{5... | collective-permute-start | bytes 393224 | tf_op jit(solution)/shard_map/ppermute | solution.py:294
  5.6 7.7 %collective-permute-start = (bf16[4,64,256]{2,1,0:T(8,128)(2,1)S(1)}, bf16[4,64,256]{2,1,0:T(8,128)(2,1)S(1)}, u32[]{:S(2)}, u32[]{:S(2)}) collective-permute-start(bf16[4,64,256]{2,1,0:T(8,128)(2,1)S(1)} %get-tuple-element.17.field), channel_id=1, source_target_pairs={{0,28},{4,8},{8,4},{12,16},{16,12},{20,24},{24,20},{28,0},{1,29},{... | collective-permute-start | bytes 393224 | tf_op jit(solution)/shard_map/ppermute | solution.py:293
  9.2 5.7 %collective-permute-start.2 = (bf16[4,64,256]{2,1,0:T(8,128)(2,1)S(1)}, bf16[4,64,256]{2,1,0:T(8,128)(2,1)S(1)}, u32[]{:S(2)}, u32[]{:S(2)}) collective-permute-start(bf16[4,64,256]{2,1,0:T(8,128)(2,1)S(1)} %get-tuple-element.17.field), channel_id=1, source_target_pairs={{0,3},{1,2},{2,1},{3,0},{4,7},{5,6},{6,5},{7,4},{8,11},{9,10},{10,... | collective-permute-start | bytes 393224 | tf_op jit(solution)/shard_map/ppermute | solution.py:291
  9.6 5.3 %collective-permute-start.3 = (bf16[4,64,256]{2,1,0:T(8,128)(2,1)S(1)}, bf16[4,64,256]{2,1,0:T(8,128)(2,1)S(1)}, u32[]{:S(2)}, u32[]{:S(2)}) collective-permute-start(bf16[4,64,256]{2,1,0:T(8,128)(2,1)S(1)} %get-tuple-element.17.field), channel_id=1, source_target_pairs={{0,1},{1,0},{2,3},{3,2},{4,5},{5,4},{6,7},{7,6},{8,9},{9,8},{10,11... | collective-permute-start | bytes 393224 | tf_op jit(solution)/shard_map/ppermute | solution.py:292
  15.3 6.2 %collective-permute-start.5 = (bf16[4,64,256]{2,1,0:T(8,128)(2,1)S(1)}, bf16[4,64,256]{2,1,0:T(8,128)(2,1)S(1)}, u32[]{:S(2)}, u32[]{:S(2)}) collective-permute-start(bf16[4,64,256]{2,1,0:T(8,128)(2,1)S(1)} %shard_map.100.field), channel_id=1, source_target_pairs={{0,4},{4,0},{8,12},{12,8},{16,20},{20,16},{24,28},{28,24},{1,5},{5... | collective-permute-start | bytes 393224 | tf_op jit(solution)/shard_map/ppermute | solution.py:294
  15.4 8.3 %collective-permute-start.4 = (bf16[4,64,256]{2,1,0:T(8,128)(2,1)S(1)}, bf16[4,64,256]{2,1,0:T(8,128)(2,1)S(1)}, u32[]{:S(2)}, u32[]{:S(2)}) collective-permute-start(bf16[4,64,256]{2,1,0:T(8,128)(2,1)S(1)} %shard_map.100.field), channel_id=1, source_target_pairs={{0,28},{4,8},{8,4},{12,16},{16,12},{20,24},{24,20},{28,0},{1,29},{... | collective-permute-start | bytes 393224 | tf_op jit(solution)/shard_map/ppermute | solution.py:293
  17.8 6.0 %collective-permute-start.6 = (bf16[4,64,256]{2,1,0:T(8,128)(2,1)S(1)}, bf16[4,64,256]{2,1,0:T(8,128)(2,1)S(1)}, u32[]{:S(2)}, u32[]{:S(2)}) collective-permute-start(bf16[4,64,256]{2,1,0:T(8,128)(2,1)S(1)} %shard_map.100.field), channel_id=1, source_target_pairs={{0,3},{1,2},{2,1},{3,0},{4,7},{5,6},{6,5},{7,4},{8,11},{9,10},{10,... | collective-permute-start | bytes 393224 | tf_op jit(solution)/shard_map/ppermute | solution.py:291
  17.8 6.0 %collective-permute-start.7 = (bf16[4,64,256]{2,1,0:T(8,128)(2,1)S(1)}, bf16[4,64,256]{2,1,0:T(8,128)(2,1)S(1)}, u32[]{:S(2)}, u32[]{:S(2)}) collective-permute-start(bf16[4,64,256]{2,1,0:T(8,128)(2,1)S(1)} %shard_map.100.field), channel_id=1, source_target_pairs={{0,1},{1,0},{2,3},{3,2},{4,5},{5,4},{6,7},{7,6},{8,9},{9,8},{10,11... | collective-permute-start | bytes 393224 | tf_op jit(solution)/shard_map/ppermute | solution.py:292
  24.2 6.0 %collective-permute-start.9 = (bf16[4,64,256]{2,1,0:T(8,128)(2,1)S(1)}, bf16[4,64,256]{2,1,0:T(8,128)(2,1)S(1)}, u32[]{:S(2)}, u32[]{:S(2)}) collective-permute-start(bf16[4,64,256]{2,1,0:T(8,128)(2,1)S(1)} %shard_map.105.field), channel_id=1, source_target_pairs={{0,4},{4,0},{8,12},{12,8},{16,20},{20,16},{24,28},{28,24},{1,5},{5... | collective-permute-start | bytes 393224 | tf_op jit(solution)/shard_map/ppermute | solution.py:294
  24.6 7.8 %collective-permute-start.8 = (bf16[4,64,256]{2,1,0:T(8,128)(2,1)S(1)}, bf16[4,64,256]{2,1,0:T(8,128)(2,1)S(1)}, u32[]{:S(2)}, u32[]{:S(2)}) collective-permute-start(bf16[4,64,256]{2,1,0:T(8,128)(2,1)S(1)} %shard_map.105.field), channel_id=1, source_target_pairs={{0,28},{4,8},{8,4},{12,16},{16,12},{20,24},{24,20},{28,0},{1,29},{... | collective-permute-start | bytes 393224 | tf_op jit(solution)/shard_map/ppermute | solution.py:293
  26.6 5.8 %collective-permute-start.10 = (bf16[4,64,256]{2,1,0:T(8,128)(2,1)S(1)}, bf16[4,64,256]{2,1,0:T(8,128)(2,1)S(1)}, u32[]{:S(2)}, u32[]{:S(2)}) collective-permute-start(bf16[4,64,256]{2,1,0:T(8,128)(2,1)S(1)} %shard_map.105.field), channel_id=1, source_target_pairs={{0,3},{1,2},{2,1},{3,0},{4,7},{5,6},{6,5},{7,4},{8,11},{9,10},{10,... | collective-permute-start | bytes 393224 | tf_op jit(solution)/shard_map/ppermute | solution.py:291
  26.6 5.8 %collective-permute-start.11 = (bf16[4,64,256]{2,1,0:T(8,128)(2,1)S(1)}, bf16[4,64,256]{2,1,0:T(8,128)(2,1)S(1)}, u32[]{:S(2)}, u32[]{:S(2)}) collective-permute-start(bf16[4,64,256]{2,1,0:T(8,128)(2,1)S(1)} %shard_map.105.field), channel_id=1, source_target_pairs={{0,1},{1,0},{2,3},{3,2},{4,5},{5,4},{6,7},{7,6},{8,9},{9,8},{10,11... | collective-permute-start | bytes 393224 | tf_op jit(solution)/shard_map/ppermute | solution.py:292
  33.4 7.4 %collective-permute-start.13 = (bf16[4,64,256]{2,1,0:T(8,128)(2,1)S(1)}, bf16[4,64,256]{2,1,0:T(8,128)(2,1)S(1)}, u32[]{:S(2)}, u32[]{:S(2)}) collective-permute-start(bf16[4,64,256]{2,1,0:T(8,128)(2,1)S(1)} %get-tuple-element.21.field), channel_id=1, source_target_pairs={{0,4},{4,0},{8,12},{12,8},{16,20},{20,16},{24,28},{28,24},{1,5},{5... | collective-permute-start | bytes 393224 | tf_op jit(solution)/shard_map/ppermute | solution.py:294
  33.8 8.0 %collective-permute-start.12 = (bf16[4,64,256]{2,1,0:T(8,128)(2,1)S(1)}, bf16[4,64,256]{2,1,0:T(8,128)(2,1)S(1)}, u32[]{:S(2)}, u32[]{:S(2)}) collective-permute-start(bf16[4,64,256]{2,1,0:T(8,128)(2,1)S(1)} %get-tuple-element.21.field), channel_id=1, source_target_pairs={{0,28},{4,8},{8,4},{12,16},{16,12},{20,24},{24,20},{28,0},{1,29},{... | collective-permute-start | bytes 393224 | tf_op jit(solution)/shard_map/ppermute | solution.py:293
  36.2 5.5 %collective-permute-start.14 = (bf16[4,64,256]{2,1,0:T(8,128)(2,1)S(1)}, bf16[4,64,256]{2,1,0:T(8,128)(2,1)S(1)}, u32[]{:S(2)}, u32[]{:S(2)}) collective-permute-start(bf16[4,64,256]{2,1,0:T(8,128)(2,1)S(1)} %get-tuple-element.21.field), channel_id=1, source_target_pairs={{0,3},{1,2},{2,1},{3,0},{4,7},{5,6},{6,5},{7,4},{8,11},{9,10},{10,... | collective-permute-start | bytes 393224 | tf_op jit(solution)/shard_map/ppermute | solution.py:291
  36.2 5.5 %collective-permute-start.15 = (bf16[4,64,256]{2,1,0:T(8,128)(2,1)S(1)}, bf16[4,64,256]{2,1,0:T(8,128)(2,1)S(1)}, u32[]{:S(2)}, u32[]{:S(2)}) collective-permute-start(bf16[4,64,256]{2,1,0:T(8,128)(2,1)S(1)} %get-tuple-element.21.field), channel_id=1, source_target_pairs={{0,1},{1,0},{2,3},{3,2},{4,5},{5,4},{6,7},{7,6},{8,9},{9,8},{10,11... | collective-permute-start | bytes 393224 | tf_op jit(solution)/shard_map/ppermute | solution.py:292
  42.2 6.4 %collective-permute-start.17 = (bf16[4,64,256]{2,1,0:T(8,128)(2,1)S(1)}, bf16[4,64,256]{2,1,0:T(8,128)(2,1)S(1)}, u32[]{:S(2)}, u32[]{:S(2)}) collective-permute-start(bf16[4,64,256]{2,1,0:T(8,128)(2,1)S(1)} %shard_map.118.field), channel_id=1, source_target_pairs={{0,4},{4,0},{8,12},{12,8},{16,20},{20,16},{24,28},{28,24},{1,5},{5... | collective-permute-start | bytes 393224 | tf_op jit(solution)/shard_map/ppermute | solution.py:294
  42.6 7.7 %collective-permute-start.16 = (bf16[4,64,256]{2,1,0:T(8,128)(2,1)S(1)}, bf16[4,64,256]{2,1,0:T(8,128)(2,1)S(1)}, u32[]{:S(2)}, u32[]{:S(2)}) collective-permute-start(bf16[4,64,256]{2,1,0:T(8,128)(2,1)S(1)} %shard_map.118.field), channel_id=1, source_target_pairs={{0,28},{4,8},{8,4},{12,16},{16,12},{20,24},{24,20},{28,0},{1,29},{... | collective-permute-start | bytes 393224 | tf_op jit(solution)/shard_map/ppermute | solution.py:293
  44.7 5.6 %collective-permute-start.18 = (bf16[4,64,256]{2,1,0:T(8,128)(2,1)S(1)}, bf16[4,64,256]{2,1,0:T(8,128)(2,1)S(1)}, u32[]{:S(2)}, u32[]{:S(2)}) collective-permute-start(bf16[4,64,256]{2,1,0:T(8,128)(2,1)S(1)} %shard_map.118.field), channel_id=1, source_target_pairs={{0,3},{1,2},{2,1},{3,0},{4,7},{5,6},{6,5},{7,4},{8,11},{9,10},{10,... | collective-permute-start | bytes 393224 | tf_op jit(solution)/shard_map/ppermute | solution.py:291
  44.8 5.4 %collective-permute-start.19 = (bf16[4,64,256]{2,1,0:T(8,128)(2,1)S(1)}, bf16[4,64,256]{2,1,0:T(8,128)(2,1)S(1)}, u32[]{:S(2)}, u32[]{:S(2)}) collective-permute-start(bf16[4,64,256]{2,1,0:T(8,128)(2,1)S(1)} %shard_map.118.field), channel_id=1, source_target_pairs={{0,1},{1,0},{2,3},{3,2},{4,5},{5,4},{6,7},{7,6},{8,9},{9,8},{10,11... | collective-permute-start | bytes 393224 | tf_op jit(solution)/shard_map/ppermute | solution.py:292
  50.7 5.9 %collective-permute-start.21 = (bf16[4,64,256]{2,1,0:T(8,128)(2,1)S(1)}, bf16[4,64,256]{2,1,0:T(8,128)(2,1)S(1)}, u32[]{:S(2)}, u32[]{:S(2)}) collective-permute-start(bf16[4,64,256]{2,1,0:T(8,128)(2,1)S(1)} %shard_map.123.field), channel_id=1, source_target_pairs={{0,4},{4,0},{8,12},{12,8},{16,20},{20,16},{24,28},{28,24},{1,5},{5... | collective-permute-start | bytes 393224 | tf_op jit(solution)/shard_map/ppermute | solution.py:294
  51.0 7.8 %collective-permute-start.20 = (bf16[4,64,256]{2,1,0:T(8,128)(2,1)S(1)}, bf16[4,64,256]{2,1,0:T(8,128)(2,1)S(1)}, u32[]{:S(2)}, u32[]{:S(2)}) collective-permute-start(bf16[4,64,256]{2,1,0:T(8,128)(2,1)S(1)} %shard_map.123.field), channel_id=1, source_target_pairs={{0,28},{4,8},{8,4},{12,16},{16,12},{20,24},{24,20},{28,0},{1,29},{... | collective-permute-start | bytes 393224 | tf_op jit(solution)/shard_map/ppermute | solution.py:293
  53.5 5.3 %collective-permute-start.22 = (bf16[4,64,256]{2,1,0:T(8,128)(2,1)S(1)}, bf16[4,64,256]{2,1,0:T(8,128)(2,1)S(1)}, u32[]{:S(2)}, u32[]{:S(2)}) collective-permute-start(bf16[4,64,256]{2,1,0:T(8,128)(2,1)S(1)} %shard_map.123.field), channel_id=1, source_target_pairs={{0,3},{1,2},{2,1},{3,0},{4,7},{5,6},{6,5},{7,4},{8,11},{9,10},{10,... | collective-permute-start | bytes 393224 | tf_op jit(solution)/shard_map/ppermute | solution.py:291
  53.6 5.2 %collective-permute-start.23 = (bf16[4,64,256]{2,1,0:T(8,128)(2,1)S(1)}, bf16[4,64,256]{2,1,0:T(8,128)(2,1)S(1)}, u32[]{:S(2)}, u32[]{:S(2)}) collective-permute-start(bf16[4,64,256]{2,1,0:T(8,128)(2,1)S(1)} %shard_map.123.field), channel_id=1, source_target_pairs={{0,1},{1,0},{2,3},{3,2},{4,5},{5,4},{6,7},{7,6},{8,9},{9,8},{10,11... | collective-permute-start | bytes 393224 | tf_op jit(solution)/shard_map/ppermute | solution.py:292
  (9 other events, 42.9 us)

commit v3 on v2

--- a/solution.py
+++ b/solution.py
@@ -65,16 +65,13 @@
         load.wait()
 
 
-def first_kernel(
-    axes, order_hbm, rhs_hbm, diag_hbm, hops, source, out, diag, local, remote, order, rhs, sems, hop_sems
-):
+def first_kernel(order_hbm, rhs_hbm, diag_hbm, source, out, diag, order, rhs, sems):
     copies = [
         pltpu.make_async_copy(order_hbm, order, sems.at[0]),
         pltpu.make_async_copy(rhs_hbm, rhs, sems.at[1]),
         pltpu.make_async_copy(diag_hbm, diag, sems.at[2]),
     ]
-    loads = hop_loads(axes, hops, local, remote, hop_sems)
-    for copy in copies + loads:
+    for copy in copies:
         copy.start()
     lx, ly = rhs.shape[0], rhs.shape[1]
     cols = order.shape[1]
@@ -98,8 +95,6 @@
     copies[2].wait()
     for x in range(lx):
         out[x] = pick(dot(diag[x], widen(fields[x])), ly).astype(BF16)
-    for load in loads:
-        load.wait()
 
 
 def local_kernel(sites, hops, source, field, residue):
@@ -120,28 +115,35 @@
         residue[x] = (source[x].astype(F32) + pick(dot(left, right), sites)).astype(BF16)
 
 
+def times_i(wide):
+    row = lax.broadcasted_iota(jnp.int32, (wide, wide), 0)
+    lane = lax.broadcasted_iota(jnp.int32, (wide, wide), 1)
+    half = wide // 2
+    return jnp.where(row == lane - half, 1.0, jnp.where(row == lane + half, -1.0, 0.0)).astype(BF16)
+
+
 def blend_kernel(sites, remote, diag, out):
+    count = remote.shape[0]
     lx, rows, wide = diag.shape
     comps = rows // sites
-    row = lax.broadcasted_iota(jnp.int32, (wide, wide), 0)
-    lane = lax.broadcasted_iota(jnp.int32, (wide, wide), 1)
-    move = jnp.where(row == lane - comps, 1.0, jnp.where(row == lane + comps, -1.0, 0.0)).astype(BF16)
-    for e in range(0, 4, 2):
+    move = times_i(wide)
+    step = 2 if count % 2 == 0 else 1
+    for e in range(0, count, step):
         for x in range(lx):
-            first, second = remote[e, x], remote[e + 1, x]
-            low_first, low_second = dot(first, move).astype(BF16), dot(second, move).astype(BF16)
+            blocks = [remote[e + n, x] for n in range(step)]
+            lower = [dot(block, move).astype(BF16) for block in blocks]
             for y in range(sites):
                 at = slice(y * comps, (y + 1) * comps)
                 right = jnp.concatenate(
                     [
-                        jnp.concatenate([first[at], second[at]], axis=1),
-                        jnp.concatenate([low_first[at], low_second[at]], axis=1),
+                        jnp.concatenate([block[at] for block in blocks], axis=1),
+                        jnp.concatenate([block[at] for block in lower], axis=1),
                     ],
                     axis=0,
                 )
-                both = dot(diag[x, at], right).astype(BF16)
-                out[e, x, at] = both[:, :wide]
-                out[e + 1, x, at] = both[:, wide:]
+                product = dot(diag[x, at], right).astype(BF16)
+                for n in range(step):
+                    out[e + n, x, at] = product[:, n * wide : (n + 1) * wide]
 
 
 def settle_kernel(sites, diag, residue, total):
@@ -153,20 +155,42 @@
     out[...] = token[...]
 
 
+def add_remote(sites, places, blended, total, fields, x):
+    right = jnp.concatenate([widen(f[x]) for f in fields], axis=0)
+    left = jnp.concatenate([blended[n, x] for n in places], axis=1)
+    return (total[x] + pick(dot(left, right), sites)).astype(BF16)
+
+
 def add_kernel(sites, places, blended, token, total, *refs):
     fields, out = refs[:-1], refs[-1]
     for x in range(out.shape[0]):
-        right = jnp.concatenate([widen(f[x]) for f in fields], axis=0)
-        left = jnp.concatenate([blended[n, x] for n in places], axis=1)
-        out[x] = (total[x] + pick(dot(left, right), sites)).astype(out.dtype)
-
-
-def insert_kernel(sites, current, diag, field, source, out):
-    lx = out.shape[0]
-    inserted = [pick(dot(current[x], widen(field[x])), sites).astype(BF16) for x in range(lx)]
-    for x in range(lx):
-        source[x] = inserted[x]
-        out[x] = pick(dot(diag[x], widen(inserted[x])), sites).astype(BF16)
+        out[x] = add_remote(sites, places, blended, total, fields, x)
+
+
+def add_insert_kernel(sites, places, blended, token, total, *refs):
+    fields, both, out, start = refs[:-3], refs[-3], refs[-2], refs[-1]
+    new = [add_remote(sites, places, blended, total, fields, x) for x in range(out.shape[0])]
+    for x in range(out.shape[0]):
+        out[x] = new[x]
+        start[x] = pick(dot(both[x], widen(new[x])), sites).astype(BF16)
+
+
+def add_gram_kernel(sites, places, blended, token, total, *refs):
+    fields, left, out, gram = refs[:-3], refs[-3], refs[-2], refs[-1]
+    new = [add_remote(sites, places, blended, total, fields, x) for x in range(out.shape[0])]
+    for x in range(out.shape[0]):
+        out[x] = new[x]
+    gram[...] = packed_gram(sites, left[...], jnp.concatenate(new, axis=0))
+
+
+def insert_kernel(sites, current, field, source):
+    for x in range(source.shape[0]):
+        source[x] = pick(dot(current[x], widen(field[x])), sites).astype(BF16)
+
+
+def turn_over_kernel(field, out):
+    lx, comps, width = field.shape
+    out[...] = field[...].reshape(lx * comps, width).astype(F32).T.astype(BF16)
 
 
 def leave_kernel(*refs):
@@ -186,13 +210,10 @@
             out[:, y] = dot(whole, place).astype(BF16).reshape(lx, comps, wide)
 
 
-def gram_kernel(sites, left, right, out):
-    lx, comps, width = left.shape
-    half = width // 2
+def packed_gram(sites, left, right):
+    half = left.shape[0] // 2
     cols = half // sites
-    a = left[...].reshape(lx * comps, width)
-    b = right[...].reshape(lx * comps, width)
-    full = lax.dot_general(a, b, (((0,), (0,)), ((), ())), preferred_element_type=F32)
+    full = dot(left, right)
     real = full[:half, :half] + full[half:, half:]
     imag = full[:half, half:] - full[half:, :half]
     group = lax.broadcasted_iota(jnp.int32, (cols, half), 1) // cols
@@ -205,14 +226,18 @@
         for y in range(1, sites):
             total = total + pltpu.roll(folded, y * cols, 1)
         sums.append(total)
-    out[...] = jnp.where(group == 0, sums[0], jnp.where(group == 1, sums[1], 0.0))
+    top = group[: cols // 2]
+    packed = jnp.where(top == 0, sums[0][: cols // 2], sums[1][: cols // 2])
+    packed = jnp.where(top == 2, sums[0][cols // 2 :], packed)
+    return jnp.where(top == 3, sums[1][cols // 2 :], packed)
 
 
 def margin_kernel(factor, summed, _, out):
     cols = out.shape[1]
     scaled = summed[...] * factor
-    out[0] = scaled[:, :cols]
-    out[1] = pltpu.roll(scaled, scaled.shape[1] - cols, 1)[:, :cols]
+    for part in range(4):
+        rows = slice(part // 2 * (cols // 2), (part // 2 + 1) * (cols // 2))
+        out[part % 2, rows] = (pltpu.roll(scaled, scaled.shape[1] - part * cols, 1) if part else scaled)[:, :cols]
 
 
 def call(kernel, outs, cost, *args, far=(), scratch=()):
@@ -284,46 +309,52 @@
 
     token_t = jax.ShapeDtypeStruct((8, 128), F32)
 
-    def sweeps(local, remote, diag, source, field):
+    def sweeps(local, remote, diag, source, field, last, last_t, extra):
         blended = call(functools.partial(blend_kernel, ly), blended_t, (4 * unit, 2**22), remote, diag)
         token = jnp.zeros(token_t.shape, F32)
-        for _ in range(SWEEPS - 1):
+        for left in reversed(range(SWEEPS - 1)):
             y = lax.ppermute(field, "tm", far_t)
             c = lax.ppermute(field, "tm", near_t)
             w = lax.ppermute(field, "space", far_s)
             e = lax.ppermute(field, "space", near_s)
+            if not isinstance(source, jax.Array):
+                source = call(functools.partial(insert_kernel, ly), field_t, (unit, 2**20), *source)
             residue = call(functools.partial(local_kernel, ly), field_t, (4 * unit, 2**21), local, source, field)
             total = call(functools.partial(settle_kernel, ly), total_t, (unit, 2**20), diag, residue)
             for arrived in (e, w):
                 token = call(after_kernel, token_t, (0, 2**24), arrived, token)
+            kernel, outs = (add_kernel, field_t) if left else (last, (field_t, last_t))
             field = call(
-                functools.partial(add_kernel, ly, (0, 1, 3, 2)), field_t, (4 * unit, 2**20), blended, token, total, e, w, y, c
+                functools.partial(kernel, ly, (0, 1, 3, 2)), outs, (4 * unit, 2**20), blended, token, total, e, w, y, c,
+                *(() if left else (extra,)),
             )
         return field
 
-    results = (field_t, field_t, jax.ShapeDtypeStruct(light_p.shape, BF16), blended_t, blended_t)
-    source, field, light_p, local, remote = call(
-        functools.partial(first_kernel, axes), results, (2 * unit, 2**20), order, rhs, light_p, light_h,
-        far=(0, 1, 2, 3),
+    results = (field_t, field_t, jax.ShapeDtypeStruct(light_p.shape, BF16))
+    source, field, light_p = call(
+        first_kernel, results, (2 * unit, 2**20), order, rhs, light_p,
+        far=(0, 1, 2),
         scratch=(
             pltpu.VMEM(order.shape, jnp.int32),
             pltpu.VMEM(rhs.shape, BF16),
             pltpu.SemaphoreType.DMA((3,)),
-            pltpu.SemaphoreType.DMA((8,)),
         ),
     )
-    light = sweeps(local, remote, light_p, source, field)
-    local, remote = call(
-        functools.partial(load_kernel, axes), (blended_t, blended_t), (0, 2**22), charm_h, far=(0,),
-        scratch=(pltpu.SemaphoreType.DMA((8,)),),
-    )
-    inserted, field = call(
-        functools.partial(insert_kernel, ly), (field_t, field_t), (2 * unit, 2**20), current, charm_p, light
-    )
-    seq = sweeps(local, remote, charm_p, inserted, field)
-    part = call(
-        functools.partial(gram_kernel, ly), jax.ShapeDtypeStruct((cols, ly * cols), F32), (unit, 2**20), light, seq
-    )
+
+    def load(hops):
+        return call(
+            functools.partial(load_kernel, axes), (blended_t, blended_t), (0, 2**22), hops, far=(0,),
+            scratch=(pltpu.SemaphoreType.DMA((8,)),),
+        )
+
+    local, remote = load(light_h)
+    one_t = jax.ShapeDtypeStruct((1, *current.shape), BF16)
+    both = call(functools.partial(blend_kernel, ly), one_t, (unit, 2**20), current[None], charm_p)[0]
+    light, field = sweeps(local, remote, light_p, source, field, add_insert_kernel, field_t, both)
+    local, remote = load(charm_h)
+    over = call(turn_over_kernel, jax.ShapeDtypeStruct((2 * ly * cols, lx * comps), BF16), (unit, 2**20), light)
+    part_t = jax.ShapeDtypeStruct((cols // 2, ly * cols), F32)
+    seq, part = sweeps(local, remote, charm_p, (current, light), field, add_gram_kernel, part_t, over)
     out_t = jax.ShapeDtypeStruct((lx, ly, comps, wide), BF16)
     light_out, seq_out, token = call(leave_kernel, (out_t, out_t, token_t), (unit, 2**22), light, seq)
     summed = total_sum(part)

time: 73.1 us -> 71.7 us (0.981)
  waiting for transfers between devices: 21.6 us -> 18.1 us
  Pallas kernels: 16.5 us -> 18.6 us
    ppermute x6, waiting for transfers between devices: 6.46 us -> 4.13 us  [sweeps(): e = lax.ppermute(field, 'space', near_s)]
    pallas_call x38 -> x40, Pallas kernels: 16.5 us -> 18.6 us  [call(): pl.pallas_call(kernel, out_shape=outs, in_specs=[HBM if i in far else VME...]
    ppermute x6, waiting for transfers between devices: 1.64 us -> 0.14 us  [sweeps(): y = lax.ppermute(field, 'tm', far_t)]
    ppermute x6, waiting for transfers between devices: 9.04 us -> 10.1 us  [sweeps(): w = lax.ppermute(field, 'space', far_s)]
  transfers between devices with their start and end apart: 31 -> 31, of which waited for: 15 -> 14; matrix products, arithmetic and copies ran while one was open for 0% -> 0% of each run, Pallas kernels for 14% -> 18%
where the time goes in v3:
time: 71.7 us; the launch traced here: 71.5 us
  starting transfers between devices  33.8 us (47%)
  Pallas kernels  18.6 us (26%)
  waiting for transfers between devices  18.1 us (25%)
  between operations  0.97 us (1%)
    pallas_call x40, Pallas kernels, call(): pl.pallas_call(kernel, out_shape=outs, in_specs=[HBM if i in far else VME...  18.6 us
    ppermute x6, starting transfers between devices, sweeps(): w = lax.ppermute(field, 'space', far_s)  14.9 us
    ppermute x6, waiting for transfers between devices, sweeps(): w = lax.ppermute(field, 'space', far_s)  10.1 us
    ppermute x7, starting transfers between devices, swap(): return lax.ppermute(value, ('space', 'tm'), list(enumerate(target)))  6.93 us
    ppermute x6, starting transfers between devices, sweeps(): c = lax.ppermute(field, 'tm', near_t)  6.75 us
    ppermute x6, starting transfers between devices, sweeps(): e = lax.ppermute(field, 'space', near_s)  4.46 us
    ppermute x6, waiting for transfers between devices, sweeps(): e = lax.ppermute(field, 'space', near_s)  4.13 us
    ppermute x7, waiting for transfers between devices, swap(): return lax.ppermute(value, ('space', 'tm'), list(enumerate(target)))  3.78 us
  transfers between devices with their start and end apart: 31, of which 14 were waited for; matrix products, arithmetic and copies ran while one was open for 0% of the time, Pallas kernels for 18%

profile of v3, /device:TPU:0, one launch (start us, length us, event | category | flops | bytes accessed | tf_op | source)
XLA Modules:
  0.0 71.5 jit_solution(564108543098708849)
XLA Ops:
  0.6 1.5 %shard_map.95 = (bf16[4,64,256]{2,1,0:T(8,128)(2,1)S(1)}, bf16[4,64,256]{2,1,0:T(8,128)(2,1)S(1)}, bf16[4,256,128]{2,1,0:T(8,128)(2,1)S(1)}) custom-call(s32[1,32]{1,0:T(1,128)} %bitcast.23, bf16[4,4,64,64]{3,2,1,0:T(8,128)(2,1)} %bitcast.21, bf16[4,256,128]{2,1,0:T(8,128)(2,1)} %bitcast.22), custom_call_target="tpu_custom_call" | custom-call | flops 134217728 | bytes 1048576 | tf_op jit(solution)/shard_map/pallas_call | solution.py:246
  2.2 3.0 %collective-permute-start.1 = (bf16[4,64,256]{2,1,0:T(8,128)(2,1)S(1)}, bf16[4,64,256]{2,1,0:T(8,128)(2,1)S(1)}, u32[]{:S(2)}, u32[]{:S(2)}) collective-permute-start(bf16[4,64,256]{2,1,0:T(8,128)(2,1)S(1)} %get-tuple-element.19.field), channel_id=1, source_target_pairs={{0,4},{4,0},{8,12},{12,8},{16,20},{20,16},{24,28},{28,24},{1,5},{5... | collective-permute-start | bytes 393224 | tf_op jit(solution)/shard_map/ppermute | solution.py:319
  5.2 3.6 %collective-permute-start = (bf16[4,64,256]{2,1,0:T(8,128)(2,1)S(1)}, bf16[4,64,256]{2,1,0:T(8,128)(2,1)S(1)}, u32[]{:S(2)}, u32[]{:S(2)}) collective-permute-start(bf16[4,64,256]{2,1,0:T(8,128)(2,1)S(1)} %get-tuple-element.19.field), channel_id=1, source_target_pairs={{0,28},{4,8},{8,4},{12,16},{16,12},{20,24},{24,20},{28,0},{1,29},{... | collective-permute-start | bytes 393224 | tf_op jit(solution)/shard_map/ppermute | solution.py:318
  9.2 1.2 %collective-permute-start.3 = (bf16[4,64,256]{2,1,0:T(8,128)(2,1)S(1)}, bf16[4,64,256]{2,1,0:T(8,128)(2,1)S(1)}, u32[]{:S(2)}, u32[]{:S(2)}) collective-permute-start(bf16[4,64,256]{2,1,0:T(8,128)(2,1)S(1)} %get-tuple-element.19.field), channel_id=1, source_target_pairs={{0,1},{1,0},{2,3},{3,2},{4,5},{5,4},{6,7},{7,6},{8,9},{9,8},{10,11... | collective-permute-start | bytes 393224 | tf_op jit(solution)/shard_map/ppermute | solution.py:317
  10.4 1.6 %shard_map.94 = (bf16[4,4,256,128]{3,2,1,0:T(8,128)(2,1)S(1)}, bf16[4,4,256,128]{3,2,1,0:T(8,128)(2,1)S(1)}) custom-call(bf16[8,4,256,128]{3,2,1,0:T(8,128)(2,1)} %bitcast.19), custom_call_target="tpu_custom_call" | custom-call | bytes 4194304 | tf_op jit(solution)/shard_map/pallas_call | solution.py:246
  12.7 1.6 %shard_map.96.blended = bf16[4,4,256,128]{3,2,1,0:T(8,128)(2,1)S(1)} custom-call(bf16[4,4,256,128]{3,2,1,0:T(8,128)(2,1)S(1)} %get-tuple-element.17.remote, bf16[4,256,128]{2,1,0:T(8,128)(2,1)S(1)} %get-tuple-element.18.diag), custom_call_target="tpu_custom_call" | custom-call | flops 268435456 | bytes 4194304 | tf_op jit(solution)/shard_map/pallas_call | solution.py:246
  15.0 2.3 %collective-permute-start.4 = (bf16[4,64,256]{2,1,0:T(8,128)(2,1)S(1)}, bf16[4,64,256]{2,1,0:T(8,128)(2,1)S(1)}, u32[]{:S(2)}, u32[]{:S(2)}) collective-permute-start(bf16[4,64,256]{2,1,0:T(8,128)(2,1)S(1)} %shard_map.101.field), channel_id=1, source_target_pairs={{0,28},{4,8},{8,4},{12,16},{16,12},{20,24},{24,20},{28,0},{1,29},{... | collective-permute-start | bytes 393224 | tf_op jit(solution)/shard_map/ppermute | solution.py:318
  17.4 1.6 %collective-permute-start.7 = (bf16[4,64,256]{2,1,0:T(8,128)(2,1)S(1)}, bf16[4,64,256]{2,1,0:T(8,128)(2,1)S(1)}, u32[]{:S(2)}, u32[]{:S(2)}) collective-permute-start(bf16[4,64,256]{2,1,0:T(8,128)(2,1)S(1)} %shard_map.101.field), channel_id=1, source_target_pairs={{0,1},{1,0},{2,3},{3,2},{4,5},{5,4},{6,7},{7,6},{8,9},{9,8},{10,11... | collective-permute-start | bytes 393224 | tf_op jit(solution)/shard_map/ppermute | solution.py:317
  19.8 1.4 %collective-permute-done.5._.refs_0_ = bf16[4,64,256]{2,1,0:T(8,128)(2,1)S(1)} collective-permute-done((bf16[4,64,256]{2,1,0:T(8,128)(2,1)S(1)}, bf16[4,64,256]{2,1,0:T(8,128)(2,1)S(1)}, u32[]{:S(2)}, u32[]{:S(2)}) %collective-permute-start.5) | collective-permute-done | bytes 131104 | tf_op jit(solution)/shard_map/ppermute | solution.py:319
  21.2 2.2 %collective-permute-done.4._.refs_1_ = bf16[4,64,256]{2,1,0:T(8,128)(2,1)S(1)} collective-permute-done((bf16[4,64,256]{2,1,0:T(8,128)(2,1)S(1)}, bf16[4,64,256]{2,1,0:T(8,128)(2,1)S(1)}, u32[]{:S(2)}, u32[]{:S(2)}) %collective-permute-start.4) | collective-permute-done | bytes 131104 | tf_op jit(solution)/shard_map/ppermute | solution.py:318
  24.2 2.0 %collective-permute-start.8 = (bf16[4,64,256]{2,1,0:T(8,128)(2,1)S(1)}, bf16[4,64,256]{2,1,0:T(8,128)(2,1)S(1)}, u32[]{:S(2)}, u32[]{:S(2)}) collective-permute-start(bf16[4,64,256]{2,1,0:T(8,128)(2,1)S(1)} %shard_map.106.field), channel_id=1, source_target_pairs={{0,28},{4,8},{8,4},{12,16},{16,12},{20,24},{24,20},{28,0},{1,29},{... | collective-permute-start | bytes 393224 | tf_op jit(solution)/shard_map/ppermute | solution.py:318
  29.9 2.2 %collective-permute-done.8._.refs_1_ = bf16[4,64,256]{2,1,0:T(8,128)(2,1)S(1)} collective-permute-done((bf16[4,64,256]{2,1,0:T(8,128)(2,1)S(1)}, bf16[4,64,256]{2,1,0:T(8,128)(2,1)S(1)}, u32[]{:S(2)}, u32[]{:S(2)}) %collective-permute-start.8) | collective-permute-done | bytes 131104 | tf_op jit(solution)/shard_map/ppermute | solution.py:318
  33.1 2.4 %collective-permute-start.12 = (bf16[4,64,256]{2,1,0:T(8,128)(2,1)S(1)}, bf16[4,64,256]{2,1,0:T(8,128)(2,1)S(1)}, u32[]{:S(2)}, u32[]{:S(2)}) collective-permute-start(bf16[4,64,256]{2,1,0:T(8,128)(2,1)S(1)} %get-tuple-element.24.field), channel_id=1, source_target_pairs={{0,28},{4,8},{8,4},{12,16},{16,12},{20,24},{24,20},{28,0},{1,29},{... | collective-permute-start | bytes 393224 | tf_op jit(solution)/shard_map/ppermute | solution.py:318
  36.2 1.6 %shard_map.113 = (bf16[4,4,256,128]{3,2,1,0:T(8,128)(2,1)S(1)}, bf16[4,4,256,128]{3,2,1,0:T(8,128)(2,1)S(1)}) custom-call(bf16[8,4,256,128]{3,2,1,0:T(8,128)(2,1)} %bitcast.20), custom_call_target="tpu_custom_call" | custom-call | bytes 4194304 | tf_op jit(solution)/shard_map/pallas_call | solution.py:246
  37.8 1.6 %shard_map.114.blended = bf16[4,4,256,128]{3,2,1,0:T(8,128)(2,1)S(1)} custom-call(bf16[4,4,256,128]{3,2,1,0:T(8,128)(2,1)S(1)} %get-tuple-element.23.remote, bf16[4,256,128]{2,1,0:T(8,128)(2,1)S(1)} %bitcast.12), custom_call_target="tpu_custom_call" | custom-call | flops 268435456 | bytes 4194304 | tf_op jit(solution)/shard_map/pallas_call | solution.py:246
  41.9 2.1 %collective-permute-start.16 = (bf16[4,64,256]{2,1,0:T(8,128)(2,1)S(1)}, bf16[4,64,256]{2,1,0:T(8,128)(2,1)S(1)}, u32[]{:S(2)}, u32[]{:S(2)}) collective-permute-start(bf16[4,64,256]{2,1,0:T(8,128)(2,1)S(1)} %shard_map.120.field), channel_id=1, source_target_pairs={{0,28},{4,8},{8,4},{12,16},{16,12},{20,24},{24,20},{28,0},{1,29},{... | collective-permute-start | bytes 393224 | tf_op jit(solution)/shard_map/ppermute | solution.py:318
  46.6 3.0 %collective-permute-done.16._.refs_1_ = bf16[4,64,256]{2,1,0:T(8,128)(2,1)S(1)} collective-permute-done((bf16[4,64,256]{2,1,0:T(8,128)(2,1)S(1)}, bf16[4,64,256]{2,1,0:T(8,128)(2,1)S(1)}, u32[]{:S(2)}, u32[]{:S(2)}) %collective-permute-start.16) | collective-permute-done | bytes 131104 | tf_op jit(solution)/shard_map/ppermute | solution.py:318
  50.3 2.5 %collective-permute-start.20 = (bf16[4,64,256]{2,1,0:T(8,128)(2,1)S(1)}, bf16[4,64,256]{2,1,0:T(8,128)(2,1)S(1)}, u32[]{:S(2)}, u32[]{:S(2)}) collective-permute-start(bf16[4,64,256]{2,1,0:T(8,128)(2,1)S(1)} %shard_map.125.field), channel_id=1, source_target_pairs={{0,28},{4,8},{8,4},{12,16},{16,12},{20,24},{24,20},{28,0},{1,29},{... | collective-permute-start | bytes 393224 | tf_op jit(solution)/shard_map/ppermute | solution.py:318
  54.8 1.2 %collective-permute-done.21._.refs_0_ = bf16[4,64,256]{2,1,0:T(8,128)(2,1)S(1)} collective-permute-done((bf16[4,64,256]{2,1,0:T(8,128)(2,1)S(1)}, bf16[4,64,256]{2,1,0:T(8,128)(2,1)S(1)}, u32[]{:S(2)}, u32[]{:S(2)}) %collective-permute-start.21) | collective-permute-done | bytes 131104 | tf_op jit(solution)/shard_map/ppermute | solution.py:319
  56.0 2.2 %collective-permute-done.20._.refs_1_ = bf16[4,64,256]{2,1,0:T(8,128)(2,1)S(1)} collective-permute-done((bf16[4,64,256]{2,1,0:T(8,128)(2,1)S(1)}, bf16[4,64,256]{2,1,0:T(8,128)(2,1)S(1)}, u32[]{:S(2)}, u32[]{:S(2)}) %collective-permute-start.20) | collective-permute-done | bytes 131104 | tf_op jit(solution)/shard_map/ppermute | solution.py:318
  59.0 1.2 %collective-permute-done.24 = f32[16,128]{1,0:T(8,128)S(1)} collective-permute-done((f32[16,128]{1,0:T(8,128)S(1)}, f32[16,128]{1,0:T(8,128)S(1)}, u32[]{:S(2)}, u32[]{:S(2)}) %collective-permute-start.24) | collective-permute-done | bytes 8224 | tf_op jit(solution)/shard_map/ppermute | solution.py:276
  60.7 1.7 %collective-permute-start.26 = (f32[16,128]{1,0:T(8,128)S(1)}, f32[16,128]{1,0:T(8,128)S(1)}, u32[]{:S(2)}, u32[]{:S(2)}) collective-permute-start(f32[16,128]{1,0:T(8,128)S(1)} %add.21), channel_id=1, source_target_pairs={{0,5},{1,4},{2,7},{3,6},{4,1},{5,0},{6,3},{7,2},{8,13},{9,12},{10,... | collective-permute-start | bytes 24584 | tf_op jit(solution)/shard_map/ppermute | solution.py:276
  64.1 1.4 %collective-permute-done.25 = f32[16,128]{1,0:T(8,128)S(1)} collective-permute-done((f32[16,128]{1,0:T(8,128)S(1)}, f32[16,128]{1,0:T(8,128)S(1)}, u32[]{:S(2)}, u32[]{:S(2)}) %collective-permute-start.25) | collective-permute-done | bytes 8224 | tf_op jit(solution)/shard_map/ppermute | solution.py:276
  67.5 1.9 %collective-permute-start.28 = (f32[16,128]{1,0:T(8,128)S(1)}, f32[16,128]{1,0:T(8,128)S(1)}, u32[]{:S(2)}, u32[]{:S(2)}) collective-permute-start(f32[16,128]{1,0:T(8,128)S(1)} %add_add_fusion.1), channel_id=1, source_target_pairs={{0,9},{1,8},{2,11},{3,10},{4,13},{5,12},{6,15},{7,14},{8,1},{9,0},... | collective-permute-start | bytes 24584 | tf_op jit(solution)/shard_map/ppermute | solution.py:276
  (86 shorter events, 23.6 us)
Async XLA Ops:
  2.2 12.2 %collective-permute-start.1 = (bf16[4,64,256]{2,1,0:T(8,128)(2,1)S(1)}, bf16[4,64,256]{2,1,0:T(8,128)(2,1)S(1)}, u32[]{:S(2)}, u32[]{:S(2)}) collective-permute-start(bf16[4,64,256]{2,1,0:T(8,128)(2,1)S(1)} %get-tuple-element.19.field), channel_id=1, source_target_pairs={{0,4},{4,0},{8,12},{12,8},{16,20},{20,16},{24,28},{28,24},{1,5},{5... | collective-permute-start | bytes 393224 | tf_op jit(solution)/shard_map/ppermute | solution.py:319
  5.2 9.2 %collective-permute-start = (bf16[4,64,256]{2,1,0:T(8,128)(2,1)S(1)}, bf16[4,64,256]{2,1,0:T(8,128)(2,1)S(1)}, u32[]{:S(2)}, u32[]{:S(2)}) collective-permute-start(bf16[4,64,256]{2,1,0:T(8,128)(2,1)S(1)} %get-tuple-element.19.field), channel_id=1, source_target_pairs={{0,28},{4,8},{8,4},{12,16},{16,12},{20,24},{24,20},{28,0},{1,29},{... | collective-permute-start | bytes 393224 | tf_op jit(solution)/shard_map/ppermute | solution.py:318
  8.8 5.7 %collective-permute-start.2 = (bf16[4,64,256]{2,1,0:T(8,128)(2,1)S(1)}, bf16[4,64,256]{2,1,0:T(8,128)(2,1)S(1)}, u32[]{:S(2)}, u32[]{:S(2)}) collective-permute-start(bf16[4,64,256]{2,1,0:T(8,128)(2,1)S(1)} %get-tuple-element.19.field), channel_id=1, source_target_pairs={{0,3},{1,2},{2,1},{3,0},{4,7},{5,6},{6,5},{7,4},{8,11},{9,10},{10,... | collective-permute-start | bytes 393224 | tf_op jit(solution)/shard_map/ppermute | solution.py:316
  9.2 5.3 %collective-permute-start.3 = (bf16[4,64,256]{2,1,0:T(8,128)(2,1)S(1)}, bf16[4,64,256]{2,1,0:T(8,128)(2,1)S(1)}, u32[]{:S(2)}, u32[]{:S(2)}) collective-permute-start(bf16[4,64,256]{2,1,0:T(8,128)(2,1)S(1)} %get-tuple-element.19.field), channel_id=1, source_target_pairs={{0,1},{1,0},{2,3},{3,2},{4,5},{5,4},{6,7},{7,6},{8,9},{9,8},{10,11... | collective-permute-start | bytes 393224 | tf_op jit(solution)/shard_map/ppermute | solution.py:317
  15.0 6.2 %collective-permute-start.5 = (bf16[4,64,256]{2,1,0:T(8,128)(2,1)S(1)}, bf16[4,64,256]{2,1,0:T(8,128)(2,1)S(1)}, u32[]{:S(2)}, u32[]{:S(2)}) collective-permute-start(bf16[4,64,256]{2,1,0:T(8,128)(2,1)S(1)} %shard_map.101.field), channel_id=1, source_target_pairs={{0,4},{4,0},{8,12},{12,8},{16,20},{20,16},{24,28},{28,24},{1,5},{5... | collective-permute-start | bytes 393224 | tf_op jit(solution)/shard_map/ppermute | solution.py:319
  15.0 8.3 %collective-permute-start.4 = (bf16[4,64,256]{2,1,0:T(8,128)(2,1)S(1)}, bf16[4,64,256]{2,1,0:T(8,128)(2,1)S(1)}, u32[]{:S(2)}, u32[]{:S(2)}) collective-permute-start(bf16[4,64,256]{2,1,0:T(8,128)(2,1)S(1)} %shard_map.101.field), channel_id=1, source_target_pairs={{0,28},{4,8},{8,4},{12,16},{16,12},{20,24},{24,20},{28,0},{1,29},{... | collective-permute-start | bytes 393224 | tf_op jit(solution)/shard_map/ppermute | solution.py:318
  17.4 6.0 %collective-permute-start.6 = (bf16[4,64,256]{2,1,0:T(8,128)(2,1)S(1)}, bf16[4,64,256]{2,1,0:T(8,128)(2,1)S(1)}, u32[]{:S(2)}, u32[]{:S(2)}) collective-permute-start(bf16[4,64,256]{2,1,0:T(8,128)(2,1)S(1)} %shard_map.101.field), channel_id=1, source_target_pairs={{0,3},{1,2},{2,1},{3,0},{4,7},{5,6},{6,5},{7,4},{8,11},{9,10},{10,... | collective-permute-start | bytes 393224 | tf_op jit(solution)/shard_map/ppermute | solution.py:316
  17.4 6.0 %collective-permute-start.7 = (bf16[4,64,256]{2,1,0:T(8,128)(2,1)S(1)}, bf16[4,64,256]{2,1,0:T(8,128)(2,1)S(1)}, u32[]{:S(2)}, u32[]{:S(2)}) collective-permute-start(bf16[4,64,256]{2,1,0:T(8,128)(2,1)S(1)} %shard_map.101.field), channel_id=1, source_target_pairs={{0,1},{1,0},{2,3},{3,2},{4,5},{5,4},{6,7},{7,6},{8,9},{9,8},{10,11... | collective-permute-start | bytes 393224 | tf_op jit(solution)/shard_map/ppermute | solution.py:317
  23.8 6.0 %collective-permute-start.9 = (bf16[4,64,256]{2,1,0:T(8,128)(2,1)S(1)}, bf16[4,64,256]{2,1,0:T(8,128)(2,1)S(1)}, u32[]{:S(2)}, u32[]{:S(2)}) collective-permute-start(bf16[4,64,256]{2,1,0:T(8,128)(2,1)S(1)} %shard_map.106.field), channel_id=1, source_target_pairs={{0,4},{4,0},{8,12},{12,8},{16,20},{20,16},{24,28},{28,24},{1,5},{5... | collective-permute-start | bytes 393224 | tf_op jit(solution)/shard_map/ppermute | solution.py:319
  24.2 7.8 %collective-permute-start.8 = (bf16[4,64,256]{2,1,0:T(8,128)(2,1)S(1)}, bf16[4,64,256]{2,1,0:T(8,128)(2,1)S(1)}, u32[]{:S(2)}, u32[]{:S(2)}) collective-permute-start(bf16[4,64,256]{2,1,0:T(8,128)(2,1)S(1)} %shard_map.106.field), channel_id=1, source_target_pairs={{0,28},{4,8},{8,4},{12,16},{16,12},{20,24},{24,20},{28,0},{1,29},{... | collective-permute-start | bytes 393224 | tf_op jit(solution)/shard_map/ppermute | solution.py:318
  26.2 5.8 %collective-permute-start.10 = (bf16[4,64,256]{2,1,0:T(8,128)(2,1)S(1)}, bf16[4,64,256]{2,1,0:T(8,128)(2,1)S(1)}, u32[]{:S(2)}, u32[]{:S(2)}) collective-permute-start(bf16[4,64,256]{2,1,0:T(8,128)(2,1)S(1)} %shard_map.106.field), channel_id=1, source_target_pairs={{0,3},{1,2},{2,1},{3,0},{4,7},{5,6},{6,5},{7,4},{8,11},{9,10},{10,... | collective-permute-start | bytes 393224 | tf_op jit(solution)/shard_map/ppermute | solution.py:316
  26.2 5.8 %collective-permute-start.11 = (bf16[4,64,256]{2,1,0:T(8,128)(2,1)S(1)}, bf16[4,64,256]{2,1,0:T(8,128)(2,1)S(1)}, u32[]{:S(2)}, u32[]{:S(2)}) collective-permute-start(bf16[4,64,256]{2,1,0:T(8,128)(2,1)S(1)} %shard_map.106.field), channel_id=1, source_target_pairs={{0,1},{1,0},{2,3},{3,2},{4,5},{5,4},{6,7},{7,6},{8,9},{9,8},{10,11... | collective-permute-start | bytes 393224 | tf_op jit(solution)/shard_map/ppermute | solution.py:317
  32.7 7.7 %collective-permute-start.13 = (bf16[4,64,256]{2,1,0:T(8,128)(2,1)S(1)}, bf16[4,64,256]{2,1,0:T(8,128)(2,1)S(1)}, u32[]{:S(2)}, u32[]{:S(2)}) collective-permute-start(bf16[4,64,256]{2,1,0:T(8,128)(2,1)S(1)} %get-tuple-element.24.field), channel_id=1, source_target_pairs={{0,4},{4,0},{8,12},{12,8},{16,20},{20,16},{24,28},{28,24},{1,5},{5... | collective-permute-start | bytes 393224 | tf_op jit(solution)/shard_map/ppermute | solution.py:319
  33.1 8.0 %collective-permute-start.12 = (bf16[4,64,256]{2,1,0:T(8,128)(2,1)S(1)}, bf16[4,64,256]{2,1,0:T(8,128)(2,1)S(1)}, u32[]{:S(2)}, u32[]{:S(2)}) collective-permute-start(bf16[4,64,256]{2,1,0:T(8,128)(2,1)S(1)} %get-tuple-element.24.field), channel_id=1, source_target_pairs={{0,28},{4,8},{8,4},{12,16},{16,12},{20,24},{24,20},{28,0},{1,29},{... | collective-permute-start | bytes 393224 | tf_op jit(solution)/shard_map/ppermute | solution.py:318
  35.5 5.6 %collective-permute-start.14 = (bf16[4,64,256]{2,1,0:T(8,128)(2,1)S(1)}, bf16[4,64,256]{2,1,0:T(8,128)(2,1)S(1)}, u32[]{:S(2)}, u32[]{:S(2)}) collective-permute-start(bf16[4,64,256]{2,1,0:T(8,128)(2,1)S(1)} %get-tuple-element.24.field), channel_id=1, source_target_pairs={{0,3},{1,2},{2,1},{3,0},{4,7},{5,6},{6,5},{7,4},{8,11},{9,10},{10,... | collective-permute-start | bytes 393224 | tf_op jit(solution)/shard_map/ppermute | solution.py:316
  35.5 5.6 %collective-permute-start.15 = (bf16[4,64,256]{2,1,0:T(8,128)(2,1)S(1)}, bf16[4,64,256]{2,1,0:T(8,128)(2,1)S(1)}, u32[]{:S(2)}, u32[]{:S(2)}) collective-permute-start(bf16[4,64,256]{2,1,0:T(8,128)(2,1)S(1)} %get-tuple-element.24.field), channel_id=1, source_target_pairs={{0,1},{1,0},{2,3},{3,2},{4,5},{5,4},{6,7},{7,6},{8,9},{9,8},{10,11... | collective-permute-start | bytes 393224 | tf_op jit(solution)/shard_map/ppermute | solution.py:317
  41.5 5.0 %collective-permute-start.17 = (bf16[4,64,256]{2,1,0:T(8,128)(2,1)S(1)}, bf16[4,64,256]{2,1,0:T(8,128)(2,1)S(1)}, u32[]{:S(2)}, u32[]{:S(2)}) collective-permute-start(bf16[4,64,256]{2,1,0:T(8,128)(2,1)S(1)} %shard_map.120.field), channel_id=1, source_target_pairs={{0,4},{4,0},{8,12},{12,8},{16,20},{20,16},{24,28},{28,24},{1,5},{5... | collective-permute-start | bytes 393224 | tf_op jit(solution)/shard_map/ppermute | solution.py:319
  41.9 7.7 %collective-permute-start.16 = (bf16[4,64,256]{2,1,0:T(8,128)(2,1)S(1)}, bf16[4,64,256]{2,1,0:T(8,128)(2,1)S(1)}, u32[]{:S(2)}, u32[]{:S(2)}) collective-permute-start(bf16[4,64,256]{2,1,0:T(8,128)(2,1)S(1)} %shard_map.120.field), channel_id=1, source_target_pairs={{0,28},{4,8},{8,4},{12,16},{16,12},{20,24},{24,20},{28,0},{1,29},{... | collective-permute-start | bytes 393224 | tf_op jit(solution)/shard_map/ppermute | solution.py:318
  44.0 5.6 %collective-permute-start.18 = (bf16[4,64,256]{2,1,0:T(8,128)(2,1)S(1)}, bf16[4,64,256]{2,1,0:T(8,128)(2,1)S(1)}, u32[]{:S(2)}, u32[]{:S(2)}) collective-permute-start(bf16[4,64,256]{2,1,0:T(8,128)(2,1)S(1)} %shard_map.120.field), channel_id=1, source_target_pairs={{0,3},{1,2},{2,1},{3,0},{4,7},{5,6},{6,5},{7,4},{8,11},{9,10},{10,... | collective-permute-start | bytes 393224 | tf_op jit(solution)/shard_map/ppermute | solution.py:316
  44.2 5.4 %collective-permute-start.19 = (bf16[4,64,256]{2,1,0:T(8,128)(2,1)S(1)}, bf16[4,64,256]{2,1,0:T(8,128)(2,1)S(1)}, u32[]{:S(2)}, u32[]{:S(2)}) collective-permute-start(bf16[4,64,256]{2,1,0:T(8,128)(2,1)S(1)} %shard_map.120.field), channel_id=1, source_target_pairs={{0,1},{1,0},{2,3},{3,2},{4,5},{5,4},{6,7},{7,6},{8,9},{9,8},{10,11... | collective-permute-start | bytes 393224 | tf_op jit(solution)/shard_map/ppermute | solution.py:317
  50.0 5.9 %collective-permute-start.21 = (bf16[4,64,256]{2,1,0:T(8,128)(2,1)S(1)}, bf16[4,64,256]{2,1,0:T(8,128)(2,1)S(1)}, u32[]{:S(2)}, u32[]{:S(2)}) collective-permute-start(bf16[4,64,256]{2,1,0:T(8,128)(2,1)S(1)} %shard_map.125.field), channel_id=1, source_target_pairs={{0,4},{4,0},{8,12},{12,8},{16,20},{20,16},{24,28},{28,24},{1,5},{5... | collective-permute-start | bytes 393224 | tf_op jit(solution)/shard_map/ppermute | solution.py:319
  50.3 7.8 %collective-permute-start.20 = (bf16[4,64,256]{2,1,0:T(8,128)(2,1)S(1)}, bf16[4,64,256]{2,1,0:T(8,128)(2,1)S(1)}, u32[]{:S(2)}, u32[]{:S(2)}) collective-permute-start(bf16[4,64,256]{2,1,0:T(8,128)(2,1)S(1)} %shard_map.125.field), channel_id=1, source_target_pairs={{0,28},{4,8},{8,4},{12,16},{16,12},{20,24},{24,20},{28,0},{1,29},{... | collective-permute-start | bytes 393224 | tf_op jit(solution)/shard_map/ppermute | solution.py:318
  52.8 5.4 %collective-permute-start.22 = (bf16[4,64,256]{2,1,0:T(8,128)(2,1)S(1)}, bf16[4,64,256]{2,1,0:T(8,128)(2,1)S(1)}, u32[]{:S(2)}, u32[]{:S(2)}) collective-permute-start(bf16[4,64,256]{2,1,0:T(8,128)(2,1)S(1)} %shard_map.125.field), channel_id=1, source_target_pairs={{0,3},{1,2},{2,1},{3,0},{4,7},{5,6},{6,5},{7,4},{8,11},{9,10},{10,... | collective-permute-start | bytes 393224 | tf_op jit(solution)/shard_map/ppermute | solution.py:316
  52.9 5.3 %collective-permute-start.23 = (bf16[4,64,256]{2,1,0:T(8,128)(2,1)S(1)}, bf16[4,64,256]{2,1,0:T(8,128)(2,1)S(1)}, u32[]{:S(2)}, u32[]{:S(2)}) collective-permute-start(bf16[4,64,256]{2,1,0:T(8,128)(2,1)S(1)} %shard_map.125.field), channel_id=1, source_target_pairs={{0,1},{1,0},{2,3},{3,2},{4,5},{5,4},{6,7},{7,6},{8,9},{9,8},{10,11... | collective-permute-start | bytes 393224 | tf_op jit(solution)/shard_map/ppermute | solution.py:317
  (9 other events, 48.7 us)

commit v4 on v3

--- a/solution.py
+++ b/solution.py
@@ -148,39 +148,48 @@
 
 def settle_kernel(sites, diag, residue, total):
     for x in range(residue.shape[0]):
-        total[x] = pick(dot(diag[x], widen(residue[x])), sites)
+        total[x] = pick(dot(diag[x], widen(residue[x].astype(BF16))), sites)
 
 
 def after_kernel(_, token, out):
     out[...] = token[...]
-
-
-def add_remote(sites, places, blended, total, fields, x):
-    right = jnp.concatenate([widen(f[x]) for f in fields], axis=0)
-    left = jnp.concatenate([blended[n, x] for n in places], axis=1)
-    return (total[x] + pick(dot(left, right), sites)).astype(BF16)
 
 
 def add_kernel(sites, places, blended, token, total, *refs):
     fields, out = refs[:-1], refs[-1]
     for x in range(out.shape[0]):
-        out[x] = add_remote(sites, places, blended, total, fields, x)
-
-
-def add_insert_kernel(sites, places, blended, token, total, *refs):
-    fields, both, out, start = refs[:-3], refs[-3], refs[-2], refs[-1]
-    new = [add_remote(sites, places, blended, total, fields, x) for x in range(out.shape[0])]
-    for x in range(out.shape[0]):
-        out[x] = new[x]
-        start[x] = pick(dot(both[x], widen(new[x])), sites).astype(BF16)
-
-
-def add_gram_kernel(sites, places, blended, token, total, *refs):
-    fields, left, out, gram = refs[:-3], refs[-3], refs[-2], refs[-1]
-    new = [add_remote(sites, places, blended, total, fields, x) for x in range(out.shape[0])]
-    for x in range(out.shape[0]):
-        out[x] = new[x]
-    gram[...] = packed_gram(sites, left[...], jnp.concatenate(new, axis=0))
+        right = jnp.concatenate([widen(f[x]) for f in fields], axis=0)
+        left = jnp.concatenate([blended[n, x] for n in places], axis=1)
+        out[x] = (total[x] + pick(dot(left, right), sites)).astype(BF16)
+
+
+def adjoint_kernel(sites, over, blended, out):
+    width = over.shape[1]
+    count, lx, rows, wide = blended.shape
+    comps = rows // sites
+    row = lax.broadcasted_iota(jnp.int32, (comps, rows), 0)
+    spread = jnp.where(row == lax.broadcasted_iota(jnp.int32, (comps, rows), 1) % comps, 1.0, 0.0).astype(BF16)
+    half = width // 2
+    site = lax.broadcasted_iota(jnp.int32, (width, rows), 0) % half // (half // sites)
+    own = site == lax.broadcasted_iota(jnp.int32, (width, rows), 1) // comps
+    low = lax.broadcasted_iota(jnp.int32, (half, wide), 1) < comps
+    for x in range(0, lx, 2):
+        blocks = [jnp.where(own, dot(over[x + k], spread), 0.0).astype(BF16) for k in range(2)]
+        at = slice(x // 2 * wide, (x // 2 + 1) * wide)
+        for n in range(count):
+            one, two = (dot(blocks[k], blended[n, x + k]) for k in range(2))
+            re = jnp.where(low, one[:half] + pltpu.roll(one[half:], comps, 1), pltpu.roll(two[:half], comps, 1) + two[half:])
+            im = jnp.where(low, one[half:] - pltpu.roll(one[:half], comps, 1), pltpu.roll(two[half:], comps, 1) - two[:half])
+            out[n, :half, at] = re.astype(BF16)
+            out[n, half:, at] = im.astype(BF16)
+
+
+def gram_kernel(sites, places, whole, adjoint, token, total, *refs):
+    fields, out = refs[:-1], refs[-1]
+    left = jnp.concatenate([whole[...]] + [adjoint[n] for n in places], axis=1)
+    right = [total[...].astype(BF16)] + [f[...] for f in fields]
+    right = jnp.concatenate([f.reshape(-1, f.shape[2]) for f in right], axis=0)
+    out[...] = packed_gram(sites, left, right)
 
 
 def insert_kernel(sites, current, field, source):
@@ -188,9 +197,11 @@
         source[x] = pick(dot(current[x], widen(field[x])), sites).astype(BF16)
 
 
-def turn_over_kernel(field, out):
+def turn_over_kernel(field, whole, out):
     lx, comps, width = field.shape
-    out[...] = field[...].reshape(lx * comps, width).astype(F32).T.astype(BF16)
+    whole[...] = field[...].reshape(lx * comps, width).astype(F32).T.astype(BF16)
+    for x in range(lx):
+        out[x] = field[x].astype(F32).T.astype(BF16)
 
 
 def leave_kernel(*refs):
@@ -232,9 +243,10 @@
     return jnp.where(top == 3, sums[1][cols // 2 :], packed)
 
 
-def margin_kernel(factor, summed, _, out):
+def margin_kernel(factor, _, token, *refs):
+    out = refs[-1]
     cols = out.shape[1]
-    scaled = summed[...] * factor
+    scaled = sum([ref[...] for ref in refs[1:-1]], refs[0][...]) * factor
     for part in range(4):
         rows = slice(part // 2 * (cols // 2), (part // 2 + 1) * (cols // 2))
         out[part % 2, rows] = (pltpu.roll(scaled, scaled.shape[1] - part * cols, 1) if part else scaled)[:, :cols]
@@ -254,6 +266,24 @@
     )(*args)
 
 
+def in_order(arrivals, token):
+    for arrived in arrivals:
+        token = call(after_kernel, jax.ShapeDtypeStruct(token.shape, token.dtype), (0, 2**24), arrived, token)
+    return token
+
+
+def sum_kernel(token, value, *refs):
+    total = value[...]
+    for ref in refs[:-1]:
+        total = total + ref[...]
+    refs[-1][...] = total
+
+
+def add_up(value, got, aside):
+    token = in_order((*aside, *got), jnp.zeros((8, 128), F32))
+    return call(sum_kernel, jax.ShapeDtypeStruct(value.shape, F32), (0, 2**14), token, value, *got)
+
+
 def swaps(axis):
     count = lax.axis_size(axis)
     if count % 2:
@@ -266,10 +296,10 @@
     return near, far
 
 
-def total_sum(value):
+def total_sum(value, last, aside):
     spaces, times = lax.axis_size("space"), lax.axis_size("tm")
     if (spaces & (spaces - 1)) or (times & (times - 1)):
-        return lax.psum(value, ("space", "tm"))
+        return last(lax.psum(value, ("space", "tm")))
 
     def swap(mask):
         target = [(s ^ mask[0]) * times + (t ^ mask[1]) for s in range(spaces) for t in range(times)]
@@ -278,14 +308,17 @@
     cross = 1 if times > 1 else 0
     steps = [(0, 1 << k) for k in range(1, times.bit_length() - 1)]
     steps[1:1] = [(1 << k, 0) for k in range(spaces.bit_length() - 1)]
-    if cross:
-        value = value + swap((0, 1))
+    groups = []
     for k in range(0, len(steps), 2):
         pair = steps[k : k + 2]
         if len(pair) == 2:
             pair.append((pair[0][0] ^ pair[1][0], pair[0][1] ^ pair[1][1]))
-        value = sum([swap((s, t ^ cross)) for s, t in pair], value)
-    return value
+        groups.append([(s, t ^ cross) for s, t in reversed(pair)])
+    if cross:
+        groups.insert(0, [(0, 1)])
+    for group in groups[:-1]:
+        value = add_up(value, [swap(mask) for mask in group], aside if group == groups[-2] else ())
+    return last(value, *[swap(mask) for mask in groups[-1]]) if groups else last(value)
 
 
 def body(right_side, batch_order, light_diag, light_hops, charm_diag, charm_hops, current_blocks):
@@ -309,8 +342,7 @@
 
     token_t = jax.ShapeDtypeStruct((8, 128), F32)
 
-    def sweeps(local, remote, diag, source, field, last, last_t, extra):
-        blended = call(functools.partial(blend_kernel, ly), blended_t, (4 * unit, 2**22), remote, diag)
+    def sweeps(local, blended, diag, source, field, aside=()):
         token = jnp.zeros(token_t.shape, F32)
         for left in reversed(range(SWEEPS - 1)):
             y = lax.ppermute(field, "tm", far_t)
@@ -321,14 +353,20 @@
                 source = call(functools.partial(insert_kernel, ly), field_t, (unit, 2**20), *source)
             residue = call(functools.partial(local_kernel, ly), field_t, (4 * unit, 2**21), local, source, field)
             total = call(functools.partial(settle_kernel, ly), total_t, (unit, 2**20), diag, residue)
-            for arrived in (e, w):
-                token = call(after_kernel, token_t, (0, 2**24), arrived, token)
-            kernel, outs = (add_kernel, field_t) if left else (last, (field_t, last_t))
-            field = call(
-                functools.partial(kernel, ly, (0, 1, 3, 2)), outs, (4 * unit, 2**20), blended, token, total, e, w, y, c,
-                *(() if left else (extra,)),
-            )
-        return field
+            token = in_order((*(aside if left == 1 else ()), e, w), token)
+
+            def finish(kernel, outs, matrices, token, total, got=(e, w, y, c)):
+                return call(
+                    functools.partial(kernel, ly, (0, 1, 3, 2)), outs, (4 * unit, 2**20), *matrices, token, total, *got
+                )
+
+            if left:
+                field = finish(add_kernel, field_t, (blended,), token, total)
+        return finish, token, total
+
+    def blend(blocks, diag):
+        outs = jax.ShapeDtypeStruct(blocks.shape, BF16)
+        return call(functools.partial(blend_kernel, ly), outs, (len(blocks) * unit, 2**22), blocks, diag)
 
     results = (field_t, field_t, jax.ShapeDtypeStruct(light_p.shape, BF16))
     source, field, light_p = call(
@@ -348,21 +386,38 @@
         )
 
     local, remote = load(light_h)
-    one_t = jax.ShapeDtypeStruct((1, *current.shape), BF16)
-    both = call(functools.partial(blend_kernel, ly), one_t, (unit, 2**20), current[None], charm_p)[0]
-    light, field = sweeps(local, remote, light_p, source, field, add_insert_kernel, field_t, both)
-    local, remote = load(charm_h)
-    over = call(turn_over_kernel, jax.ShapeDtypeStruct((2 * ly * cols, lx * comps), BF16), (unit, 2**20), light)
+    blended = blend(remote, light_p)
+    both = blend(current[None], charm_p)[0]
+    ahead = blend(blended, both)
+    next_local, next_remote = load(charm_h)
+    finish, token, total = sweeps(local, blended, light_p, source, field, (both, next_local))
+    start = call(functools.partial(settle_kernel, ly), total_t, (unit, 2**20), both, total)
+    field = finish(add_kernel, field_t, (ahead,), token, start)
+    light = finish(add_kernel, field_t, (blended,), field, total)
+    local, blended = next_local, blend(next_remote, charm_p)
+    over_t = (
+        jax.ShapeDtypeStruct((2 * ly * cols, lx * comps), BF16),
+        jax.ShapeDtypeStruct((lx, 2 * ly * cols, comps), BF16),
+    )
+    whole, over = call(turn_over_kernel, over_t, (unit, 2**20), light)
+    out_t = jax.ShapeDtypeStruct((lx, ly, comps, wide), BF16)
+    light_out, left_light = call(leave_kernel, (out_t, token_t), (unit, 2**21), light)
+    finish, token, total = sweeps(local, blended, charm_p, (current, light), field, (left_light,))
+    adjoint_t = jax.ShapeDtypeStruct((4, 2 * ly * cols, lx * comps), BF16)
+    adjoint = call(functools.partial(adjoint_kernel, ly), adjoint_t, (4 * unit, 2**21), over, blended)
     part_t = jax.ShapeDtypeStruct((cols // 2, ly * cols), F32)
-    seq, part = sweeps(local, remote, charm_p, (current, light), field, add_gram_kernel, part_t, over)
-    out_t = jax.ShapeDtypeStruct((lx, ly, comps, wide), BF16)
-    light_out, seq_out, token = call(leave_kernel, (out_t, out_t, token_t), (unit, 2**22), light, seq)
-    summed = total_sum(part)
+    part = finish(gram_kernel, part_t, (whole, adjoint), token, total)
+    seq = finish(add_kernel, field_t, (blended,), part, total)
+    seq_out, token = call(leave_kernel, (out_t, token_t), (unit, 2**21), seq)
     site_count = lx * ly * lax.axis_size("space") * lax.axis_size("tm")
     factor = 1.0 / math.sqrt(site_count * comps)
-    margin = call(
-        functools.partial(margin_kernel, factor), jax.ShapeDtypeStruct((2, cols, cols), F32), (2**14, 2**14), summed, token
-    )
+
+    def last(value, *got):
+        ordered = in_order(got, jnp.zeros(token_t.shape, F32))
+        margin_t = jax.ShapeDtypeStruct((2, cols, cols), F32)
+        return call(functools.partial(margin_kernel, factor), margin_t, (2**14, 2**14), token, ordered, value, *got)
+
+    margin = total_sum(part, last, (token,))
     return light_out.reshape(right_side.shape), seq_out.reshape(right_side.shape), margin
 
 

time: 71.7 us -> 71.2 us (level)
  waiting for transfers between devices: 18.1 us -> 13.3 us
  Pallas kernels: 18.6 us -> 22.8 us
    pallas_call x40 -> x59, Pallas kernels: 18.6 us -> 22.8 us  [call(): pl.pallas_call(kernel, out_shape=outs, in_specs=[HBM if i in far else VME...]
    ppermute x6, waiting for transfers between devices: 4.13 us -> 0.99 us  [sweeps(): e = lax.ppermute(field, 'space', near_s)]
    ppermute x6, waiting for transfers between devices: 10.1 us -> 8.71 us  [sweeps(): w = lax.ppermute(field, 'space', far_s)]
  transfers between devices with their start and end apart: 31 -> 31, of which waited for: 14 -> 12; matrix products, arithmetic and copies ran while one was open for 0% -> 0% of each run, Pallas kernels for 18% -> 25%
where the time goes in v4:
time: 71.2 us; the launch traced here: 71 us
  starting transfers between devices  33.8 us (47%)
  Pallas kernels  22.8 us (32%)
  waiting for transfers between devices  13.3 us (19%)
  between operations  1.08 us (2%)
    pallas_call x59, Pallas kernels, call(): pl.pallas_call(kernel, out_shape=outs, in_specs=[HBM if i in far else VME...  22.8 us
    ppermute x6, starting transfers between devices, sweeps(): w = lax.ppermute(field, 'space', far_s)  15 us
    ppermute x6, waiting for transfers between devices, sweeps(): w = lax.ppermute(field, 'space', far_s)  8.71 us
    ppermute x7, starting transfers between devices, swap(): return lax.ppermute(value, ('space', 'tm'), list(enumerate(target)))  6.93 us
    ppermute x6, starting transfers between devices, sweeps(): c = lax.ppermute(field, 'tm', near_t)  6.71 us
    ppermute x6, starting transfers between devices, sweeps(): e = lax.ppermute(field, 'space', near_s)  4.4 us
    ppermute x7, waiting for transfers between devices, swap(): return lax.ppermute(value, ('space', 'tm'), list(enumerate(target)))  3.5 us
  transfers between devices with their start and end apart: 31, of which 12 were waited for; matrix products, arithmetic and copies ran while one was open for 0% of the time, Pallas kernels for 25%

profile of v4, /device:TPU:0, one launch (start us, length us, event | category | flops | bytes accessed | tf_op | source)
XLA Modules:
  0.0 71.0 jit_solution(6808779731480826597)
XLA Ops:
  0.6 1.5 %shard_map.95 = (bf16[4,64,256]{2,1,0:T(8,128)(2,1)S(1)}, bf16[4,64,256]{2,1,0:T(8,128)(2,1)S(1)}, bf16[4,256,128]{2,1,0:T(8,128)(2,1)S(1)}) custom-call(s32[1,32]{1,0:T(1,128)} %bitcast.25, bf16[4,4,64,64]{3,2,1,0:T(8,128)(2,1)} %bitcast.23, bf16[4,256,128]{2,1,0:T(8,128)(2,1)} %bitcast.24), custom_call_target="tpu_custom_call" | custom-call | flops 134217728 | bytes 1048576 | tf_op jit(solution)/shard_map/pallas_call | solution.py:258
  2.2 3.0 %collective-permute-start.1 = (bf16[4,64,256]{2,1,0:T(8,128)(2,1)S(1)}, bf16[4,64,256]{2,1,0:T(8,128)(2,1)S(1)}, u32[]{:S(2)}, u32[]{:S(2)}) collective-permute-start(bf16[4,64,256]{2,1,0:T(8,128)(2,1)S(1)} %get-tuple-element.18.field), channel_id=1, source_target_pairs={{0,4},{4,0},{8,12},{12,8},{16,20},{20,16},{24,28},{28,24},{1,5},{5... | collective-permute-start | bytes 393224 | tf_op jit(solution)/shard_map/ppermute | solution.py:351
  5.2 3.6 %collective-permute-start = (bf16[4,64,256]{2,1,0:T(8,128)(2,1)S(1)}, bf16[4,64,256]{2,1,0:T(8,128)(2,1)S(1)}, u32[]{:S(2)}, u32[]{:S(2)}) collective-permute-start(bf16[4,64,256]{2,1,0:T(8,128)(2,1)S(1)} %get-tuple-element.18.field), channel_id=1, source_target_pairs={{0,28},{4,8},{8,4},{12,16},{16,12},{20,24},{24,20},{28,0},{1,29},{... | collective-permute-start | bytes 393224 | tf_op jit(solution)/shard_map/ppermute | solution.py:350
  9.2 1.2 %collective-permute-start.3 = (bf16[4,64,256]{2,1,0:T(8,128)(2,1)S(1)}, bf16[4,64,256]{2,1,0:T(8,128)(2,1)S(1)}, u32[]{:S(2)}, u32[]{:S(2)}) collective-permute-start(bf16[4,64,256]{2,1,0:T(8,128)(2,1)S(1)} %get-tuple-element.18.field), channel_id=1, source_target_pairs={{0,1},{1,0},{2,3},{3,2},{4,5},{5,4},{6,7},{7,6},{8,9},{9,8},{10,11... | collective-permute-start | bytes 393224 | tf_op jit(solution)/shard_map/ppermute | solution.py:349
  10.4 1.6 %shard_map.94 = (bf16[4,4,256,128]{3,2,1,0:T(8,128)(2,1)S(1)}, bf16[4,4,256,128]{3,2,1,0:T(8,128)(2,1)S(1)}) custom-call(bf16[8,4,256,128]{3,2,1,0:T(8,128)(2,1)} %bitcast.21), custom_call_target="tpu_custom_call" | custom-call | bytes 4194304 | tf_op jit(solution)/shard_map/pallas_call | solution.py:258
  12.7 1.6 %shard_map.96.remote.blended = bf16[4,4,256,128]{3,2,1,0:T(8,128)(2,1)S(1)} custom-call(bf16[4,4,256,128]{3,2,1,0:T(8,128)(2,1)S(1)} %get-tuple-element.16.remote, bf16[4,256,128]{2,1,0:T(8,128)(2,1)S(1)} %get-tuple-element.17.diag), custom_call_target="tpu_custom_call" | custom-call | flops 268435456 | bytes 4194304 | tf_op jit(solution)/shard_map/pallas_call | solution.py:258
  15.0 2.4 %collective-permute-start.4 = (bf16[4,64,256]{2,1,0:T(8,128)(2,1)S(1)}, bf16[4,64,256]{2,1,0:T(8,128)(2,1)S(1)}, u32[]{:S(2)}, u32[]{:S(2)}) collective-permute-start(bf16[4,64,256]{2,1,0:T(8,128)(2,1)S(1)} %shard_map.103.field), channel_id=1, source_target_pairs={{0,28},{4,8},{8,4},{12,16},{16,12},{20,24},{24,20},{28,0},{1,29},{... | collective-permute-start | bytes 393224 | tf_op jit(solution)/shard_map/ppermute | solution.py:350
  17.4 1.6 %collective-permute-start.7 = (bf16[4,64,256]{2,1,0:T(8,128)(2,1)S(1)}, bf16[4,64,256]{2,1,0:T(8,128)(2,1)S(1)}, u32[]{:S(2)}, u32[]{:S(2)}) collective-permute-start(bf16[4,64,256]{2,1,0:T(8,128)(2,1)S(1)} %shard_map.103.field), channel_id=1, source_target_pairs={{0,1},{1,0},{2,3},{3,2},{4,5},{5,4},{6,7},{7,6},{8,9},{9,8},{10,11... | collective-permute-start | bytes 393224 | tf_op jit(solution)/shard_map/ppermute | solution.py:349
  19.0 1.6 %shard_map.104 = (bf16[4,4,256,128]{3,2,1,0:T(8,128)(2,1)S(1)}, bf16[4,4,256,128]{3,2,1,0:T(8,128)(2,1)S(1)}) custom-call(bf16[8,4,256,128]{3,2,1,0:T(8,128)(2,1)} %bitcast.22), custom_call_target="tpu_custom_call" | custom-call | bytes 4194304 | tf_op jit(solution)/shard_map/pallas_call | solution.py:258
  22.2 1.1 %collective-permute-done.4._.refs_1_ = bf16[4,64,256]{2,1,0:T(8,128)(2,1)S(1)} collective-permute-done((bf16[4,64,256]{2,1,0:T(8,128)(2,1)S(1)}, bf16[4,64,256]{2,1,0:T(8,128)(2,1)S(1)}, u32[]{:S(2)}, u32[]{:S(2)}) %collective-permute-start.4) | collective-permute-done | bytes 131104 | tf_op jit(solution)/shard_map/ppermute | solution.py:350
  24.2 2.0 %collective-permute-start.8 = (bf16[4,64,256]{2,1,0:T(8,128)(2,1)S(1)}, bf16[4,64,256]{2,1,0:T(8,128)(2,1)S(1)}, u32[]{:S(2)}, u32[]{:S(2)}) collective-permute-start(bf16[4,64,256]{2,1,0:T(8,128)(2,1)S(1)} %shard_map.111.field), channel_id=1, source_target_pairs={{0,28},{4,8},{8,4},{12,16},{16,12},{20,24},{24,20},{28,0},{1,29},{... | collective-permute-start | bytes 393224 | tf_op jit(solution)/shard_map/ppermute | solution.py:350
  27.3 1.6 %shard_map.98.blended = bf16[4,4,256,128]{3,2,1,0:T(8,128)(2,1)S(1)} custom-call(bf16[4,4,256,128]{3,2,1,0:T(8,128)(2,1)S(1)} %shard_map.96.remote.blended, bf16[4,256,128]{2,1,0:T(8,128)(2,1)S(1)} %bitcast.17), custom_call_target="tpu_custom_call" | custom-call | flops 268435456 | bytes 4194304 | tf_op jit(solution)/shard_map/pallas_call | solution.py:258
  30.0 2.1 %collective-permute-done.8._.refs_1_ = bf16[4,64,256]{2,1,0:T(8,128)(2,1)S(1)} collective-permute-done((bf16[4,64,256]{2,1,0:T(8,128)(2,1)S(1)}, bf16[4,64,256]{2,1,0:T(8,128)(2,1)S(1)}, u32[]{:S(2)}, u32[]{:S(2)}) %collective-permute-start.8) | collective-permute-done | bytes 131104 | tf_op jit(solution)/shard_map/ppermute | solution.py:350
  32.9 2.4 %collective-permute-start.12 = (bf16[4,64,256]{2,1,0:T(8,128)(2,1)S(1)}, bf16[4,64,256]{2,1,0:T(8,128)(2,1)S(1)}, u32[]{:S(2)}, u32[]{:S(2)}) collective-permute-start(bf16[4,64,256]{2,1,0:T(8,128)(2,1)S(1)} %shard_map.117.token.field), channel_id=1, source_target_pairs={{0,28},{4,8},{8,4},{12,16},{16,12},{20,24},{24,20},{28,0},{1,29},{... | collective-permute-start | bytes 393224 | tf_op jit(solution)/shard_map/ppermute | solution.py:350
  36.0 1.6 %shard_map.120.blended = bf16[4,4,256,128]{3,2,1,0:T(8,128)(2,1)S(1)} custom-call(bf16[4,4,256,128]{3,2,1,0:T(8,128)(2,1)S(1)} %get-tuple-element.23.remote, bf16[4,256,128]{2,1,0:T(8,128)(2,1)S(1)} %bitcast.12), custom_call_target="tpu_custom_call" | custom-call | flops 268435456 | bytes 4194304 | tf_op jit(solution)/shard_map/pallas_call | solution.py:258
  39.1 1.8 %collective-permute-done.12._.refs_1_ = bf16[4,64,256]{2,1,0:T(8,128)(2,1)S(1)} collective-permute-done((bf16[4,64,256]{2,1,0:T(8,128)(2,1)S(1)}, bf16[4,64,256]{2,1,0:T(8,128)(2,1)S(1)}, u32[]{:S(2)}, u32[]{:S(2)}) %collective-permute-start.12) | collective-permute-done | bytes 131104 | tf_op jit(solution)/shard_map/ppermute | solution.py:350
  41.7 2.1 %collective-permute-start.16 = (bf16[4,64,256]{2,1,0:T(8,128)(2,1)S(1)}, bf16[4,64,256]{2,1,0:T(8,128)(2,1)S(1)}, u32[]{:S(2)}, u32[]{:S(2)}) collective-permute-start(bf16[4,64,256]{2,1,0:T(8,128)(2,1)S(1)} %shard_map.128.field), channel_id=1, source_target_pairs={{0,28},{4,8},{8,4},{12,16},{16,12},{20,24},{24,20},{28,0},{1,29},{... | collective-permute-start | bytes 393224 | tf_op jit(solution)/shard_map/ppermute | solution.py:350
  47.7 1.6 %collective-permute-done.16._.refs_1_ = bf16[4,64,256]{2,1,0:T(8,128)(2,1)S(1)} collective-permute-done((bf16[4,64,256]{2,1,0:T(8,128)(2,1)S(1)}, bf16[4,64,256]{2,1,0:T(8,128)(2,1)S(1)}, u32[]{:S(2)}, u32[]{:S(2)}) %collective-permute-start.16) | collective-permute-done | bytes 131104 | tf_op jit(solution)/shard_map/ppermute | solution.py:350
  50.0 2.5 %collective-permute-start.20 = (bf16[4,64,256]{2,1,0:T(8,128)(2,1)S(1)}, bf16[4,64,256]{2,1,0:T(8,128)(2,1)S(1)}, u32[]{:S(2)}, u32[]{:S(2)}) collective-permute-start(bf16[4,64,256]{2,1,0:T(8,128)(2,1)S(1)} %shard_map.134.field), channel_id=1, source_target_pairs={{0,28},{4,8},{8,4},{12,16},{16,12},{20,24},{24,20},{28,0},{1,29},{... | collective-permute-start | bytes 393224 | tf_op jit(solution)/shard_map/ppermute | solution.py:350
  55.7 2.2 %collective-permute-done.20._.refs_1_ = bf16[4,64,256]{2,1,0:T(8,128)(2,1)S(1)} collective-permute-done((bf16[4,64,256]{2,1,0:T(8,128)(2,1)S(1)}, bf16[4,64,256]{2,1,0:T(8,128)(2,1)S(1)}, u32[]{:S(2)}, u32[]{:S(2)}) %collective-permute-start.20) | collective-permute-done | bytes 131104 | tf_op jit(solution)/shard_map/ppermute | solution.py:350
  58.4 1.2 %collective-permute-done.24._.refs_0_ = f32[16,128]{1,0:T(8,128)S(1)} collective-permute-done((f32[16,128]{1,0:T(8,128)S(1)}, f32[16,128]{1,0:T(8,128)S(1)}, u32[]{:S(2)}, u32[]{:S(2)}) %collective-permute-start.24) | collective-permute-done | bytes 8224 | tf_op jit(solution)/shard_map/ppermute | solution.py:306
  60.1 1.9 %collective-permute-start.26 = (f32[16,128]{1,0:T(8,128)S(1)}, f32[16,128]{1,0:T(8,128)S(1)}, u32[]{:S(2)}, u32[]{:S(2)}) collective-permute-start(f32[16,128]{1,0:T(8,128)S(1)} %shard_map.143.value), channel_id=1, source_target_pairs={{0,5},{1,4},{2,7},{3,6},{4,1},{5,0},{6,3},{7,2},{8,13},{9,12},{10,... | collective-permute-start | bytes 24584 | tf_op jit(solution)/shard_map/ppermute | solution.py:306
  65.0 1.1 %collective-permute-start.30 = (f32[16,128]{1,0:T(8,128)S(1)}, f32[16,128]{1,0:T(8,128)S(1)}, u32[]{:S(2)}, u32[]{:S(2)}) collective-permute-start(f32[16,128]{1,0:T(8,128)S(1)} %shard_map.148.refs_0_), channel_id=1, source_target_pairs={{0,25},{1,24},{2,27},{3,26},{4,29},{5,28},{6,31},{7,30},{8,17},{9,... | collective-permute-start | bytes 24584 | tf_op jit(solution)/shard_map/ppermute | solution.py:306
  67.0 1.9 %collective-permute-start.28 = (f32[16,128]{1,0:T(8,128)S(1)}, f32[16,128]{1,0:T(8,128)S(1)}, u32[]{:S(2)}, u32[]{:S(2)}) collective-permute-start(f32[16,128]{1,0:T(8,128)S(1)} %shard_map.148.refs_0_), channel_id=1, source_target_pairs={{0,9},{1,8},{2,11},{3,10},{4,13},{5,12},{6,15},{7,14},{8,1},{9,0},... | collective-permute-start | bytes 24584 | tf_op jit(solution)/shard_map/ppermute | solution.py:306
  (102 shorter events, 24.9 us)
Async XLA Ops:
  2.2 12.1 %collective-permute-start.1 = (bf16[4,64,256]{2,1,0:T(8,128)(2,1)S(1)}, bf16[4,64,256]{2,1,0:T(8,128)(2,1)S(1)}, u32[]{:S(2)}, u32[]{:S(2)}) collective-permute-start(bf16[4,64,256]{2,1,0:T(8,128)(2,1)S(1)} %get-tuple-element.18.field), channel_id=1, source_target_pairs={{0,4},{4,0},{8,12},{12,8},{16,20},{20,16},{24,28},{28,24},{1,5},{5... | collective-permute-start | bytes 393224 | tf_op jit(solution)/shard_map/ppermute | solution.py:351
  5.2 9.2 %collective-permute-start = (bf16[4,64,256]{2,1,0:T(8,128)(2,1)S(1)}, bf16[4,64,256]{2,1,0:T(8,128)(2,1)S(1)}, u32[]{:S(2)}, u32[]{:S(2)}) collective-permute-start(bf16[4,64,256]{2,1,0:T(8,128)(2,1)S(1)} %get-tuple-element.18.field), channel_id=1, source_target_pairs={{0,28},{4,8},{8,4},{12,16},{16,12},{20,24},{24,20},{28,0},{1,29},{... | collective-permute-start | bytes 393224 | tf_op jit(solution)/shard_map/ppermute | solution.py:350
  8.8 5.7 %collective-permute-start.2 = (bf16[4,64,256]{2,1,0:T(8,128)(2,1)S(1)}, bf16[4,64,256]{2,1,0:T(8,128)(2,1)S(1)}, u32[]{:S(2)}, u32[]{:S(2)}) collective-permute-start(bf16[4,64,256]{2,1,0:T(8,128)(2,1)S(1)} %get-tuple-element.18.field), channel_id=1, source_target_pairs={{0,3},{1,2},{2,1},{3,0},{4,7},{5,6},{6,5},{7,4},{8,11},{9,10},{10,... | collective-permute-start | bytes 393224 | tf_op jit(solution)/shard_map/ppermute | solution.py:348
  9.2 5.3 %collective-permute-start.3 = (bf16[4,64,256]{2,1,0:T(8,128)(2,1)S(1)}, bf16[4,64,256]{2,1,0:T(8,128)(2,1)S(1)}, u32[]{:S(2)}, u32[]{:S(2)}) collective-permute-start(bf16[4,64,256]{2,1,0:T(8,128)(2,1)S(1)} %get-tuple-element.18.field), channel_id=1, source_target_pairs={{0,1},{1,0},{2,3},{3,2},{4,5},{5,4},{6,7},{7,6},{8,9},{9,8},{10,11... | collective-permute-start | bytes 393224 | tf_op jit(solution)/shard_map/ppermute | solution.py:349
  14.9 7.2 %collective-permute-start.5 = (bf16[4,64,256]{2,1,0:T(8,128)(2,1)S(1)}, bf16[4,64,256]{2,1,0:T(8,128)(2,1)S(1)}, u32[]{:S(2)}, u32[]{:S(2)}) collective-permute-start(bf16[4,64,256]{2,1,0:T(8,128)(2,1)S(1)} %shard_map.103.field), channel_id=1, source_target_pairs={{0,4},{4,0},{8,12},{12,8},{16,20},{20,16},{24,28},{28,24},{1,5},{5... | collective-permute-start | bytes 393224 | tf_op jit(solution)/shard_map/ppermute | solution.py:351
  15.0 8.3 %collective-permute-start.4 = (bf16[4,64,256]{2,1,0:T(8,128)(2,1)S(1)}, bf16[4,64,256]{2,1,0:T(8,128)(2,1)S(1)}, u32[]{:S(2)}, u32[]{:S(2)}) collective-permute-start(bf16[4,64,256]{2,1,0:T(8,128)(2,1)S(1)} %shard_map.103.field), channel_id=1, source_target_pairs={{0,28},{4,8},{8,4},{12,16},{16,12},{20,24},{24,20},{28,0},{1,29},{... | collective-permute-start | bytes 393224 | tf_op jit(solution)/shard_map/ppermute | solution.py:350
  17.4 6.0 %collective-permute-start.6 = (bf16[4,64,256]{2,1,0:T(8,128)(2,1)S(1)}, bf16[4,64,256]{2,1,0:T(8,128)(2,1)S(1)}, u32[]{:S(2)}, u32[]{:S(2)}) collective-permute-start(bf16[4,64,256]{2,1,0:T(8,128)(2,1)S(1)} %shard_map.103.field), channel_id=1, source_target_pairs={{0,3},{1,2},{2,1},{3,0},{4,7},{5,6},{6,5},{7,4},{8,11},{9,10},{10,... | collective-permute-start | bytes 393224 | tf_op jit(solution)/shard_map/ppermute | solution.py:348
  17.4 6.0 %collective-permute-start.7 = (bf16[4,64,256]{2,1,0:T(8,128)(2,1)S(1)}, bf16[4,64,256]{2,1,0:T(8,128)(2,1)S(1)}, u32[]{:S(2)}, u32[]{:S(2)}) collective-permute-start(bf16[4,64,256]{2,1,0:T(8,128)(2,1)S(1)} %shard_map.103.field), channel_id=1, source_target_pairs={{0,1},{1,0},{2,3},{3,2},{4,5},{5,4},{6,7},{7,6},{8,9},{9,8},{10,11... | collective-permute-start | bytes 393224 | tf_op jit(solution)/shard_map/ppermute | solution.py:349
  23.8 6.2 %collective-permute-start.9 = (bf16[4,64,256]{2,1,0:T(8,128)(2,1)S(1)}, bf16[4,64,256]{2,1,0:T(8,128)(2,1)S(1)}, u32[]{:S(2)}, u32[]{:S(2)}) collective-permute-start(bf16[4,64,256]{2,1,0:T(8,128)(2,1)S(1)} %shard_map.111.field), channel_id=1, source_target_pairs={{0,4},{4,0},{8,12},{12,8},{16,20},{20,16},{24,28},{28,24},{1,5},{5... | collective-permute-start | bytes 393224 | tf_op jit(solution)/shard_map/ppermute | solution.py:351
  24.2 7.9 %collective-permute-start.8 = (bf16[4,64,256]{2,1,0:T(8,128)(2,1)S(1)}, bf16[4,64,256]{2,1,0:T(8,128)(2,1)S(1)}, u32[]{:S(2)}, u32[]{:S(2)}) collective-permute-start(bf16[4,64,256]{2,1,0:T(8,128)(2,1)S(1)} %shard_map.111.field), channel_id=1, source_target_pairs={{0,28},{4,8},{8,4},{12,16},{16,12},{20,24},{24,20},{28,0},{1,29},{... | collective-permute-start | bytes 393224 | tf_op jit(solution)/shard_map/ppermute | solution.py:350
  26.2 5.8 %collective-permute-start.10 = (bf16[4,64,256]{2,1,0:T(8,128)(2,1)S(1)}, bf16[4,64,256]{2,1,0:T(8,128)(2,1)S(1)}, u32[]{:S(2)}, u32[]{:S(2)}) collective-permute-start(bf16[4,64,256]{2,1,0:T(8,128)(2,1)S(1)} %shard_map.111.field), channel_id=1, source_target_pairs={{0,3},{1,2},{2,1},{3,0},{4,7},{5,6},{6,5},{7,4},{8,11},{9,10},{10,... | collective-permute-start | bytes 393224 | tf_op jit(solution)/shard_map/ppermute | solution.py:348
  26.2 5.8 %collective-permute-start.11 = (bf16[4,64,256]{2,1,0:T(8,128)(2,1)S(1)}, bf16[4,64,256]{2,1,0:T(8,128)(2,1)S(1)}, u32[]{:S(2)}, u32[]{:S(2)}) collective-permute-start(bf16[4,64,256]{2,1,0:T(8,128)(2,1)S(1)} %shard_map.111.field), channel_id=1, source_target_pairs={{0,1},{1,0},{2,3},{3,2},{4,5},{5,4},{6,7},{7,6},{8,9},{9,8},{10,11... | collective-permute-start | bytes 393224 | tf_op jit(solution)/shard_map/ppermute | solution.py:349
  32.5 6.6 %collective-permute-start.13 = (bf16[4,64,256]{2,1,0:T(8,128)(2,1)S(1)}, bf16[4,64,256]{2,1,0:T(8,128)(2,1)S(1)}, u32[]{:S(2)}, u32[]{:S(2)}) collective-permute-start(bf16[4,64,256]{2,1,0:T(8,128)(2,1)S(1)} %shard_map.117.token.field), channel_id=1, source_target_pairs={{0,4},{4,0},{8,12},{12,8},{16,20},{20,16},{24,28},{28,24},{1,5},{5... | collective-permute-start | bytes 393224 | tf_op jit(solution)/shard_map/ppermute | solution.py:351
  32.9 8.0 %collective-permute-start.12 = (bf16[4,64,256]{2,1,0:T(8,128)(2,1)S(1)}, bf16[4,64,256]{2,1,0:T(8,128)(2,1)S(1)}, u32[]{:S(2)}, u32[]{:S(2)}) collective-permute-start(bf16[4,64,256]{2,1,0:T(8,128)(2,1)S(1)} %shard_map.117.token.field), channel_id=1, source_target_pairs={{0,28},{4,8},{8,4},{12,16},{16,12},{20,24},{24,20},{28,0},{1,29},{... | collective-permute-start | bytes 393224 | tf_op jit(solution)/shard_map/ppermute | solution.py:350
  35.3 5.6 %collective-permute-start.14 = (bf16[4,64,256]{2,1,0:T(8,128)(2,1)S(1)}, bf16[4,64,256]{2,1,0:T(8,128)(2,1)S(1)}, u32[]{:S(2)}, u32[]{:S(2)}) collective-permute-start(bf16[4,64,256]{2,1,0:T(8,128)(2,1)S(1)} %shard_map.117.token.field), channel_id=1, source_target_pairs={{0,3},{1,2},{2,1},{3,0},{4,7},{5,6},{6,5},{7,4},{8,11},{9,10},{10,... | collective-permute-start | bytes 393224 | tf_op jit(solution)/shard_map/ppermute | solution.py:348
  35.3 5.6 %collective-permute-start.15 = (bf16[4,64,256]{2,1,0:T(8,128)(2,1)S(1)}, bf16[4,64,256]{2,1,0:T(8,128)(2,1)S(1)}, u32[]{:S(2)}, u32[]{:S(2)}) collective-permute-start(bf16[4,64,256]{2,1,0:T(8,128)(2,1)S(1)} %shard_map.117.token.field), channel_id=1, source_target_pairs={{0,1},{1,0},{2,3},{3,2},{4,5},{5,4},{6,7},{7,6},{8,9},{9,8},{10,11... | collective-permute-start | bytes 393224 | tf_op jit(solution)/shard_map/ppermute | solution.py:349
  41.3 6.4 %collective-permute-start.17 = (bf16[4,64,256]{2,1,0:T(8,128)(2,1)S(1)}, bf16[4,64,256]{2,1,0:T(8,128)(2,1)S(1)}, u32[]{:S(2)}, u32[]{:S(2)}) collective-permute-start(bf16[4,64,256]{2,1,0:T(8,128)(2,1)S(1)} %shard_map.128.field), channel_id=1, source_target_pairs={{0,4},{4,0},{8,12},{12,8},{16,20},{20,16},{24,28},{28,24},{1,5},{5... | collective-permute-start | bytes 393224 | tf_op jit(solution)/shard_map/ppermute | solution.py:351
  41.7 7.7 %collective-permute-start.16 = (bf16[4,64,256]{2,1,0:T(8,128)(2,1)S(1)}, bf16[4,64,256]{2,1,0:T(8,128)(2,1)S(1)}, u32[]{:S(2)}, u32[]{:S(2)}) collective-permute-start(bf16[4,64,256]{2,1,0:T(8,128)(2,1)S(1)} %shard_map.128.field), channel_id=1, source_target_pairs={{0,28},{4,8},{8,4},{12,16},{16,12},{20,24},{24,20},{28,0},{1,29},{... | collective-permute-start | bytes 393224 | tf_op jit(solution)/shard_map/ppermute | solution.py:350
  43.7 5.6 %collective-permute-start.18 = (bf16[4,64,256]{2,1,0:T(8,128)(2,1)S(1)}, bf16[4,64,256]{2,1,0:T(8,128)(2,1)S(1)}, u32[]{:S(2)}, u32[]{:S(2)}) collective-permute-start(bf16[4,64,256]{2,1,0:T(8,128)(2,1)S(1)} %shard_map.128.field), channel_id=1, source_target_pairs={{0,3},{1,2},{2,1},{3,0},{4,7},{5,6},{6,5},{7,4},{8,11},{9,10},{10,... | collective-permute-start | bytes 393224 | tf_op jit(solution)/shard_map/ppermute | solution.py:348
  43.9 5.4 %collective-permute-start.19 = (bf16[4,64,256]{2,1,0:T(8,128)(2,1)S(1)}, bf16[4,64,256]{2,1,0:T(8,128)(2,1)S(1)}, u32[]{:S(2)}, u32[]{:S(2)}) collective-permute-start(bf16[4,64,256]{2,1,0:T(8,128)(2,1)S(1)} %shard_map.128.field), channel_id=1, source_target_pairs={{0,1},{1,0},{2,3},{3,2},{4,5},{5,4},{6,7},{7,6},{8,9},{9,8},{10,11... | collective-permute-start | bytes 393224 | tf_op jit(solution)/shard_map/ppermute | solution.py:349
  49.8 5.9 %collective-permute-start.21 = (bf16[4,64,256]{2,1,0:T(8,128)(2,1)S(1)}, bf16[4,64,256]{2,1,0:T(8,128)(2,1)S(1)}, u32[]{:S(2)}, u32[]{:S(2)}) collective-permute-start(bf16[4,64,256]{2,1,0:T(8,128)(2,1)S(1)} %shard_map.134.field), channel_id=1, source_target_pairs={{0,4},{4,0},{8,12},{12,8},{16,20},{20,16},{24,28},{28,24},{1,5},{5... | collective-permute-start | bytes 393224 | tf_op jit(solution)/shard_map/ppermute | solution.py:351
  50.0 7.9 %collective-permute-start.20 = (bf16[4,64,256]{2,1,0:T(8,128)(2,1)S(1)}, bf16[4,64,256]{2,1,0:T(8,128)(2,1)S(1)}, u32[]{:S(2)}, u32[]{:S(2)}) collective-permute-start(bf16[4,64,256]{2,1,0:T(8,128)(2,1)S(1)} %shard_map.134.field), channel_id=1, source_target_pairs={{0,28},{4,8},{8,4},{12,16},{16,12},{20,24},{24,20},{28,0},{1,29},{... | collective-permute-start | bytes 393224 | tf_op jit(solution)/shard_map/ppermute | solution.py:350
  52.5 5.4 %collective-permute-start.22 = (bf16[4,64,256]{2,1,0:T(8,128)(2,1)S(1)}, bf16[4,64,256]{2,1,0:T(8,128)(2,1)S(1)}, u32[]{:S(2)}, u32[]{:S(2)}) collective-permute-start(bf16[4,64,256]{2,1,0:T(8,128)(2,1)S(1)} %shard_map.134.field), channel_id=1, source_target_pairs={{0,3},{1,2},{2,1},{3,0},{4,7},{5,6},{6,5},{7,4},{8,11},{9,10},{10,... | collective-permute-start | bytes 393224 | tf_op jit(solution)/shard_map/ppermute | solution.py:348
  52.7 5.2 %collective-permute-start.23 = (bf16[4,64,256]{2,1,0:T(8,128)(2,1)S(1)}, bf16[4,64,256]{2,1,0:T(8,128)(2,1)S(1)}, u32[]{:S(2)}, u32[]{:S(2)}) collective-permute-start(bf16[4,64,256]{2,1,0:T(8,128)(2,1)S(1)} %shard_map.134.field), channel_id=1, source_target_pairs={{0,1},{1,0},{2,3},{3,2},{4,5},{5,4},{6,7},{7,6},{8,9},{9,8},{10,11... | collective-permute-start | bytes 393224 | tf_op jit(solution)/shard_map/ppermute | solution.py:349
  (9 other events, 37.2 us)

commit v5 on v4

--- a/solution.py
+++ b/solution.py
@@ -184,12 +184,16 @@
             out[n, half:, at] = im.astype(BF16)
 
 
-def gram_kernel(sites, places, whole, adjoint, token, total, *refs):
+def base_kernel(sites, whole, total, out):
+    total = total[...].astype(BF16)
+    out[...] = packed_gram(sites, whole[...], total.reshape(-1, total.shape[2]))
+
+
+def gram_kernel(sites, places, adjoint, token, base, *refs):
     fields, out = refs[:-1], refs[-1]
-    left = jnp.concatenate([whole[...]] + [adjoint[n] for n in places], axis=1)
-    right = [total[...].astype(BF16)] + [f[...] for f in fields]
-    right = jnp.concatenate([f.reshape(-1, f.shape[2]) for f in right], axis=0)
-    out[...] = packed_gram(sites, left, right)
+    left = jnp.concatenate([adjoint[n] for n in places], axis=1)
+    right = jnp.concatenate([f[...].reshape(-1, f.shape[2]) for f in fields], axis=0)
+    out[...] = base[...] + packed_gram(sites, left, right)
 
 
 def insert_kernel(sites, current, field, source):
@@ -342,7 +346,7 @@
 
     token_t = jax.ShapeDtypeStruct((8, 128), F32)
 
-    def sweeps(local, blended, diag, source, field, aside=()):
+    def sweeps(local, blended, diag, source, field, aside={}):
         token = jnp.zeros(token_t.shape, F32)
         for left in reversed(range(SWEEPS - 1)):
             y = lax.ppermute(field, "tm", far_t)
@@ -353,7 +357,7 @@
                 source = call(functools.partial(insert_kernel, ly), field_t, (unit, 2**20), *source)
             residue = call(functools.partial(local_kernel, ly), field_t, (4 * unit, 2**21), local, source, field)
             total = call(functools.partial(settle_kernel, ly), total_t, (unit, 2**20), diag, residue)
-            token = in_order((*(aside if left == 1 else ()), e, w), token)
+            token = in_order((*aside.get(left, ()), e, w), token)
 
             def finish(kernel, outs, matrices, token, total, got=(e, w, y, c)):
                 return call(
@@ -390,7 +394,7 @@
     both = blend(current[None], charm_p)[0]
     ahead = blend(blended, both)
     next_local, next_remote = load(charm_h)
-    finish, token, total = sweeps(local, blended, light_p, source, field, (both, next_local))
+    finish, token, total = sweeps(local, blended, light_p, source, field, {1: (both, next_local)})
     start = call(functools.partial(settle_kernel, ly), total_t, (unit, 2**20), both, total)
     field = finish(add_kernel, field_t, (ahead,), token, start)
     light = finish(add_kernel, field_t, (blended,), field, total)
@@ -402,11 +406,12 @@
     whole, over = call(turn_over_kernel, over_t, (unit, 2**20), light)
     out_t = jax.ShapeDtypeStruct((lx, ly, comps, wide), BF16)
     light_out, left_light = call(leave_kernel, (out_t, token_t), (unit, 2**21), light)
-    finish, token, total = sweeps(local, blended, charm_p, (current, light), field, (left_light,))
     adjoint_t = jax.ShapeDtypeStruct((4, 2 * ly * cols, lx * comps), BF16)
     adjoint = call(functools.partial(adjoint_kernel, ly), adjoint_t, (4 * unit, 2**21), over, blended)
+    finish, token, total = sweeps(local, blended, charm_p, (current, light), field, {1: (adjoint,), 0: (left_light,)})
     part_t = jax.ShapeDtypeStruct((cols // 2, ly * cols), F32)
-    part = finish(gram_kernel, part_t, (whole, adjoint), token, total)
+    base = call(functools.partial(base_kernel, ly), part_t, (unit, 2**20), whole, total)
+    part = finish(gram_kernel, part_t, (adjoint,), token, base)
     seq = finish(add_kernel, field_t, (blended,), part, total)
     seq_out, token = call(leave_kernel, (out_t, token_t), (unit, 2**21), seq)
     site_count = lx * ly * lax.axis_size("space") * lax.axis_size("tm")

time: 71.2 us -> 71.1 us (level)
    pallas_call x59 -> x61, Pallas kernels: 22.8 us -> 23 us  [call(): pl.pallas_call(kernel, out_shape=outs, in_specs=[HBM if i in far else VME...]
  transfers between devices with their start and end apart: 31 -> 31, of which waited for: 12 -> 12; matrix products, arithmetic and copies ran while one was open for 0% -> 0% of each run, Pallas kernels for 25% -> 26%
where the time goes in v5:
time: 71.1 us; the launch traced here: 70.9 us
  starting transfers between devices  33.8 us (48%)
  Pallas kernels  23 us (32%)
  waiting for transfers between devices  13 us (18%)
  between operations  1.11 us (2%)
    pallas_call x61, Pallas kernels, call(): pl.pallas_call(kernel, out_shape=outs, in_specs=[HBM if i in far else VME...  23 us
    ppermute x6, starting transfers between devices, sweeps(): w = lax.ppermute(field, 'space', far_s)  15 us
    ppermute x6, waiting for transfers between devices, sweeps(): w = lax.ppermute(field, 'space', far_s)  8.69 us
    ppermute x7, starting transfers between devices, swap(): return lax.ppermute(value, ('space', 'tm'), list(enumerate(target)))  6.93 us
    ppermute x6, starting transfers between devices, sweeps(): c = lax.ppermute(field, 'tm', near_t)  6.71 us
    ppermute x6, starting transfers between devices, sweeps(): e = lax.ppermute(field, 'space', near_s)  4.4 us
    ppermute x7, waiting for transfers between devices, swap(): return lax.ppermute(value, ('space', 'tm'), list(enumerate(target)))  3.5 us
  transfers between devices with their start and end apart: 31, of which 12 were waited for; matrix products, arithmetic and copies ran while one was open for 0% of the time, Pallas kernels for 26%

profile of v5, /device:TPU:0, one launch (start us, length us, event | category | flops | bytes accessed | tf_op | source)
XLA Modules:
  0.0 70.9 jit_solution(15658721747902189877)
XLA Ops:
  0.6 1.5 %shard_map.95 = (bf16[4,64,256]{2,1,0:T(8,128)(2,1)S(1)}, bf16[4,64,256]{2,1,0:T(8,128)(2,1)S(1)}, bf16[4,256,128]{2,1,0:T(8,128)(2,1)S(1)}) custom-call(s32[1,32]{1,0:T(1,128)} %bitcast.25, bf16[4,4,64,64]{3,2,1,0:T(8,128)(2,1)} %bitcast.23, bf16[4,256,128]{2,1,0:T(8,128)(2,1)} %bitcast.24), custom_call_target="tpu_custom_call" | custom-call | flops 134217728 | bytes 1048576 | tf_op jit(solution)/shard_map/pallas_call | solution.py:262
  2.2 3.0 %collective-permute-start.1 = (bf16[4,64,256]{2,1,0:T(8,128)(2,1)S(1)}, bf16[4,64,256]{2,1,0:T(8,128)(2,1)S(1)}, u32[]{:S(2)}, u32[]{:S(2)}) collective-permute-start(bf16[4,64,256]{2,1,0:T(8,128)(2,1)S(1)} %get-tuple-element.18.field), channel_id=1, source_target_pairs={{0,4},{4,0},{8,12},{12,8},{16,20},{20,16},{24,28},{28,24},{1,5},{5... | collective-permute-start | bytes 393224 | tf_op jit(solution)/shard_map/ppermute | solution.py:355
  5.2 3.6 %collective-permute-start = (bf16[4,64,256]{2,1,0:T(8,128)(2,1)S(1)}, bf16[4,64,256]{2,1,0:T(8,128)(2,1)S(1)}, u32[]{:S(2)}, u32[]{:S(2)}) collective-permute-start(bf16[4,64,256]{2,1,0:T(8,128)(2,1)S(1)} %get-tuple-element.18.field), channel_id=1, source_target_pairs={{0,28},{4,8},{8,4},{12,16},{16,12},{20,24},{24,20},{28,0},{1,29},{... | collective-permute-start | bytes 393224 | tf_op jit(solution)/shard_map/ppermute | solution.py:354
  9.2 1.2 %collective-permute-start.3 = (bf16[4,64,256]{2,1,0:T(8,128)(2,1)S(1)}, bf16[4,64,256]{2,1,0:T(8,128)(2,1)S(1)}, u32[]{:S(2)}, u32[]{:S(2)}) collective-permute-start(bf16[4,64,256]{2,1,0:T(8,128)(2,1)S(1)} %get-tuple-element.18.field), channel_id=1, source_target_pairs={{0,1},{1,0},{2,3},{3,2},{4,5},{5,4},{6,7},{7,6},{8,9},{9,8},{10,11... | collective-permute-start | bytes 393224 | tf_op jit(solution)/shard_map/ppermute | solution.py:353
  10.4 1.6 %shard_map.94 = (bf16[4,4,256,128]{3,2,1,0:T(8,128)(2,1)S(1)}, bf16[4,4,256,128]{3,2,1,0:T(8,128)(2,1)S(1)}) custom-call(bf16[8,4,256,128]{3,2,1,0:T(8,128)(2,1)} %bitcast.21), custom_call_target="tpu_custom_call" | custom-call | bytes 4194304 | tf_op jit(solution)/shard_map/pallas_call | solution.py:262
  12.7 1.6 %shard_map.96.remote.blended = bf16[4,4,256,128]{3,2,1,0:T(8,128)(2,1)S(1)} custom-call(bf16[4,4,256,128]{3,2,1,0:T(8,128)(2,1)S(1)} %get-tuple-element.16.remote, bf16[4,256,128]{2,1,0:T(8,128)(2,1)S(1)} %get-tuple-element.17.diag), custom_call_target="tpu_custom_call" | custom-call | flops 268435456 | bytes 4194304 | tf_op jit(solution)/shard_map/pallas_call | solution.py:262
  15.0 2.4 %collective-permute-start.4 = (bf16[4,64,256]{2,1,0:T(8,128)(2,1)S(1)}, bf16[4,64,256]{2,1,0:T(8,128)(2,1)S(1)}, u32[]{:S(2)}, u32[]{:S(2)}) collective-permute-start(bf16[4,64,256]{2,1,0:T(8,128)(2,1)S(1)} %shard_map.103.field), channel_id=1, source_target_pairs={{0,28},{4,8},{8,4},{12,16},{16,12},{20,24},{24,20},{28,0},{1,29},{... | collective-permute-start | bytes 393224 | tf_op jit(solution)/shard_map/ppermute | solution.py:354
  17.4 1.6 %collective-permute-start.7 = (bf16[4,64,256]{2,1,0:T(8,128)(2,1)S(1)}, bf16[4,64,256]{2,1,0:T(8,128)(2,1)S(1)}, u32[]{:S(2)}, u32[]{:S(2)}) collective-permute-start(bf16[4,64,256]{2,1,0:T(8,128)(2,1)S(1)} %shard_map.103.field), channel_id=1, source_target_pairs={{0,1},{1,0},{2,3},{3,2},{4,5},{5,4},{6,7},{7,6},{8,9},{9,8},{10,11... | collective-permute-start | bytes 393224 | tf_op jit(solution)/shard_map/ppermute | solution.py:353
  19.0 1.6 %shard_map.104 = (bf16[4,4,256,128]{3,2,1,0:T(8,128)(2,1)S(1)}, bf16[4,4,256,128]{3,2,1,0:T(8,128)(2,1)S(1)}) custom-call(bf16[8,4,256,128]{3,2,1,0:T(8,128)(2,1)} %bitcast.22), custom_call_target="tpu_custom_call" | custom-call | bytes 4194304 | tf_op jit(solution)/shard_map/pallas_call | solution.py:262
  22.2 1.1 %collective-permute-done.4._.refs_1_ = bf16[4,64,256]{2,1,0:T(8,128)(2,1)S(1)} collective-permute-done((bf16[4,64,256]{2,1,0:T(8,128)(2,1)S(1)}, bf16[4,64,256]{2,1,0:T(8,128)(2,1)S(1)}, u32[]{:S(2)}, u32[]{:S(2)}) %collective-permute-start.4) | collective-permute-done | bytes 131104 | tf_op jit(solution)/shard_map/ppermute | solution.py:354
  24.2 2.0 %collective-permute-start.8 = (bf16[4,64,256]{2,1,0:T(8,128)(2,1)S(1)}, bf16[4,64,256]{2,1,0:T(8,128)(2,1)S(1)}, u32[]{:S(2)}, u32[]{:S(2)}) collective-permute-start(bf16[4,64,256]{2,1,0:T(8,128)(2,1)S(1)} %shard_map.111.field), channel_id=1, source_target_pairs={{0,28},{4,8},{8,4},{12,16},{16,12},{20,24},{24,20},{28,0},{1,29},{... | collective-permute-start | bytes 393224 | tf_op jit(solution)/shard_map/ppermute | solution.py:354
  27.3 1.6 %shard_map.98.blended = bf16[4,4,256,128]{3,2,1,0:T(8,128)(2,1)S(1)} custom-call(bf16[4,4,256,128]{3,2,1,0:T(8,128)(2,1)S(1)} %shard_map.96.remote.blended, bf16[4,256,128]{2,1,0:T(8,128)(2,1)S(1)} %bitcast.17), custom_call_target="tpu_custom_call" | custom-call | flops 268435456 | bytes 4194304 | tf_op jit(solution)/shard_map/pallas_call | solution.py:262
  30.0 2.1 %collective-permute-done.8._.refs_1_ = bf16[4,64,256]{2,1,0:T(8,128)(2,1)S(1)} collective-permute-done((bf16[4,64,256]{2,1,0:T(8,128)(2,1)S(1)}, bf16[4,64,256]{2,1,0:T(8,128)(2,1)S(1)}, u32[]{:S(2)}, u32[]{:S(2)}) %collective-permute-start.8) | collective-permute-done | bytes 131104 | tf_op jit(solution)/shard_map/ppermute | solution.py:354
  32.9 2.4 %collective-permute-start.12 = (bf16[4,64,256]{2,1,0:T(8,128)(2,1)S(1)}, bf16[4,64,256]{2,1,0:T(8,128)(2,1)S(1)}, u32[]{:S(2)}, u32[]{:S(2)}) collective-permute-start(bf16[4,64,256]{2,1,0:T(8,128)(2,1)S(1)} %shard_map.117.token.field), channel_id=1, source_target_pairs={{0,28},{4,8},{8,4},{12,16},{16,12},{20,24},{24,20},{28,0},{1,29},{... | collective-permute-start | bytes 393224 | tf_op jit(solution)/shard_map/ppermute | solution.py:354
  36.0 1.6 %shard_map.120.blended = bf16[4,4,256,128]{3,2,1,0:T(8,128)(2,1)S(1)} custom-call(bf16[4,4,256,128]{3,2,1,0:T(8,128)(2,1)S(1)} %get-tuple-element.23.remote, bf16[4,256,128]{2,1,0:T(8,128)(2,1)S(1)} %bitcast.12), custom_call_target="tpu_custom_call" | custom-call | flops 268435456 | bytes 4194304 | tf_op jit(solution)/shard_map/pallas_call | solution.py:262
  39.1 1.8 %collective-permute-done.12._.refs_1_ = bf16[4,64,256]{2,1,0:T(8,128)(2,1)S(1)} collective-permute-done((bf16[4,64,256]{2,1,0:T(8,128)(2,1)S(1)}, bf16[4,64,256]{2,1,0:T(8,128)(2,1)S(1)}, u32[]{:S(2)}, u32[]{:S(2)}) %collective-permute-start.12) | collective-permute-done | bytes 131104 | tf_op jit(solution)/shard_map/ppermute | solution.py:354
  41.7 2.1 %collective-permute-start.16 = (bf16[4,64,256]{2,1,0:T(8,128)(2,1)S(1)}, bf16[4,64,256]{2,1,0:T(8,128)(2,1)S(1)}, u32[]{:S(2)}, u32[]{:S(2)}) collective-permute-start(bf16[4,64,256]{2,1,0:T(8,128)(2,1)S(1)} %shard_map.128.field), channel_id=1, source_target_pairs={{0,28},{4,8},{8,4},{12,16},{16,12},{20,24},{24,20},{28,0},{1,29},{... | collective-permute-start | bytes 393224 | tf_op jit(solution)/shard_map/ppermute | solution.py:354
  47.7 1.6 %collective-permute-done.16._.refs_1_ = bf16[4,64,256]{2,1,0:T(8,128)(2,1)S(1)} collective-permute-done((bf16[4,64,256]{2,1,0:T(8,128)(2,1)S(1)}, bf16[4,64,256]{2,1,0:T(8,128)(2,1)S(1)}, u32[]{:S(2)}, u32[]{:S(2)}) %collective-permute-start.16) | collective-permute-done | bytes 131104 | tf_op jit(solution)/shard_map/ppermute | solution.py:354
  50.0 2.5 %collective-permute-start.20 = (bf16[4,64,256]{2,1,0:T(8,128)(2,1)S(1)}, bf16[4,64,256]{2,1,0:T(8,128)(2,1)S(1)}, u32[]{:S(2)}, u32[]{:S(2)}) collective-permute-start(bf16[4,64,256]{2,1,0:T(8,128)(2,1)S(1)} %shard_map.134.field), channel_id=1, source_target_pairs={{0,28},{4,8},{8,4},{12,16},{16,12},{20,24},{24,20},{28,0},{1,29},{... | collective-permute-start | bytes 393224 | tf_op jit(solution)/shard_map/ppermute | solution.py:354
  55.7 2.1 %collective-permute-done.20._.refs_1_ = bf16[4,64,256]{2,1,0:T(8,128)(2,1)S(1)} collective-permute-done((bf16[4,64,256]{2,1,0:T(8,128)(2,1)S(1)}, bf16[4,64,256]{2,1,0:T(8,128)(2,1)S(1)}, u32[]{:S(2)}, u32[]{:S(2)}) %collective-permute-start.20) | collective-permute-done | bytes 131104 | tf_op jit(solution)/shard_map/ppermute | solution.py:354
  58.4 1.2 %collective-permute-done.24._.refs_0_ = f32[16,128]{1,0:T(8,128)S(1)} collective-permute-done((f32[16,128]{1,0:T(8,128)S(1)}, f32[16,128]{1,0:T(8,128)S(1)}, u32[]{:S(2)}, u32[]{:S(2)}) %collective-permute-start.24) | collective-permute-done | bytes 8224 | tf_op jit(solution)/shard_map/ppermute | solution.py:310
  60.0 1.9 %collective-permute-start.26 = (f32[16,128]{1,0:T(8,128)S(1)}, f32[16,128]{1,0:T(8,128)S(1)}, u32[]{:S(2)}, u32[]{:S(2)}) collective-permute-start(f32[16,128]{1,0:T(8,128)S(1)} %shard_map.145.value), channel_id=1, source_target_pairs={{0,5},{1,4},{2,7},{3,6},{4,1},{5,0},{6,3},{7,2},{8,13},{9,12},{10,... | collective-permute-start | bytes 24584 | tf_op jit(solution)/shard_map/ppermute | solution.py:310
  65.0 1.1 %collective-permute-start.30 = (f32[16,128]{1,0:T(8,128)S(1)}, f32[16,128]{1,0:T(8,128)S(1)}, u32[]{:S(2)}, u32[]{:S(2)}) collective-permute-start(f32[16,128]{1,0:T(8,128)S(1)} %shard_map.150.refs_0_), channel_id=1, source_target_pairs={{0,25},{1,24},{2,27},{3,26},{4,29},{5,28},{6,31},{7,30},{8,17},{9,... | collective-permute-start | bytes 24584 | tf_op jit(solution)/shard_map/ppermute | solution.py:310
  67.0 1.9 %collective-permute-start.28 = (f32[16,128]{1,0:T(8,128)S(1)}, f32[16,128]{1,0:T(8,128)S(1)}, u32[]{:S(2)}, u32[]{:S(2)}) collective-permute-start(f32[16,128]{1,0:T(8,128)S(1)} %shard_map.150.refs_0_), channel_id=1, source_target_pairs={{0,9},{1,8},{2,11},{3,10},{4,13},{5,12},{6,15},{7,14},{8,1},{9,0},... | collective-permute-start | bytes 24584 | tf_op jit(solution)/shard_map/ppermute | solution.py:310
  (104 shorter events, 24.9 us)
Async XLA Ops:
  2.2 12.1 %collective-permute-start.1 = (bf16[4,64,256]{2,1,0:T(8,128)(2,1)S(1)}, bf16[4,64,256]{2,1,0:T(8,128)(2,1)S(1)}, u32[]{:S(2)}, u32[]{:S(2)}) collective-permute-start(bf16[4,64,256]{2,1,0:T(8,128)(2,1)S(1)} %get-tuple-element.18.field), channel_id=1, source_target_pairs={{0,4},{4,0},{8,12},{12,8},{16,20},{20,16},{24,28},{28,24},{1,5},{5... | collective-permute-start | bytes 393224 | tf_op jit(solution)/shard_map/ppermute | solution.py:355
  5.2 9.2 %collective-permute-start = (bf16[4,64,256]{2,1,0:T(8,128)(2,1)S(1)}, bf16[4,64,256]{2,1,0:T(8,128)(2,1)S(1)}, u32[]{:S(2)}, u32[]{:S(2)}) collective-permute-start(bf16[4,64,256]{2,1,0:T(8,128)(2,1)S(1)} %get-tuple-element.18.field), channel_id=1, source_target_pairs={{0,28},{4,8},{8,4},{12,16},{16,12},{20,24},{24,20},{28,0},{1,29},{... | collective-permute-start | bytes 393224 | tf_op jit(solution)/shard_map/ppermute | solution.py:354
  8.8 5.7 %collective-permute-start.2 = (bf16[4,64,256]{2,1,0:T(8,128)(2,1)S(1)}, bf16[4,64,256]{2,1,0:T(8,128)(2,1)S(1)}, u32[]{:S(2)}, u32[]{:S(2)}) collective-permute-start(bf16[4,64,256]{2,1,0:T(8,128)(2,1)S(1)} %get-tuple-element.18.field), channel_id=1, source_target_pairs={{0,3},{1,2},{2,1},{3,0},{4,7},{5,6},{6,5},{7,4},{8,11},{9,10},{10,... | collective-permute-start | bytes 393224 | tf_op jit(solution)/shard_map/ppermute | solution.py:352
  9.2 5.3 %collective-permute-start.3 = (bf16[4,64,256]{2,1,0:T(8,128)(2,1)S(1)}, bf16[4,64,256]{2,1,0:T(8,128)(2,1)S(1)}, u32[]{:S(2)}, u32[]{:S(2)}) collective-permute-start(bf16[4,64,256]{2,1,0:T(8,128)(2,1)S(1)} %get-tuple-element.18.field), channel_id=1, source_target_pairs={{0,1},{1,0},{2,3},{3,2},{4,5},{5,4},{6,7},{7,6},{8,9},{9,8},{10,11... | collective-permute-start | bytes 393224 | tf_op jit(solution)/shard_map/ppermute | solution.py:353
  14.9 7.2 %collective-permute-start.5 = (bf16[4,64,256]{2,1,0:T(8,128)(2,1)S(1)}, bf16[4,64,256]{2,1,0:T(8,128)(2,1)S(1)}, u32[]{:S(2)}, u32[]{:S(2)}) collective-permute-start(bf16[4,64,256]{2,1,0:T(8,128)(2,1)S(1)} %shard_map.103.field), channel_id=1, source_target_pairs={{0,4},{4,0},{8,12},{12,8},{16,20},{20,16},{24,28},{28,24},{1,5},{5... | collective-permute-start | bytes 393224 | tf_op jit(solution)/shard_map/ppermute | solution.py:355
  15.0 8.3 %collective-permute-start.4 = (bf16[4,64,256]{2,1,0:T(8,128)(2,1)S(1)}, bf16[4,64,256]{2,1,0:T(8,128)(2,1)S(1)}, u32[]{:S(2)}, u32[]{:S(2)}) collective-permute-start(bf16[4,64,256]{2,1,0:T(8,128)(2,1)S(1)} %shard_map.103.field), channel_id=1, source_target_pairs={{0,28},{4,8},{8,4},{12,16},{16,12},{20,24},{24,20},{28,0},{1,29},{... | collective-permute-start | bytes 393224 | tf_op jit(solution)/shard_map/ppermute | solution.py:354
  17.4 6.0 %collective-permute-start.6 = (bf16[4,64,256]{2,1,0:T(8,128)(2,1)S(1)}, bf16[4,64,256]{2,1,0:T(8,128)(2,1)S(1)}, u32[]{:S(2)}, u32[]{:S(2)}) collective-permute-start(bf16[4,64,256]{2,1,0:T(8,128)(2,1)S(1)} %shard_map.103.field), channel_id=1, source_target_pairs={{0,3},{1,2},{2,1},{3,0},{4,7},{5,6},{6,5},{7,4},{8,11},{9,10},{10,... | collective-permute-start | bytes 393224 | tf_op jit(solution)/shard_map/ppermute | solution.py:352
  17.4 6.0 %collective-permute-start.7 = (bf16[4,64,256]{2,1,0:T(8,128)(2,1)S(1)}, bf16[4,64,256]{2,1,0:T(8,128)(2,1)S(1)}, u32[]{:S(2)}, u32[]{:S(2)}) collective-permute-start(bf16[4,64,256]{2,1,0:T(8,128)(2,1)S(1)} %shard_map.103.field), channel_id=1, source_target_pairs={{0,1},{1,0},{2,3},{3,2},{4,5},{5,4},{6,7},{7,6},{8,9},{9,8},{10,11... | collective-permute-start | bytes 393224 | tf_op jit(solution)/shard_map/ppermute | solution.py:353
  23.8 6.2 %collective-permute-start.9 = (bf16[4,64,256]{2,1,0:T(8,128)(2,1)S(1)}, bf16[4,64,256]{2,1,0:T(8,128)(2,1)S(1)}, u32[]{:S(2)}, u32[]{:S(2)}) collective-permute-start(bf16[4,64,256]{2,1,0:T(8,128)(2,1)S(1)} %shard_map.111.field), channel_id=1, source_target_pairs={{0,4},{4,0},{8,12},{12,8},{16,20},{20,16},{24,28},{28,24},{1,5},{5... | collective-permute-start | bytes 393224 | tf_op jit(solution)/shard_map/ppermute | solution.py:355
  24.2 7.9 %collective-permute-start.8 = (bf16[4,64,256]{2,1,0:T(8,128)(2,1)S(1)}, bf16[4,64,256]{2,1,0:T(8,128)(2,1)S(1)}, u32[]{:S(2)}, u32[]{:S(2)}) collective-permute-start(bf16[4,64,256]{2,1,0:T(8,128)(2,1)S(1)} %shard_map.111.field), channel_id=1, source_target_pairs={{0,28},{4,8},{8,4},{12,16},{16,12},{20,24},{24,20},{28,0},{1,29},{... | collective-permute-start | bytes 393224 | tf_op jit(solution)/shard_map/ppermute | solution.py:354
  26.2 5.8 %collective-permute-start.10 = (bf16[4,64,256]{2,1,0:T(8,128)(2,1)S(1)}, bf16[4,64,256]{2,1,0:T(8,128)(2,1)S(1)}, u32[]{:S(2)}, u32[]{:S(2)}) collective-permute-start(bf16[4,64,256]{2,1,0:T(8,128)(2,1)S(1)} %shard_map.111.field), channel_id=1, source_target_pairs={{0,3},{1,2},{2,1},{3,0},{4,7},{5,6},{6,5},{7,4},{8,11},{9,10},{10,... | collective-permute-start | bytes 393224 | tf_op jit(solution)/shard_map/ppermute | solution.py:352
  26.2 5.8 %collective-permute-start.11 = (bf16[4,64,256]{2,1,0:T(8,128)(2,1)S(1)}, bf16[4,64,256]{2,1,0:T(8,128)(2,1)S(1)}, u32[]{:S(2)}, u32[]{:S(2)}) collective-permute-start(bf16[4,64,256]{2,1,0:T(8,128)(2,1)S(1)} %shard_map.111.field), channel_id=1, source_target_pairs={{0,1},{1,0},{2,3},{3,2},{4,5},{5,4},{6,7},{7,6},{8,9},{9,8},{10,11... | collective-permute-start | bytes 393224 | tf_op jit(solution)/shard_map/ppermute | solution.py:353
  32.5 6.6 %collective-permute-start.13 = (bf16[4,64,256]{2,1,0:T(8,128)(2,1)S(1)}, bf16[4,64,256]{2,1,0:T(8,128)(2,1)S(1)}, u32[]{:S(2)}, u32[]{:S(2)}) collective-permute-start(bf16[4,64,256]{2,1,0:T(8,128)(2,1)S(1)} %shard_map.117.token.field), channel_id=1, source_target_pairs={{0,4},{4,0},{8,12},{12,8},{16,20},{20,16},{24,28},{28,24},{1,5},{5... | collective-permute-start | bytes 393224 | tf_op jit(solution)/shard_map/ppermute | solution.py:355
  32.9 8.0 %collective-permute-start.12 = (bf16[4,64,256]{2,1,0:T(8,128)(2,1)S(1)}, bf16[4,64,256]{2,1,0:T(8,128)(2,1)S(1)}, u32[]{:S(2)}, u32[]{:S(2)}) collective-permute-start(bf16[4,64,256]{2,1,0:T(8,128)(2,1)S(1)} %shard_map.117.token.field), channel_id=1, source_target_pairs={{0,28},{4,8},{8,4},{12,16},{16,12},{20,24},{24,20},{28,0},{1,29},{... | collective-permute-start | bytes 393224 | tf_op jit(solution)/shard_map/ppermute | solution.py:354
  35.3 5.6 %collective-permute-start.14 = (bf16[4,64,256]{2,1,0:T(8,128)(2,1)S(1)}, bf16[4,64,256]{2,1,0:T(8,128)(2,1)S(1)}, u32[]{:S(2)}, u32[]{:S(2)}) collective-permute-start(bf16[4,64,256]{2,1,0:T(8,128)(2,1)S(1)} %shard_map.117.token.field), channel_id=1, source_target_pairs={{0,3},{1,2},{2,1},{3,0},{4,7},{5,6},{6,5},{7,4},{8,11},{9,10},{10,... | collective-permute-start | bytes 393224 | tf_op jit(solution)/shard_map/ppermute | solution.py:352
  35.3 5.6 %collective-permute-start.15 = (bf16[4,64,256]{2,1,0:T(8,128)(2,1)S(1)}, bf16[4,64,256]{2,1,0:T(8,128)(2,1)S(1)}, u32[]{:S(2)}, u32[]{:S(2)}) collective-permute-start(bf16[4,64,256]{2,1,0:T(8,128)(2,1)S(1)} %shard_map.117.token.field), channel_id=1, source_target_pairs={{0,1},{1,0},{2,3},{3,2},{4,5},{5,4},{6,7},{7,6},{8,9},{9,8},{10,11... | collective-permute-start | bytes 393224 | tf_op jit(solution)/shard_map/ppermute | solution.py:353
  41.3 6.4 %collective-permute-start.17 = (bf16[4,64,256]{2,1,0:T(8,128)(2,1)S(1)}, bf16[4,64,256]{2,1,0:T(8,128)(2,1)S(1)}, u32[]{:S(2)}, u32[]{:S(2)}) collective-permute-start(bf16[4,64,256]{2,1,0:T(8,128)(2,1)S(1)} %shard_map.128.field), channel_id=1, source_target_pairs={{0,4},{4,0},{8,12},{12,8},{16,20},{20,16},{24,28},{28,24},{1,5},{5... | collective-permute-start | bytes 393224 | tf_op jit(solution)/shard_map/ppermute | solution.py:355
  41.7 7.7 %collective-permute-start.16 = (bf16[4,64,256]{2,1,0:T(8,128)(2,1)S(1)}, bf16[4,64,256]{2,1,0:T(8,128)(2,1)S(1)}, u32[]{:S(2)}, u32[]{:S(2)}) collective-permute-start(bf16[4,64,256]{2,1,0:T(8,128)(2,1)S(1)} %shard_map.128.field), channel_id=1, source_target_pairs={{0,28},{4,8},{8,4},{12,16},{16,12},{20,24},{24,20},{28,0},{1,29},{... | collective-permute-start | bytes 393224 | tf_op jit(solution)/shard_map/ppermute | solution.py:354
  43.7 5.6 %collective-permute-start.18 = (bf16[4,64,256]{2,1,0:T(8,128)(2,1)S(1)}, bf16[4,64,256]{2,1,0:T(8,128)(2,1)S(1)}, u32[]{:S(2)}, u32[]{:S(2)}) collective-permute-start(bf16[4,64,256]{2,1,0:T(8,128)(2,1)S(1)} %shard_map.128.field), channel_id=1, source_target_pairs={{0,3},{1,2},{2,1},{3,0},{4,7},{5,6},{6,5},{7,4},{8,11},{9,10},{10,... | collective-permute-start | bytes 393224 | tf_op jit(solution)/shard_map/ppermute | solution.py:352
  43.9 5.4 %collective-permute-start.19 = (bf16[4,64,256]{2,1,0:T(8,128)(2,1)S(1)}, bf16[4,64,256]{2,1,0:T(8,128)(2,1)S(1)}, u32[]{:S(2)}, u32[]{:S(2)}) collective-permute-start(bf16[4,64,256]{2,1,0:T(8,128)(2,1)S(1)} %shard_map.128.field), channel_id=1, source_target_pairs={{0,1},{1,0},{2,3},{3,2},{4,5},{5,4},{6,7},{7,6},{8,9},{9,8},{10,11... | collective-permute-start | bytes 393224 | tf_op jit(solution)/shard_map/ppermute | solution.py:353
  49.8 5.9 %collective-permute-start.21 = (bf16[4,64,256]{2,1,0:T(8,128)(2,1)S(1)}, bf16[4,64,256]{2,1,0:T(8,128)(2,1)S(1)}, u32[]{:S(2)}, u32[]{:S(2)}) collective-permute-start(bf16[4,64,256]{2,1,0:T(8,128)(2,1)S(1)} %shard_map.134.field), channel_id=1, source_target_pairs={{0,4},{4,0},{8,12},{12,8},{16,20},{20,16},{24,28},{28,24},{1,5},{5... | collective-permute-start | bytes 393224 | tf_op jit(solution)/shard_map/ppermute | solution.py:355
  50.0 7.9 %collective-permute-start.20 = (bf16[4,64,256]{2,1,0:T(8,128)(2,1)S(1)}, bf16[4,64,256]{2,1,0:T(8,128)(2,1)S(1)}, u32[]{:S(2)}, u32[]{:S(2)}) collective-permute-start(bf16[4,64,256]{2,1,0:T(8,128)(2,1)S(1)} %shard_map.134.field), channel_id=1, source_target_pairs={{0,28},{4,8},{8,4},{12,16},{16,12},{20,24},{24,20},{28,0},{1,29},{... | collective-permute-start | bytes 393224 | tf_op jit(solution)/shard_map/ppermute | solution.py:354
  52.6 5.4 %collective-permute-start.22 = (bf16[4,64,256]{2,1,0:T(8,128)(2,1)S(1)}, bf16[4,64,256]{2,1,0:T(8,128)(2,1)S(1)}, u32[]{:S(2)}, u32[]{:S(2)}) collective-permute-start(bf16[4,64,256]{2,1,0:T(8,128)(2,1)S(1)} %shard_map.134.field), channel_id=1, source_target_pairs={{0,3},{1,2},{2,1},{3,0},{4,7},{5,6},{6,5},{7,4},{8,11},{9,10},{10,... | collective-permute-start | bytes 393224 | tf_op jit(solution)/shard_map/ppermute | solution.py:352
  52.7 5.2 %collective-permute-start.23 = (bf16[4,64,256]{2,1,0:T(8,128)(2,1)S(1)}, bf16[4,64,256]{2,1,0:T(8,128)(2,1)S(1)}, u32[]{:S(2)}, u32[]{:S(2)}) collective-permute-start(bf16[4,64,256]{2,1,0:T(8,128)(2,1)S(1)} %shard_map.134.field), channel_id=1, source_target_pairs={{0,1},{1,0},{2,3},{3,2},{4,5},{5,4},{6,7},{7,6},{8,9},{9,8},{10,11... | collective-permute-start | bytes 393224 | tf_op jit(solution)/shard_map/ppermute | solution.py:353
  (9 other events, 37.3 us)

commit v6 on v4

--- a/solution.py
+++ b/solution.py
@@ -115,6 +115,11 @@
         residue[x] = (source[x].astype(F32) + pick(dot(left, right), sites)).astype(BF16)
 
 
+def rest_kernel(sites, hops, diag, source, field, total, residue):
+    local_kernel(sites, hops, source, field, residue)
+    settle_kernel(sites, diag, residue, total)
+
+
 def times_i(wide):
     row = lax.broadcasted_iota(jnp.int32, (wide, wide), 0)
     lane = lax.broadcasted_iota(jnp.int32, (wide, wide), 1)
@@ -315,9 +320,9 @@
             pair.append((pair[0][0] ^ pair[1][0], pair[0][1] ^ pair[1][1]))
         groups.append([(s, t ^ cross) for s, t in reversed(pair)])
     if cross:
-        groups.insert(0, [(0, 1)])
+        groups.insert(1, [(0, 1)])
     for group in groups[:-1]:
-        value = add_up(value, [swap(mask) for mask in group], aside if group == groups[-2] else ())
+        value = add_up(value, [swap(mask) for mask in group], aside if group == groups[0] else ())
     return last(value, *[swap(mask) for mask in groups[-1]]) if groups else last(value)
 
 
@@ -351,8 +356,10 @@
             e = lax.ppermute(field, "space", near_s)
             if not isinstance(source, jax.Array):
                 source = call(functools.partial(insert_kernel, ly), field_t, (unit, 2**20), *source)
-            residue = call(functools.partial(local_kernel, ly), field_t, (4 * unit, 2**21), local, source, field)
-            total = call(functools.partial(settle_kernel, ly), total_t, (unit, 2**20), diag, residue)
+            total = call(
+                functools.partial(rest_kernel, ly), total_t, (5 * unit, 2**21), local, diag, source, field,
+                scratch=(pltpu.VMEM(shape, BF16),),
+            )
             token = in_order((*(aside if left == 1 else ()), e, w), token)
 
             def finish(kernel, outs, matrices, token, total, got=(e, w, y, c)):

time: 71.2 us -> 71.3 us (level)
  waiting for transfers between devices: 13.3 us -> 14.1 us
    pallas_call x59 -> x53, Pallas kernels: 22.8 us -> 22.4 us  [call(): pl.pallas_call(kernel, out_shape=outs, in_specs=[HBM if i in far else VME...]
  transfers between devices with their start and end apart: 31 -> 31, of which waited for: 12 -> 13; matrix products, arithmetic and copies ran while one was open for 0% -> 0% of each run, Pallas kernels for 25% -> 25%
where the time goes in v6:
time: 71.3 us; the launch traced here: 71.1 us
  starting transfers between devices  33.5 us (47%)
  Pallas kernels  22.4 us (31%)
  waiting for transfers between devices  14.1 us (20%)
  between operations  1.03 us (1%)
    pallas_call x53, Pallas kernels, call(): pl.pallas_call(kernel, out_shape=outs, in_specs=[HBM if i in far else VME...  22.4 us
    ppermute x6, starting transfers between devices, sweeps(): w = lax.ppermute(field, 'space', far_s)  15 us
    ppermute x6, waiting for transfers between devices, sweeps(): w = lax.ppermute(field, 'space', far_s)  8.92 us
    ppermute x6, starting transfers between devices, sweeps(): c = lax.ppermute(field, 'tm', near_t)  6.7 us
    ppermute x7, starting transfers between devices, swap(): return lax.ppermute(value, ('space', 'tm'), list(enumerate(target)))  6.64 us
    ppermute x6, starting transfers between devices, sweeps(): e = lax.ppermute(field, 'space', near_s)  4.38 us
    ppermute x7, waiting for transfers between devices, swap(): return lax.ppermute(value, ('space', 'tm'), list(enumerate(target)))  3.87 us
  transfers between devices with their start and end apart: 31, of which 13 were waited for; matrix products, arithmetic and copies ran while one was open for 0% of the time, Pallas kernels for 25%

profile of v6, /device:TPU:0, one launch (start us, length us, event | category | flops | bytes accessed | tf_op | source)
XLA Modules:
  0.0 71.1 jit_solution(4338362298339343379)
XLA Ops:
  0.6 1.5 %shard_map.95 = (bf16[4,64,256]{2,1,0:T(8,128)(2,1)S(1)}, bf16[4,64,256]{2,1,0:T(8,128)(2,1)S(1)}, bf16[4,256,128]{2,1,0:T(8,128)(2,1)S(1)}) custom-call(s32[1,32]{1,0:T(1,128)} %bitcast.25, bf16[4,4,64,64]{3,2,1,0:T(8,128)(2,1)} %bitcast.23, bf16[4,256,128]{2,1,0:T(8,128)(2,1)} %bitcast.24), custom_call_target="tpu_custom_call" | custom-call | flops 134217728 | bytes 1048576 | tf_op jit(solution)/shard_map/pallas_call | solution.py:263
  2.2 3.0 %collective-permute-start.1 = (bf16[4,64,256]{2,1,0:T(8,128)(2,1)S(1)}, bf16[4,64,256]{2,1,0:T(8,128)(2,1)S(1)}, u32[]{:S(2)}, u32[]{:S(2)}) collective-permute-start(bf16[4,64,256]{2,1,0:T(8,128)(2,1)S(1)} %get-tuple-element.18.field), channel_id=1, source_target_pairs={{0,4},{4,0},{8,12},{12,8},{16,20},{20,16},{24,28},{28,24},{1,5},{5... | collective-permute-start | bytes 393224 | tf_op jit(solution)/shard_map/ppermute | solution.py:356
  5.2 3.6 %collective-permute-start = (bf16[4,64,256]{2,1,0:T(8,128)(2,1)S(1)}, bf16[4,64,256]{2,1,0:T(8,128)(2,1)S(1)}, u32[]{:S(2)}, u32[]{:S(2)}) collective-permute-start(bf16[4,64,256]{2,1,0:T(8,128)(2,1)S(1)} %get-tuple-element.18.field), channel_id=1, source_target_pairs={{0,28},{4,8},{8,4},{12,16},{16,12},{20,24},{24,20},{28,0},{1,29},{... | collective-permute-start | bytes 393224 | tf_op jit(solution)/shard_map/ppermute | solution.py:355
  9.2 1.2 %collective-permute-start.3 = (bf16[4,64,256]{2,1,0:T(8,128)(2,1)S(1)}, bf16[4,64,256]{2,1,0:T(8,128)(2,1)S(1)}, u32[]{:S(2)}, u32[]{:S(2)}) collective-permute-start(bf16[4,64,256]{2,1,0:T(8,128)(2,1)S(1)} %get-tuple-element.18.field), channel_id=1, source_target_pairs={{0,1},{1,0},{2,3},{3,2},{4,5},{5,4},{6,7},{7,6},{8,9},{9,8},{10,11... | collective-permute-start | bytes 393224 | tf_op jit(solution)/shard_map/ppermute | solution.py:354
  10.4 1.6 %shard_map.94 = (bf16[4,4,256,128]{3,2,1,0:T(8,128)(2,1)S(1)}, bf16[4,4,256,128]{3,2,1,0:T(8,128)(2,1)S(1)}) custom-call(bf16[8,4,256,128]{3,2,1,0:T(8,128)(2,1)} %bitcast.21), custom_call_target="tpu_custom_call" | custom-call | bytes 4194304 | tf_op jit(solution)/shard_map/pallas_call | solution.py:263
  12.0 1.6 %shard_map.96.remote.blended = bf16[4,4,256,128]{3,2,1,0:T(8,128)(2,1)S(1)} custom-call(bf16[4,4,256,128]{3,2,1,0:T(8,128)(2,1)S(1)} %get-tuple-element.16.remote, bf16[4,256,128]{2,1,0:T(8,128)(2,1)S(1)} %get-tuple-element.17.diag), custom_call_target="tpu_custom_call" | custom-call | flops 268435456 | bytes 4194304 | tf_op jit(solution)/shard_map/pallas_call | solution.py:263
  15.0 2.4 %collective-permute-start.4 = (bf16[4,64,256]{2,1,0:T(8,128)(2,1)S(1)}, bf16[4,64,256]{2,1,0:T(8,128)(2,1)S(1)}, u32[]{:S(2)}, u32[]{:S(2)}) collective-permute-start(bf16[4,64,256]{2,1,0:T(8,128)(2,1)S(1)} %shard_map.102.field), channel_id=1, source_target_pairs={{0,28},{4,8},{8,4},{12,16},{16,12},{20,24},{24,20},{28,0},{1,29},{... | collective-permute-start | bytes 393224 | tf_op jit(solution)/shard_map/ppermute | solution.py:355
  17.4 1.6 %collective-permute-start.7 = (bf16[4,64,256]{2,1,0:T(8,128)(2,1)S(1)}, bf16[4,64,256]{2,1,0:T(8,128)(2,1)S(1)}, u32[]{:S(2)}, u32[]{:S(2)}) collective-permute-start(bf16[4,64,256]{2,1,0:T(8,128)(2,1)S(1)} %shard_map.102.field), channel_id=1, source_target_pairs={{0,1},{1,0},{2,3},{3,2},{4,5},{5,4},{6,7},{7,6},{8,9},{9,8},{10,11... | collective-permute-start | bytes 393224 | tf_op jit(solution)/shard_map/ppermute | solution.py:354
  19.0 1.6 %shard_map.103 = (bf16[4,4,256,128]{3,2,1,0:T(8,128)(2,1)S(1)}, bf16[4,4,256,128]{3,2,1,0:T(8,128)(2,1)S(1)}) custom-call(bf16[8,4,256,128]{3,2,1,0:T(8,128)(2,1)} %bitcast.22), custom_call_target="tpu_custom_call" | custom-call | bytes 4194304 | tf_op jit(solution)/shard_map/pallas_call | solution.py:263
  22.1 1.2 %collective-permute-done.4._.refs_1_ = bf16[4,64,256]{2,1,0:T(8,128)(2,1)S(1)} collective-permute-done((bf16[4,64,256]{2,1,0:T(8,128)(2,1)S(1)}, bf16[4,64,256]{2,1,0:T(8,128)(2,1)S(1)}, u32[]{:S(2)}, u32[]{:S(2)}) %collective-permute-start.4) | collective-permute-done | bytes 131104 | tf_op jit(solution)/shard_map/ppermute | solution.py:355
  24.2 2.0 %collective-permute-start.8 = (bf16[4,64,256]{2,1,0:T(8,128)(2,1)S(1)}, bf16[4,64,256]{2,1,0:T(8,128)(2,1)S(1)}, u32[]{:S(2)}, u32[]{:S(2)}) collective-permute-start(bf16[4,64,256]{2,1,0:T(8,128)(2,1)S(1)} %shard_map.109.field), channel_id=1, source_target_pairs={{0,28},{4,8},{8,4},{12,16},{16,12},{20,24},{24,20},{28,0},{1,29},{... | collective-permute-start | bytes 393224 | tf_op jit(solution)/shard_map/ppermute | solution.py:355
  27.3 1.6 %shard_map.98.blended = bf16[4,4,256,128]{3,2,1,0:T(8,128)(2,1)S(1)} custom-call(bf16[4,4,256,128]{3,2,1,0:T(8,128)(2,1)S(1)} %shard_map.96.remote.blended, bf16[4,256,128]{2,1,0:T(8,128)(2,1)S(1)} %bitcast.17), custom_call_target="tpu_custom_call" | custom-call | flops 268435456 | bytes 4194304 | tf_op jit(solution)/shard_map/pallas_call | solution.py:263
  29.9 2.1 %collective-permute-done.8._.refs_1_ = bf16[4,64,256]{2,1,0:T(8,128)(2,1)S(1)} collective-permute-done((bf16[4,64,256]{2,1,0:T(8,128)(2,1)S(1)}, bf16[4,64,256]{2,1,0:T(8,128)(2,1)S(1)}, u32[]{:S(2)}, u32[]{:S(2)}) %collective-permute-start.8) | collective-permute-done | bytes 131104 | tf_op jit(solution)/shard_map/ppermute | solution.py:355
  32.9 2.4 %collective-permute-start.12 = (bf16[4,64,256]{2,1,0:T(8,128)(2,1)S(1)}, bf16[4,64,256]{2,1,0:T(8,128)(2,1)S(1)}, u32[]{:S(2)}, u32[]{:S(2)}) collective-permute-start(bf16[4,64,256]{2,1,0:T(8,128)(2,1)S(1)} %shard_map.114.token.field), channel_id=1, source_target_pairs={{0,28},{4,8},{8,4},{12,16},{16,12},{20,24},{24,20},{28,0},{1,29},{... | collective-permute-start | bytes 393224 | tf_op jit(solution)/shard_map/ppermute | solution.py:355
  36.0 1.6 %shard_map.117.blended = bf16[4,4,256,128]{3,2,1,0:T(8,128)(2,1)S(1)} custom-call(bf16[4,4,256,128]{3,2,1,0:T(8,128)(2,1)S(1)} %get-tuple-element.23.remote, bf16[4,256,128]{2,1,0:T(8,128)(2,1)S(1)} %bitcast.12), custom_call_target="tpu_custom_call" | custom-call | flops 268435456 | bytes 4194304 | tf_op jit(solution)/shard_map/pallas_call | solution.py:263
  39.0 1.8 %collective-permute-done.12._.refs_1_ = bf16[4,64,256]{2,1,0:T(8,128)(2,1)S(1)} collective-permute-done((bf16[4,64,256]{2,1,0:T(8,128)(2,1)S(1)}, bf16[4,64,256]{2,1,0:T(8,128)(2,1)S(1)}, u32[]{:S(2)}, u32[]{:S(2)}) %collective-permute-start.12) | collective-permute-done | bytes 131104 | tf_op jit(solution)/shard_map/ppermute | solution.py:355
  41.7 2.1 %collective-permute-start.16 = (bf16[4,64,256]{2,1,0:T(8,128)(2,1)S(1)}, bf16[4,64,256]{2,1,0:T(8,128)(2,1)S(1)}, u32[]{:S(2)}, u32[]{:S(2)}) collective-permute-start(bf16[4,64,256]{2,1,0:T(8,128)(2,1)S(1)} %shard_map.124.field), channel_id=1, source_target_pairs={{0,28},{4,8},{8,4},{12,16},{16,12},{20,24},{24,20},{28,0},{1,29},{... | collective-permute-start | bytes 393224 | tf_op jit(solution)/shard_map/ppermute | solution.py:355
  43.9 1.1 %collective-permute-start.19 = (bf16[4,64,256]{2,1,0:T(8,128)(2,1)S(1)}, bf16[4,64,256]{2,1,0:T(8,128)(2,1)S(1)}, u32[]{:S(2)}, u32[]{:S(2)}) collective-permute-start(bf16[4,64,256]{2,1,0:T(8,128)(2,1)S(1)} %shard_map.124.field), channel_id=1, source_target_pairs={{0,1},{1,0},{2,3},{3,2},{4,5},{5,4},{6,7},{7,6},{8,9},{9,8},{10,11... | collective-permute-start | bytes 393224 | tf_op jit(solution)/shard_map/ppermute | solution.py:354
  47.7 1.6 %collective-permute-done.16._.refs_1_ = bf16[4,64,256]{2,1,0:T(8,128)(2,1)S(1)} collective-permute-done((bf16[4,64,256]{2,1,0:T(8,128)(2,1)S(1)}, bf16[4,64,256]{2,1,0:T(8,128)(2,1)S(1)}, u32[]{:S(2)}, u32[]{:S(2)}) %collective-permute-start.16) | collective-permute-done | bytes 131104 | tf_op jit(solution)/shard_map/ppermute | solution.py:355
  50.0 2.5 %collective-permute-start.20 = (bf16[4,64,256]{2,1,0:T(8,128)(2,1)S(1)}, bf16[4,64,256]{2,1,0:T(8,128)(2,1)S(1)}, u32[]{:S(2)}, u32[]{:S(2)}) collective-permute-start(bf16[4,64,256]{2,1,0:T(8,128)(2,1)S(1)} %shard_map.129.field), channel_id=1, source_target_pairs={{0,28},{4,8},{8,4},{12,16},{16,12},{20,24},{24,20},{28,0},{1,29},{... | collective-permute-start | bytes 393224 | tf_op jit(solution)/shard_map/ppermute | solution.py:355
  55.7 2.2 %collective-permute-done.20._.refs_1_ = bf16[4,64,256]{2,1,0:T(8,128)(2,1)S(1)} collective-permute-done((bf16[4,64,256]{2,1,0:T(8,128)(2,1)S(1)}, bf16[4,64,256]{2,1,0:T(8,128)(2,1)S(1)}, u32[]{:S(2)}, u32[]{:S(2)}) %collective-permute-start.20) | collective-permute-done | bytes 131104 | tf_op jit(solution)/shard_map/ppermute | solution.py:355
  58.5 2.2 %collective-permute-start.25 = (f32[16,128]{1,0:T(8,128)S(1)}, f32[16,128]{1,0:T(8,128)S(1)}, u32[]{:S(2)}, u32[]{:S(2)}) collective-permute-start(f32[16,128]{1,0:T(8,128)S(1)} %shard_map.133.token.value), channel_id=1, source_target_pairs={{0,5},{1,4},{2,7},{3,6},{4,1},{5,0},{6,3},{7,2},{8,13},{9,12},{10,... | collective-permute-start | bytes 24584 | tf_op jit(solution)/shard_map/ppermute | solution.py:311
  62.5 1.4 %collective-permute-done.24._.refs_2_ = f32[16,128]{1,0:T(8,128)S(1)} collective-permute-done((f32[16,128]{1,0:T(8,128)S(1)}, f32[16,128]{1,0:T(8,128)S(1)}, u32[]{:S(2)}, u32[]{:S(2)}) %collective-permute-start.24) | collective-permute-done | bytes 8224 | tf_op jit(solution)/shard_map/ppermute | solution.py:311
  67.0 2.0 %collective-permute-start.28 = (f32[16,128]{1,0:T(8,128)S(1)}, f32[16,128]{1,0:T(8,128)S(1)}, u32[]{:S(2)}, u32[]{:S(2)}) collective-permute-start(f32[16,128]{1,0:T(8,128)S(1)} %shard_map.142.refs_0_), channel_id=1, source_target_pairs={{0,9},{1,8},{2,11},{3,10},{4,13},{5,12},{6,15},{7,14},{8,1},{9,0},... | collective-permute-start | bytes 24584 | tf_op jit(solution)/shard_map/ppermute | solution.py:311
  (96 shorter events, 24.1 us)
Async XLA Ops:
  2.2 12.1 %collective-permute-start.1 = (bf16[4,64,256]{2,1,0:T(8,128)(2,1)S(1)}, bf16[4,64,256]{2,1,0:T(8,128)(2,1)S(1)}, u32[]{:S(2)}, u32[]{:S(2)}) collective-permute-start(bf16[4,64,256]{2,1,0:T(8,128)(2,1)S(1)} %get-tuple-element.18.field), channel_id=1, source_target_pairs={{0,4},{4,0},{8,12},{12,8},{16,20},{20,16},{24,28},{28,24},{1,5},{5... | collective-permute-start | bytes 393224 | tf_op jit(solution)/shard_map/ppermute | solution.py:356
  5.2 9.1 %collective-permute-start = (bf16[4,64,256]{2,1,0:T(8,128)(2,1)S(1)}, bf16[4,64,256]{2,1,0:T(8,128)(2,1)S(1)}, u32[]{:S(2)}, u32[]{:S(2)}) collective-permute-start(bf16[4,64,256]{2,1,0:T(8,128)(2,1)S(1)} %get-tuple-element.18.field), channel_id=1, source_target_pairs={{0,28},{4,8},{8,4},{12,16},{16,12},{20,24},{24,20},{28,0},{1,29},{... | collective-permute-start | bytes 393224 | tf_op jit(solution)/shard_map/ppermute | solution.py:355
  8.8 5.7 %collective-permute-start.2 = (bf16[4,64,256]{2,1,0:T(8,128)(2,1)S(1)}, bf16[4,64,256]{2,1,0:T(8,128)(2,1)S(1)}, u32[]{:S(2)}, u32[]{:S(2)}) collective-permute-start(bf16[4,64,256]{2,1,0:T(8,128)(2,1)S(1)} %get-tuple-element.18.field), channel_id=1, source_target_pairs={{0,3},{1,2},{2,1},{3,0},{4,7},{5,6},{6,5},{7,4},{8,11},{9,10},{10,... | collective-permute-start | bytes 393224 | tf_op jit(solution)/shard_map/ppermute | solution.py:353
  9.2 5.3 %collective-permute-start.3 = (bf16[4,64,256]{2,1,0:T(8,128)(2,1)S(1)}, bf16[4,64,256]{2,1,0:T(8,128)(2,1)S(1)}, u32[]{:S(2)}, u32[]{:S(2)}) collective-permute-start(bf16[4,64,256]{2,1,0:T(8,128)(2,1)S(1)} %get-tuple-element.18.field), channel_id=1, source_target_pairs={{0,1},{1,0},{2,3},{3,2},{4,5},{5,4},{6,7},{7,6},{8,9},{9,8},{10,11... | collective-permute-start | bytes 393224 | tf_op jit(solution)/shard_map/ppermute | solution.py:354
  14.9 7.2 %collective-permute-start.5 = (bf16[4,64,256]{2,1,0:T(8,128)(2,1)S(1)}, bf16[4,64,256]{2,1,0:T(8,128)(2,1)S(1)}, u32[]{:S(2)}, u32[]{:S(2)}) collective-permute-start(bf16[4,64,256]{2,1,0:T(8,128)(2,1)S(1)} %shard_map.102.field), channel_id=1, source_target_pairs={{0,4},{4,0},{8,12},{12,8},{16,20},{20,16},{24,28},{28,24},{1,5},{5... | collective-permute-start | bytes 393224 | tf_op jit(solution)/shard_map/ppermute | solution.py:356
  15.0 8.3 %collective-permute-start.4 = (bf16[4,64,256]{2,1,0:T(8,128)(2,1)S(1)}, bf16[4,64,256]{2,1,0:T(8,128)(2,1)S(1)}, u32[]{:S(2)}, u32[]{:S(2)}) collective-permute-start(bf16[4,64,256]{2,1,0:T(8,128)(2,1)S(1)} %shard_map.102.field), channel_id=1, source_target_pairs={{0,28},{4,8},{8,4},{12,16},{16,12},{20,24},{24,20},{28,0},{1,29},{... | collective-permute-start | bytes 393224 | tf_op jit(solution)/shard_map/ppermute | solution.py:355
  17.4 6.0 %collective-permute-start.6 = (bf16[4,64,256]{2,1,0:T(8,128)(2,1)S(1)}, bf16[4,64,256]{2,1,0:T(8,128)(2,1)S(1)}, u32[]{:S(2)}, u32[]{:S(2)}) collective-permute-start(bf16[4,64,256]{2,1,0:T(8,128)(2,1)S(1)} %shard_map.102.field), channel_id=1, source_target_pairs={{0,3},{1,2},{2,1},{3,0},{4,7},{5,6},{6,5},{7,4},{8,11},{9,10},{10,... | collective-permute-start | bytes 393224 | tf_op jit(solution)/shard_map/ppermute | solution.py:353
  17.4 6.0 %collective-permute-start.7 = (bf16[4,64,256]{2,1,0:T(8,128)(2,1)S(1)}, bf16[4,64,256]{2,1,0:T(8,128)(2,1)S(1)}, u32[]{:S(2)}, u32[]{:S(2)}) collective-permute-start(bf16[4,64,256]{2,1,0:T(8,128)(2,1)S(1)} %shard_map.102.field), channel_id=1, source_target_pairs={{0,1},{1,0},{2,3},{3,2},{4,5},{5,4},{6,7},{7,6},{8,9},{9,8},{10,11... | collective-permute-start | bytes 393224 | tf_op jit(solution)/shard_map/ppermute | solution.py:354
  23.8 6.1 %collective-permute-start.9 = (bf16[4,64,256]{2,1,0:T(8,128)(2,1)S(1)}, bf16[4,64,256]{2,1,0:T(8,128)(2,1)S(1)}, u32[]{:S(2)}, u32[]{:S(2)}) collective-permute-start(bf16[4,64,256]{2,1,0:T(8,128)(2,1)S(1)} %shard_map.109.field), channel_id=1, source_target_pairs={{0,4},{4,0},{8,12},{12,8},{16,20},{20,16},{24,28},{28,24},{1,5},{5... | collective-permute-start | bytes 393224 | tf_op jit(solution)/shard_map/ppermute | solution.py:356
  24.2 7.9 %collective-permute-start.8 = (bf16[4,64,256]{2,1,0:T(8,128)(2,1)S(1)}, bf16[4,64,256]{2,1,0:T(8,128)(2,1)S(1)}, u32[]{:S(2)}, u32[]{:S(2)}) collective-permute-start(bf16[4,64,256]{2,1,0:T(8,128)(2,1)S(1)} %shard_map.109.field), channel_id=1, source_target_pairs={{0,28},{4,8},{8,4},{12,16},{16,12},{20,24},{24,20},{28,0},{1,29},{... | collective-permute-start | bytes 393224 | tf_op jit(solution)/shard_map/ppermute | solution.py:355
  26.2 5.8 %collective-permute-start.10 = (bf16[4,64,256]{2,1,0:T(8,128)(2,1)S(1)}, bf16[4,64,256]{2,1,0:T(8,128)(2,1)S(1)}, u32[]{:S(2)}, u32[]{:S(2)}) collective-permute-start(bf16[4,64,256]{2,1,0:T(8,128)(2,1)S(1)} %shard_map.109.field), channel_id=1, source_target_pairs={{0,3},{1,2},{2,1},{3,0},{4,7},{5,6},{6,5},{7,4},{8,11},{9,10},{10,... | collective-permute-start | bytes 393224 | tf_op jit(solution)/shard_map/ppermute | solution.py:353
  26.2 5.8 %collective-permute-start.11 = (bf16[4,64,256]{2,1,0:T(8,128)(2,1)S(1)}, bf16[4,64,256]{2,1,0:T(8,128)(2,1)S(1)}, u32[]{:S(2)}, u32[]{:S(2)}) collective-permute-start(bf16[4,64,256]{2,1,0:T(8,128)(2,1)S(1)} %shard_map.109.field), channel_id=1, source_target_pairs={{0,1},{1,0},{2,3},{3,2},{4,5},{5,4},{6,7},{7,6},{8,9},{9,8},{10,11... | collective-permute-start | bytes 393224 | tf_op jit(solution)/shard_map/ppermute | solution.py:354
  32.5 6.5 %collective-permute-start.13 = (bf16[4,64,256]{2,1,0:T(8,128)(2,1)S(1)}, bf16[4,64,256]{2,1,0:T(8,128)(2,1)S(1)}, u32[]{:S(2)}, u32[]{:S(2)}) collective-permute-start(bf16[4,64,256]{2,1,0:T(8,128)(2,1)S(1)} %shard_map.114.token.field), channel_id=1, source_target_pairs={{0,4},{4,0},{8,12},{12,8},{16,20},{20,16},{24,28},{28,24},{1,5},{5... | collective-permute-start | bytes 393224 | tf_op jit(solution)/shard_map/ppermute | solution.py:356
  32.9 8.0 %collective-permute-start.12 = (bf16[4,64,256]{2,1,0:T(8,128)(2,1)S(1)}, bf16[4,64,256]{2,1,0:T(8,128)(2,1)S(1)}, u32[]{:S(2)}, u32[]{:S(2)}) collective-permute-start(bf16[4,64,256]{2,1,0:T(8,128)(2,1)S(1)} %shard_map.114.token.field), channel_id=1, source_target_pairs={{0,28},{4,8},{8,4},{12,16},{16,12},{20,24},{24,20},{28,0},{1,29},{... | collective-permute-start | bytes 393224 | tf_op jit(solution)/shard_map/ppermute | solution.py:355
  35.3 5.6 %collective-permute-start.14 = (bf16[4,64,256]{2,1,0:T(8,128)(2,1)S(1)}, bf16[4,64,256]{2,1,0:T(8,128)(2,1)S(1)}, u32[]{:S(2)}, u32[]{:S(2)}) collective-permute-start(bf16[4,64,256]{2,1,0:T(8,128)(2,1)S(1)} %shard_map.114.token.field), channel_id=1, source_target_pairs={{0,3},{1,2},{2,1},{3,0},{4,7},{5,6},{6,5},{7,4},{8,11},{9,10},{10,... | collective-permute-start | bytes 393224 | tf_op jit(solution)/shard_map/ppermute | solution.py:353
  35.3 5.6 %collective-permute-start.15 = (bf16[4,64,256]{2,1,0:T(8,128)(2,1)S(1)}, bf16[4,64,256]{2,1,0:T(8,128)(2,1)S(1)}, u32[]{:S(2)}, u32[]{:S(2)}) collective-permute-start(bf16[4,64,256]{2,1,0:T(8,128)(2,1)S(1)} %shard_map.114.token.field), channel_id=1, source_target_pairs={{0,1},{1,0},{2,3},{3,2},{4,5},{5,4},{6,7},{7,6},{8,9},{9,8},{10,11... | collective-permute-start | bytes 393224 | tf_op jit(solution)/shard_map/ppermute | solution.py:354
  41.3 6.4 %collective-permute-start.17 = (bf16[4,64,256]{2,1,0:T(8,128)(2,1)S(1)}, bf16[4,64,256]{2,1,0:T(8,128)(2,1)S(1)}, u32[]{:S(2)}, u32[]{:S(2)}) collective-permute-start(bf16[4,64,256]{2,1,0:T(8,128)(2,1)S(1)} %shard_map.124.field), channel_id=1, source_target_pairs={{0,4},{4,0},{8,12},{12,8},{16,20},{20,16},{24,28},{28,24},{1,5},{5... | collective-permute-start | bytes 393224 | tf_op jit(solution)/shard_map/ppermute | solution.py:356
  41.7 7.7 %collective-permute-start.16 = (bf16[4,64,256]{2,1,0:T(8,128)(2,1)S(1)}, bf16[4,64,256]{2,1,0:T(8,128)(2,1)S(1)}, u32[]{:S(2)}, u32[]{:S(2)}) collective-permute-start(bf16[4,64,256]{2,1,0:T(8,128)(2,1)S(1)} %shard_map.124.field), channel_id=1, source_target_pairs={{0,28},{4,8},{8,4},{12,16},{16,12},{20,24},{24,20},{28,0},{1,29},{... | collective-permute-start | bytes 393224 | tf_op jit(solution)/shard_map/ppermute | solution.py:355
  43.7 5.6 %collective-permute-start.18 = (bf16[4,64,256]{2,1,0:T(8,128)(2,1)S(1)}, bf16[4,64,256]{2,1,0:T(8,128)(2,1)S(1)}, u32[]{:S(2)}, u32[]{:S(2)}) collective-permute-start(bf16[4,64,256]{2,1,0:T(8,128)(2,1)S(1)} %shard_map.124.field), channel_id=1, source_target_pairs={{0,3},{1,2},{2,1},{3,0},{4,7},{5,6},{6,5},{7,4},{8,11},{9,10},{10,... | collective-permute-start | bytes 393224 | tf_op jit(solution)/shard_map/ppermute | solution.py:353
  43.9 5.4 %collective-permute-start.19 = (bf16[4,64,256]{2,1,0:T(8,128)(2,1)S(1)}, bf16[4,64,256]{2,1,0:T(8,128)(2,1)S(1)}, u32[]{:S(2)}, u32[]{:S(2)}) collective-permute-start(bf16[4,64,256]{2,1,0:T(8,128)(2,1)S(1)} %shard_map.124.field), channel_id=1, source_target_pairs={{0,1},{1,0},{2,3},{3,2},{4,5},{5,4},{6,7},{7,6},{8,9},{9,8},{10,11... | collective-permute-start | bytes 393224 | tf_op jit(solution)/shard_map/ppermute | solution.py:354
  49.8 5.9 %collective-permute-start.21 = (bf16[4,64,256]{2,1,0:T(8,128)(2,1)S(1)}, bf16[4,64,256]{2,1,0:T(8,128)(2,1)S(1)}, u32[]{:S(2)}, u32[]{:S(2)}) collective-permute-start(bf16[4,64,256]{2,1,0:T(8,128)(2,1)S(1)} %shard_map.129.field), channel_id=1, source_target_pairs={{0,4},{4,0},{8,12},{12,8},{16,20},{20,16},{24,28},{28,24},{1,5},{5... | collective-permute-start | bytes 393224 | tf_op jit(solution)/shard_map/ppermute | solution.py:356
  50.0 7.9 %collective-permute-start.20 = (bf16[4,64,256]{2,1,0:T(8,128)(2,1)S(1)}, bf16[4,64,256]{2,1,0:T(8,128)(2,1)S(1)}, u32[]{:S(2)}, u32[]{:S(2)}) collective-permute-start(bf16[4,64,256]{2,1,0:T(8,128)(2,1)S(1)} %shard_map.129.field), channel_id=1, source_target_pairs={{0,28},{4,8},{8,4},{12,16},{16,12},{20,24},{24,20},{28,0},{1,29},{... | collective-permute-start | bytes 393224 | tf_op jit(solution)/shard_map/ppermute | solution.py:355
  52.5 5.4 %collective-permute-start.22 = (bf16[4,64,256]{2,1,0:T(8,128)(2,1)S(1)}, bf16[4,64,256]{2,1,0:T(8,128)(2,1)S(1)}, u32[]{:S(2)}, u32[]{:S(2)}) collective-permute-start(bf16[4,64,256]{2,1,0:T(8,128)(2,1)S(1)} %shard_map.129.field), channel_id=1, source_target_pairs={{0,3},{1,2},{2,1},{3,0},{4,7},{5,6},{6,5},{7,4},{8,11},{9,10},{10,... | collective-permute-start | bytes 393224 | tf_op jit(solution)/shard_map/ppermute | solution.py:353
  52.7 5.2 %collective-permute-start.23 = (bf16[4,64,256]{2,1,0:T(8,128)(2,1)S(1)}, bf16[4,64,256]{2,1,0:T(8,128)(2,1)S(1)}, u32[]{:S(2)}, u32[]{:S(2)}) collective-permute-start(bf16[4,64,256]{2,1,0:T(8,128)(2,1)S(1)} %shard_map.129.field), channel_id=1, source_target_pairs={{0,1},{1,0},{2,3},{3,2},{4,5},{5,4},{6,7},{7,6},{8,9},{9,8},{10,11... | collective-permute-start | bytes 393224 | tf_op jit(solution)/shard_map/ppermute | solution.py:354
  (9 other events, 37.2 us)
